TPU v7x, 32 devices: a whole 2x2x4 slice. The times are simulated.
32 devices in a mesh: clip: 8 (over z, x), frame: 4 (over y, core).
Axes of the slice: x: 2, y: 2, z: 4, core: 2. Of those that a mesh axis runs over, the one named last changes fastest.
Arguments:
- tokens: bfloat16 [2, 8, 1024, 768], P(None, 'clip', 'frame'), may hold values from -30 to 30
- counts: int32 [2, 8, 16], P(None, 'clip', 'frame'), may hold values from 16 to 64, as said below
- first_gain: bfloat16 [768], replicated, may hold values from 0.5 to 1.5
- first_bias: bfloat16 [768], replicated, may hold values from -3 to 3
- input_weight: bfloat16 [768, 2304], replicated, may hold values from -0.21875 to 0.21875
- input_bias: bfloat16 [2, 768], replicated, may hold values from -3 to 3
- output_weight: bfloat16 [768, 768], replicated, may hold values from -6 to 6
- output_bias: bfloat16 [768], replicated, may hold values from -3 to 3
- second_gain: bfloat16 [768], replicated, may hold values from 0.5 to 1.5
- second_bias: bfloat16 [768], replicated, may hold values from -3 to 3
- expand_weight: bfloat16 [768, 3072], replicated, may hold values from -0.21875 to 0.21875
- expand_bias: bfloat16 [3072], replicated, may hold values from -3 to 3
- reduce_weight: bfloat16 [3072, 768], replicated, may hold values from -0.109375 to 0.109375
- reduce_bias: bfloat16 [768], replicated, may hold values from -3 to 3
- cotangent: bfloat16 [2, 8, 1024, 768], P(None, 'clip', 'frame'), may hold values from -6 to 6
Outputs:
- layer_out: bfloat16 [2, 8, 1024, 768], P(None, 'clip', 'frame')
- grad_tokens: float32 [2, 8, 1024, 768], P(None, 'clip', 'frame')
- grad_first_gain: float32 [768], P('frame')
- grad_first_bias: float32 [768], P('frame')
- grad_input_weight: float32 [768, 2304], P('frame')
- grad_input_bias: float32 [2, 768], P(None, 'frame')
- grad_output_weight: float32 [768, 768], P('frame')
- grad_output_bias: float32 [768], P('frame')
- grad_second_gain: float32 [768], P('frame')
- grad_second_bias: float32 [768], P('frame')
- grad_expand_weight: float32 [768, 3072], P('frame')
- grad_expand_bias: float32 [3072], P('frame')
- grad_reduce_weight: float32 [3072, 768], P('frame')
- grad_reduce_bias: float32 [768], P('frame')
Inputs may be any that keep to these rules, and one draw needn't show every extreme that they name: `counts`: slot s of a frame holds a kept patch when s < that frame's count; the later slots are padding.
All inputs are finite; a program needn't handle non-finite values.
Results may differ from a plain program's by a relative error of at most 0.02.
Values may be sent and summed in bfloat16 or wider, within the bound.
A program may use at most 128 MiB of HBM per device.

v0:
```python
import jax
import jax.numpy as jnp
from jax import lax
from jax.sharding import PartitionSpec as P

D = 768
H = 12
HD = 64
MICRO = 2
FRAME_DEV = 4
SLOTS = 64
BLOCK = 256


epsilon = 1e-06


def from_behind(block, axis, distance):
    devices = range(lax.axis_size(axis))
    route = [((i - distance) % len(devices), i) for i in devices]
    return lax.ppermute(block, axis, route)


def norm_rows(values, gain, shift):
    mean = jnp.mean(values, axis=-1, keepdims=True)
    centred = values - mean
    spread = jnp.mean(centred * centred, axis=-1, keepdims=True)
    return centred * lax.rsqrt(spread + epsilon) * gain + shift


def gelu_exact(values):
    return jax.nn.gelu(values, approximate=False)


def key_valid(every_count, source):
    frame_counts = lax.dynamic_slice_in_dim(every_count, source * FRAME_DEV, FRAME_DEV, 1)
    slot_index = jnp.arange(SLOTS, dtype=jnp.int32)
    return (slot_index[None, None, :] < frame_counts[:, :, None]).reshape(MICRO, BLOCK)


def scores_of(query, keys, valid):
    key_heads = keys.reshape(MICRO, BLOCK, H, HD)
    scores = jnp.einsum("mqhd,mkhd->mhqk", query, key_heads, preferred_element_type=jnp.float32)
    return jnp.where(valid[:, None, None, :], scores, -1e30)


def absorb(state, query, keys, values, valid):
    top, total, summed = state
    scores = scores_of(query, keys, valid)
    new_top = jnp.maximum(top, jnp.max(scores, axis=-1, keepdims=True))
    factor = jnp.exp(top - new_top)
    lifted = jnp.exp(scores - new_top)
    total = total * factor + jnp.sum(lifted, axis=-1, keepdims=True)
    value_heads = values.reshape(MICRO, BLOCK, H, HD)
    summed = summed * factor + jnp.einsum(
        "mhqk,mkhd->mhqd",
        lifted.astype(jnp.bfloat16),
        value_heads,
        preferred_element_type=jnp.float32,
    )
    return (new_top, total, summed)


def block_back(query, keys, values, valid, log_total, delta, grad_heads):
    scores = scores_of(query, keys, valid)
    weights = jnp.exp(scores - log_total)
    key_heads = keys.reshape(MICRO, BLOCK, H, HD)
    value_heads = values.reshape(MICRO, BLOCK, H, HD)
    grad_weights = jnp.einsum(
        "mqhd,mkhd->mhqk", grad_heads, value_heads, preferred_element_type=jnp.float32
    )
    grad_scores = (weights * (grad_weights - delta)).astype(jnp.bfloat16)
    grad_query = jnp.einsum(
        "mhqk,mkhd->mqhd", grad_scores, key_heads, preferred_element_type=jnp.float32
    )
    grad_keys = jnp.einsum(
        "mhqk,mqhd->mkhd", grad_scores, query, preferred_element_type=jnp.float32
    )
    grad_values = jnp.einsum(
        "mhqk,mqhd->mkhd",
        weights.astype(jnp.bfloat16),
        grad_heads,
        preferred_element_type=jnp.float32,
    )
    return (grad_query, grad_keys.reshape(MICRO, BLOCK, D), grad_values.reshape(MICRO, BLOCK, D))


def local(
    tokens,
    counts,
    first_gain,
    first_bias,
    input_weight,
    input_bias,
    output_weight,
    output_bias,
    second_gain,
    second_bias,
    expand_weight,
    expand_bias,
    reduce_weight,
    reduce_bias,
    cotangent,
):
    members = lax.axis_size("frame")
    myself = lax.axis_index("frame")
    total_rows = MICRO * BLOCK
    seq_in = tokens.reshape(total_rows, D).astype(jnp.float32)
    every_count = lax.all_gather(counts.reshape(MICRO, FRAME_DEV), "frame", axis=1, tiled=True)
    gain_one = first_gain.astype(jnp.float32)
    shift_one = first_bias.astype(jnp.float32)
    gain_two = second_gain.astype(jnp.float32)
    shift_two = second_bias.astype(jnp.float32)
    qv_bias = input_bias.astype(jnp.float32)
    first_low = norm_rows(seq_in, gain_one, shift_one).astype(jnp.bfloat16)
    projected = jnp.dot(first_low, input_weight, preferred_element_type=jnp.float32)
    query = (
        ((projected[:, :D] + qv_bias[0]) * 0.125).astype(jnp.bfloat16).reshape(MICRO, BLOCK, H, HD)
    )
    keys = projected[:, D : 2 * D].astype(jnp.bfloat16).reshape(MICRO, BLOCK, D)
    values = (projected[:, 2 * D :] + qv_bias[1]).astype(jnp.bfloat16).reshape(MICRO, BLOCK, D)
    start = (
        jnp.full((MICRO, H, BLOCK, 1), -1e30, jnp.float32),
        jnp.zeros((MICRO, H, BLOCK, 1), jnp.float32),
        jnp.zeros((MICRO, H, BLOCK, HD), jnp.float32),
    )
    state = absorb(start, query, keys, values, key_valid(every_count, myself))
    stored = ()

    def forward_hop(step, carry):
        state_now, moving, kept = carry
        moving = from_behind((moving[0], moving[1]), "frame", 1)
        source = (myself - step) % members
        state_now = absorb(state_now, query, moving[0], moving[1], key_valid(every_count, source))
        return (state_now, moving, kept)

    state, _, stored = lax.fori_loop(1, members, forward_hop, (state, (keys, values), stored))
    top, total, summed = state
    log_total = top + jnp.log(total)
    attend_full = jnp.transpose(summed / total, (0, 2, 1, 3))
    attend_low = attend_full.reshape(total_rows, D).astype(jnp.bfloat16)
    middle = (
        seq_in
        + jnp.dot(attend_low, output_weight, preferred_element_type=jnp.float32)
        + output_bias.astype(jnp.float32)
    )
    second_low = norm_rows(middle, gain_two, shift_two).astype(jnp.bfloat16)
    before = jnp.dot(
        second_low, expand_weight, preferred_element_type=jnp.float32
    ) + expand_bias.astype(jnp.float32)
    active_low = gelu_exact(before).astype(jnp.bfloat16)
    result = (
        middle
        + jnp.dot(active_low, reduce_weight, preferred_element_type=jnp.float32)
        + reduce_bias.astype(jnp.float32)
    )
    layer_out = result.astype(jnp.bfloat16).reshape(MICRO, 1, BLOCK, D)
    upstream_low = cotangent.reshape(total_rows, D)
    upstream = upstream_low.astype(jnp.float32)
    grad_reduce_weight = jnp.dot(active_low.T, upstream_low, preferred_element_type=jnp.float32)
    grad_reduce_bias = jnp.sum(upstream, axis=0)
    grad_active = jnp.dot(upstream_low, reduce_weight.T, preferred_element_type=jnp.float32)
    _, gelu_back = jax.vjp(gelu_exact, before)
    grad_before = gelu_back(grad_active)[0].astype(jnp.bfloat16)
    grad_expand_weight = jnp.dot(second_low.T, grad_before, preferred_element_type=jnp.float32)
    grad_expand_bias = jnp.sum(grad_before.astype(jnp.float32), axis=0)
    grad_second = jnp.dot(grad_before, expand_weight.T, preferred_element_type=jnp.float32)
    _, second_back = jax.vjp(norm_rows, middle, gain_two, shift_two)
    middle_part, grad_second_gain, grad_second_bias = second_back(grad_second)
    grad_middle = upstream + middle_part
    grad_branch = grad_middle.astype(jnp.bfloat16)
    grad_output_weight = jnp.dot(attend_low.T, grad_branch, preferred_element_type=jnp.float32)
    grad_output_bias = jnp.sum(grad_branch.astype(jnp.float32), axis=0)
    grad_attend = jnp.dot(grad_branch, output_weight.T, preferred_element_type=jnp.float32).astype(
        jnp.bfloat16
    )
    grad_heads = grad_attend.reshape(MICRO, BLOCK, H, HD)
    delta = jnp.transpose(
        jnp.sum(grad_heads.astype(jnp.float32) * attend_full, axis=-1), (0, 2, 1)
    )[..., None]
    first_terms = block_back(
        query, keys, values, key_valid(every_count, myself), log_total, delta, grad_heads
    )

    def backward_hop(step, carry):
        grad_query, running, moving = carry
        running = (
            from_behind(running[0].astype(jnp.bfloat16), "frame", 1).astype(jnp.float32),
            from_behind(running[1].astype(jnp.bfloat16), "frame", 1).astype(jnp.float32),
        )
        current = from_behind((moving[0], moving[1]), "frame", 1)
        source = (myself - step) % members
        add_query, add_keys, add_values = block_back(
            query,
            current[0],
            current[1],
            key_valid(every_count, source),
            log_total,
            delta,
            grad_heads,
        )
        return (grad_query + add_query, (running[0] + add_keys, running[1] + add_values), current)

    grad_query, running, _ = lax.fori_loop(
        1, members, backward_hop, (first_terms[0], (first_terms[1], first_terms[2]), (keys, values))
    )
    finished = (
        from_behind(running[0].astype(jnp.bfloat16), "frame", 1).astype(jnp.float32),
        from_behind(running[1].astype(jnp.bfloat16), "frame", 1).astype(jnp.float32),
    )
    query_low = grad_query.astype(jnp.bfloat16).reshape(total_rows, D) * 0.125
    keys_low = finished[0].astype(jnp.bfloat16).reshape(total_rows, D)
    values_low = finished[1].astype(jnp.bfloat16).reshape(total_rows, D)
    grad_projected = jnp.concatenate([query_low, keys_low, values_low], axis=1)
    grad_input_weight = jnp.dot(first_low.T, grad_projected, preferred_element_type=jnp.float32)
    grad_input_bias = jnp.stack(
        [
            jnp.sum(query_low.astype(jnp.float32), axis=0),
            jnp.sum(values_low.astype(jnp.float32), axis=0),
        ]
    )
    grad_first = jnp.dot(grad_projected, input_weight.T, preferred_element_type=jnp.float32)
    _, first_back = jax.vjp(norm_rows, seq_in, gain_one, shift_one)
    input_part, grad_first_gain, grad_first_bias = first_back(grad_first)
    grad_tokens = (grad_middle + input_part).reshape(MICRO, 1, BLOCK, D)
    shares = (
        lax.psum_scatter(
            grad_first_gain.astype(jnp.bfloat16), "frame", scatter_dimension=0, tiled=True
        ).astype(jnp.float32),
        lax.psum_scatter(
            grad_first_bias.astype(jnp.bfloat16), "frame", scatter_dimension=0, tiled=True
        ).astype(jnp.float32),
        lax.psum_scatter(
            grad_input_weight.astype(jnp.bfloat16), "frame", scatter_dimension=0, tiled=True
        ).astype(jnp.float32),
        lax.psum_scatter(
            grad_input_bias.astype(jnp.bfloat16), "frame", scatter_dimension=1, tiled=True
        ).astype(jnp.float32),
        lax.psum_scatter(
            grad_output_weight.astype(jnp.bfloat16), "frame", scatter_dimension=0, tiled=True
        ).astype(jnp.float32),
        lax.psum_scatter(
            grad_output_bias.astype(jnp.bfloat16), "frame", scatter_dimension=0, tiled=True
        ).astype(jnp.float32),
        lax.psum_scatter(
            grad_second_gain.astype(jnp.bfloat16), "frame", scatter_dimension=0, tiled=True
        ).astype(jnp.float32),
        lax.psum_scatter(
            grad_second_bias.astype(jnp.bfloat16), "frame", scatter_dimension=0, tiled=True
        ).astype(jnp.float32),
        lax.psum_scatter(
            grad_expand_weight.astype(jnp.bfloat16), "frame", scatter_dimension=0, tiled=True
        ).astype(jnp.float32),
        lax.psum_scatter(
            grad_expand_bias.astype(jnp.bfloat16), "frame", scatter_dimension=0, tiled=True
        ).astype(jnp.float32),
        lax.psum_scatter(
            grad_reduce_weight.astype(jnp.bfloat16), "frame", scatter_dimension=0, tiled=True
        ).astype(jnp.float32),
        lax.psum_scatter(
            grad_reduce_bias.astype(jnp.bfloat16), "frame", scatter_dimension=0, tiled=True
        ).astype(jnp.float32),
    )
    totals = (
        lax.psum(shares[0].astype(jnp.bfloat16), "clip").astype(jnp.float32),
        lax.psum(shares[1].astype(jnp.bfloat16), "clip").astype(jnp.float32),
        lax.psum(shares[2].astype(jnp.bfloat16), "clip").astype(jnp.float32),
        lax.psum(shares[3].astype(jnp.bfloat16), "clip").astype(jnp.float32),
        lax.psum(shares[4].astype(jnp.bfloat16), "clip").astype(jnp.float32),
        lax.psum(shares[5].astype(jnp.bfloat16), "clip").astype(jnp.float32),
        lax.psum(shares[6].astype(jnp.bfloat16), "clip").astype(jnp.float32),
        lax.psum(shares[7].astype(jnp.bfloat16), "clip").astype(jnp.float32),
        lax.psum(shares[8].astype(jnp.bfloat16), "clip").astype(jnp.float32),
        lax.psum(shares[9].astype(jnp.bfloat16), "clip").astype(jnp.float32),
        lax.psum(shares[10].astype(jnp.bfloat16), "clip").astype(jnp.float32),
        lax.psum(shares[11].astype(jnp.bfloat16), "clip").astype(jnp.float32),
    )
    return (
        layer_out,
        grad_tokens,
        totals[0],
        totals[1],
        totals[2],
        totals[3],
        totals[4],
        totals[5],
        totals[6],
        totals[7],
        totals[8],
        totals[9],
        totals[10],
        totals[11],
    )


def solution(mesh):
    return jax.shard_map(
        local,
        mesh=mesh,
        in_specs=(
            P(None, "clip", "frame", None),
            P(None, "clip", "frame"),
            P(),
            P(),
            P(),
            P(),
            P(),
            P(),
            P(),
            P(),
            P(),
            P(),
            P(),
            P(),
            P(None, "clip", "frame", None),
        ),
        out_specs=(
            P(None, "clip", "frame", None),
            P(None, "clip", "frame", None),
            P("frame"),
            P("frame"),
            P("frame", None),
            P(None, "frame"),
            P("frame", None),
            P("frame"),
            P("frame"),
            P("frame"),
            P("frame", None),
            P("frame"),
            P("frame", None),
            P("frame"),
        ),
        check_vma=False,
    )
```

profile of v0, /device:TPU:0, one launch (start us, length us, event | category | flops | bytes accessed | tf_op | source)
XLA Modules:
  0.0 704.7 jit_solution(9484547704837622580)
XLA Ops:
  18.0 8.0 %all-gather = s32[2,1,16]{0,1,2:T(1,128)} all-gather(s32[2,1,4]{0,1,2:T(1,128)} %copy.88), channel_id=2, replica_groups=mesh['clip'=8,'frame'=4] {'frame'}, dimensions={2}, use_global_device_ids=true | all-gather | bytes 160 | tf_op jit(solution)/shard_map/all_gather | solution.py:109
  42.3 2.9 reshape.336
  59.7 2.9 reshape_reshape.10
  62.6 2.9 reshape_reshape.4
  65.6 2.7 select_reduce_fusion.1
  70.9 2.5 fusion.53
  73.3 83.2 %while.46 = (s32[]{:T(128)}, f32[2,12,256,1]{2,1,0,3:T(8,128)}, f32[2,12,256,1]{2,1,0,3:T(8,128)}, f32[2,12,256,64]{2,3,1,0:T(8,128)}, bf16[2,256,768]{1,2,0:T(8...) while((s32[]{:T(128)}, f32[2,12,256,1]{2,1,0,3:T(8,128)}, ...), condition=%wide.region_7.8_spmd, body=%wide.region_4.7_spmd.sunk | while | flops 416041472 | bytes 47102572 | solution.py:137
  75.0 10.5 %collective-permute-done = bf16[2,256,768]{1,2,0:T(8,128)(2,1)} collective-permute-done((bf16[2,256,768]{1,2,0:T(8,128)(2,1)}, bf16[2,256,768]{1,2,0:T(8,128)(2,1)}, u32[]{:S(2)}, u32[]{:S(2)}) %collective-permute-start) | collective-permute-done | bytes 786464 | tf_op jit(solution)/shard_map/while/body/eval_jaxpr/ppermute | solution.py:21
  85.5 2.6 select_reduce_fusion.3
  90.0 3.9 collective-permute-done.1
  93.9 2.7 multiply_add_fusion.3
  96.6 2.6 copy.177
  102.6 10.5 %collective-permute-done = bf16[2,256,768]{1,2,0:T(8,128)(2,1)} collective-permute-done((bf16[2,256,768]{1,2,0:T(8,128)(2,1)}, bf16[2,256,768]{1,2,0:T(8,128)(2,1)}, u32[]{:S(2)}, u32[]{:S(2)}) %collective-permute-start) | collective-permute-done | bytes 786464 | tf_op jit(solution)/shard_map/while/body/eval_jaxpr/ppermute | solution.py:21
  113.1 2.6 select_reduce_fusion.3
  117.6 3.9 collective-permute-done.1
  121.5 2.7 multiply_add_fusion.3
  124.2 2.6 copy.177
  130.2 10.5 %collective-permute-done = bf16[2,256,768]{1,2,0:T(8,128)(2,1)} collective-permute-done((bf16[2,256,768]{1,2,0:T(8,128)(2,1)}, bf16[2,256,768]{1,2,0:T(8,128)(2,1)}, u32[]{:S(2)}, u32[]{:S(2)}) %collective-permute-start) | collective-permute-done | bytes 786464 | tf_op jit(solution)/shard_map/while/body/eval_jaxpr/ppermute | solution.py:21
  140.7 2.6 select_reduce_fusion.3
  145.2 3.9 collective-permute-done.1
  149.1 2.7 multiply_add_fusion.3
  151.8 2.6 copy.177
  157.5 4.2 bitcast_convert_fusion
  163.3 5.3 fusion.76
  168.6 19.1 %fusion.79 = (bf16[3072]{0:T(1024)(128)(2,1)}, bf16[512,3072]{1,0:T(8,128)(2,1)S(1)}, f32[512,3072]{1,0:T(8,128)}) fusion(f32[512,3072]{1,0:T(8,128)S(1)} %fusion.76, f32[3072]{0:T(1024)S(1)} %copy-done.42, bf16[512,768]{1,0:T(8,128)(2,1)S(1)} %bitcast.205, bf16[3072,768]{1,0:T(8,128)(2,1)S(1)} %bitcast.237), kind=kOutput, calls=%fused_computation.145 | convolution fusion | flops 2532307968 | bytes 21252096 | tf_op jit(solution)/shard_map/dot_general | solution.py:162
  187.7 3.5 multiply_reduce_fusion
  196.7 3.3 convolution_convert_fusion.4
  203.0 3.1 reshape.341
  210.9 5.1 fusion.27
  216.0 4.2 multiply_convert_fusion.1
  224.5 125.1 %while.47 = (s32[]{:T(128)}, f32[2,256,12,64]{1,3,2,0:T(8,128)}, bf16[2,256,768]{1,2,0:T(8,128)(2,1)}, bf16[2,256,768]{1,2,0:T(8,128)(2,1)}, bf16[2,256,768]{1,2...) while((s32[]{:T(128)}, f32[2,256,12,64]{1,3,2,0:T(8,128)}, ...), condition=%wide.region_14.15_spmd, body=%wide.region_13.14_spmd.sunk | while | flops 1021968896 | bytes 81287400 | solution.py:204
  227.1 9.1 %collective-permute-done.2 = bf16[2,256,768]{1,2,0:T(8,128)(2,1)} collective-permute-done((bf16[2,256,768]{1,2,0:T(8,128)(2,1)}, bf16[2,256,768]{1,2,0:T(8,128)(2,1)}, u32[]{:S(2)}, u32[]{:S(2)}) %collective-permute-start.2) | collective-permute-done | bytes 786464 | tf_op jit(solution)/shard_map/while/body/eval_jaxpr/ppermute | solution.py:21
  236.2 2.5 fusion.157
  240.2 4.4 collective-permute-done.3
  244.7 3.4 multiply_convert_fusion.4
  248.1 5.0 collective-permute-done.5
  263.4 2.8 bitcast_add_fusion.12
  268.8 9.1 %collective-permute-done.2 = bf16[2,256,768]{1,2,0:T(8,128)(2,1)} collective-permute-done((bf16[2,256,768]{1,2,0:T(8,128)(2,1)}, bf16[2,256,768]{1,2,0:T(8,128)(2,1)}, u32[]{:S(2)}, u32[]{:S(2)}) %collective-permute-start.2) | collective-permute-done | bytes 786464 | tf_op jit(solution)/shard_map/while/body/eval_jaxpr/ppermute | solution.py:21
  277.9 2.5 fusion.157
  281.9 4.4 collective-permute-done.3
  286.4 3.4 multiply_convert_fusion.4
  289.8 5.0 collective-permute-done.5
  305.1 2.8 bitcast_add_fusion.12
  310.5 9.1 %collective-permute-done.2 = bf16[2,256,768]{1,2,0:T(8,128)(2,1)} collective-permute-done((bf16[2,256,768]{1,2,0:T(8,128)(2,1)}, bf16[2,256,768]{1,2,0:T(8,128)(2,1)}, u32[]{:S(2)}, u32[]{:S(2)}) %collective-permute-start.2) | collective-permute-done | bytes 786464 | tf_op jit(solution)/shard_map/while/body/eval_jaxpr/ppermute | solution.py:21
  323.6 4.4 collective-permute-done.3
  328.0 3.4 multiply_convert_fusion.4
  331.5 5.0 collective-permute-done.5
  346.8 2.8 bitcast_add_fusion.12
  358.8 4.8 collective-permute-done.6
  365.9 6.1 collective-permute-done.7
  374.3 5.6 convolution_convert_fusion.2
  380.7 6.2 multiply_convert_fusion.2
  388.5 4.3 convolution_convert_fusion
  393.6 7.4 %convolution_convert_fusion.1 = bf16[768,3072]{1,0:T(8,128)(2,1)} fusion(bf16[512,3072]{1,0:T(8,128)(2,1)} %copy-done.65, f32[512,768]{1,0:T(8,128)} %copy-done.16, f32[768]{0:T(1024)} %convert_element_type.278, f32[768]{0:T(1024)S(1)} %copy-done.56, f32[512]{0:T(512)S(1)} %copy-done.58, f32[512]{0:T(512)S(1)} %copy-done.52), kind=kOutput, calls=%fused_computation.53 | convolution fusion | flops 2420244480 | bytes 9447424 | tf_op jit(solution)/shard_map/dot_general | solution.py:165
  403.7 17.4 %reduce-scatter.8.cloned.1.call-done = bf16[192,2304]{1,0:T(8,128)(2,1)} async-done(((bf16[768,2304]{1,0:T(8,128)(2,1)}), bf16[192,2304]{1,0:T(8,128)(2,1)}) %reduce-scatter.8.cloned.1.call-update) | async-done | bytes 884752 | tf_op jit(solution)/shard_map/reduce_scatter | solution.py:233
  421.1 50.4 %reduce-scatter.14.cloned.1.call-done = bf16[768,768]{1,0:T(8,128)(2,1)} async-done(((bf16[3072,768]{1,0:T(8,128)(2,1)}), bf16[768,768]{1,0:T(8,128)(2,1)}) %reduce-scatter.14.cloned.1.call-update) | async-done | bytes 1179664 | tf_op jit(solution)/shard_map/reduce_scatter | solution.py:257
  471.5 50.4 %reduce-scatter.12.cloned.1.call-done = bf16[192,3072]{1,0:T(8,128)(2,1)} async-done(((bf16[768,3072]{1,0:T(8,128)(2,1)}), bf16[192,3072]{1,0:T(8,128)(2,1)}) %reduce-scatter.12.cloned.1.call-update) | async-done | bytes 1179664 | tf_op jit(solution)/shard_map/reduce_scatter | solution.py:251
  526.4 7.4 %add_convert_fusion.1 = bf16[512,768]{1,0:T(8,128)(2,1)} fusion(f32[512,768]{1,0:T(8,128)} %copy-done.16, bf16[512,3072]{1,0:T(8,128)(2,1)} %copy-done.26, bf16[3072,768]{1,0:T(8,128)(2,1)} %param.31, f32[768]{0:T(1024)S(1)} %convert_element_type.282), kind=kOutput, calls=%fused_computation.97 | convolution fusion | flops 2417098752 | bytes 10226688 | tf_op jit(solution)/shard_map/dot_general | solution.py:154
  533.9 2.8 fusion.77
  538.1 11.8 %all-reduce.9 = (bf16[768]{0:T(1024)(128)(2,1)}, bf16[768]{0:T(1024)(128)(2,1)}, bf16[768]{0:T(1024)(128)(2,1)}, bf16[768]{0:T(1024)(128)(2,1)}, bf16[768]{0:T(1...) all-reduce(bf16[768]{0:T(1024)(128)(2,1)} %get-tuple-element.639, ...), channel_id=3, replica_groups=mesh['clip'=8,'frame'=4] {'frame'}, use_global_device_ids=true, to_apply=%region_18.19.clone | all-reduce | flops 7680 | bytes 30720
  559.5 4.2 add_add_fusion.2
  564.5 23.9 %all-reduce.7 = (bf16[192]{0:T(256)(128)(2,1)}, bf16[192]{0:T(256)(128)(2,1)}, bf16[2,192]{1,0:T(2,128)(2,1)S(1)}, bf16[192]{0:T(256)(128)(2,1)}, bf16[192]{0:T(...) all-reduce(bf16[192]{0:T(256)(128)(2,1)} %dynamic-slice.2, ...), channel_id=1, replica_groups=mesh['clip'=8,'frame'=4] {'clip'}, use_global_device_ids=true, to_apply=%region_19.20 | all-reduce | flops 2304 | bytes 9216 | tf_op jit(solution)/shard_map/psum | solution.py:265
  596.3 93.4 %all-reduce.12.cloned.1.call-done = (bf16[192,2304]{1,0:T(8,128)(2,1)}, bf16[192,768]{1,0:T(8,128)(2,1)}, bf16[192,3072]{1,0:T(8,128)(2,1)}, bf16[768,768]{1,0:T(8,128)(2,1)}) async-done(((bf16[192,2304]{1,0:T(8,128)(2,1)}, bf16[192,768]{1,0:T(8,128)(2,1)}, bf16[192,3072]{1,0:T(8,128)(2,1)}, bf16[768,768]{1,0:T(8,128)(2,1)}), (bf16[192,2304]{1,0:T(8,128)(2,1)}, bf16[192,768]{1,0:T(8,128)(2,1)}, ...) | async-done | bytes 3538960 | tf_op jit(solution)/shard_map/psum | solution.py:267
  691.6 2.6 convert_element_type.299
  (388 shorter events, 172.7 us)
Async XLA Ops:
  7.2 28.4 %copy-start = (bf16[768,2304]{1,0:T(8,128)(2,1)S(1)}, bf16[768,2304]{1,0:T(8,128)(2,1)}, u32[]{:S(2)}) copy-start(bf16[768,2304]{1,0:T(8,128)(2,1)} %param.23) | copy-start | bytes 10616836
  7.2 396.5 %reduce-scatter.10.cloned.1.call-start = ((), (), s32[]{:S(2)}) async-start(), calls=%async_computation.6 | async-start | bytes 1474560 | tf_op jit(solution)/shard_map/reduce_scatter | solution.py:239
  10.7 26.9 %copy-start.44 = (f32[1,2,2,128]{3,1,2,0:T(2,128)}, f32[1,2,2,128]{3,1,2,0:T(2,128)S(1)}, u32[]{:S(2)}) copy-start(f32[1,2,2,128]{3,1,2,0:T(2,128)S(1)} %copy.134) | copy-start | bytes 6148
  12.2 5.8 copy-start.53
  12.3 25.3 %copy-start.46 = (f32[512]{0:T(512)}, f32[512]{0:T(512)S(1)}, u32[]{:S(2)}) copy-start(f32[512]{0:T(512)S(1)} %rsqrt.22) | copy-start | bytes 6148
  12.9 24.6 %copy-start.38 = (f32[768]{0:T(1024)}, f32[768]{0:T(1024)S(1)}, u32[]{:S(2)}) copy-start(f32[768]{0:T(1024)S(1)} %convert_element_type.267) | copy-start | bytes 9220
  56.8 8.8 %copy-start.59 = (s32[2,256]{1,0:T(2,128)S(1)}, s32[2,256]{1,0:T(2,128)}, u32[]{:S(2)}) copy-start(s32[2,256]{1,0:T(2,128)} %lt.175) | copy-start | bytes 6148
  56.8 8.8 %copy-start.62 = (s32[256]{0:T(256)S(1)}, s32[256]{0:T(256)}, u32[]{:S(2)}) copy-start(s32[256]{0:T(256)} %lt.171) | copy-start | bytes 3076
  73.7 11.8 %collective-permute-start = (bf16[2,256,768]{1,2,0:T(8,128)(2,1)}, bf16[2,256,768]{1,2,0:T(8,128)(2,1)}, u32[]{:S(2)}, u32[]{:S(2)}) collective-permute-start(bf16[2,256,768]{1,2,0:T(8,128)(2,1)} %get-tuple-element.889), channel_id=1, source_target_pairs={{3,0},{0,1},{1,2},{2,3},{7,4},{4,5},{5,6},{6,7},{11,8},{8,9},{9,10... | collective-permute-start | bytes 2359304 | tf_op jit(solution)/shard_map/while/body/eval_jaxpr/ppermute | solution.py:21
  74.0 19.8 %collective-permute-start.1 = (bf16[2,256,768]{1,2,0:T(8,128)(2,1)}, bf16[2,256,768]{1,2,0:T(8,128)(2,1)}, u32[]{:S(2)}, u32[]{:S(2)}) collective-permute-start(bf16[2,256,768]{1,2,0:T(8,128)(2,1)} %get-tuple-element.890), channel_id=1, source_target_pairs={{3,0},{0,1},{1,2},{2,3},{7,4},{4,5},{5,6},{6,7},{11,8},{8,9},{9,10... | collective-permute-start | bytes 2359304 | tf_op jit(solution)/shard_map/while/body/eval_jaxpr/ppermute | solution.py:21
  88.1 5.8 copy-start.6
  89.4 7.2 %copy-start.28 = (f32[2,12,256,1]{2,1,0,3:T(8,128)}, f32[2,12,256,1]{2,1,0,3:T(8,128)S(1)}, u32[]{:S(2)}) copy-start(f32[2,12,256,1]{2,1,0,3:T(8,128)S(1)} %bitcast_add_fusion.10) | copy-start | bytes 73732 | tf_op jit(solution)/shard_map/while
  101.3 11.7 %collective-permute-start = (bf16[2,256,768]{1,2,0:T(8,128)(2,1)}, bf16[2,256,768]{1,2,0:T(8,128)(2,1)}, u32[]{:S(2)}, u32[]{:S(2)}) collective-permute-start(bf16[2,256,768]{1,2,0:T(8,128)(2,1)} %get-tuple-element.889), channel_id=1, source_target_pairs={{3,0},{0,1},{1,2},{2,3},{7,4},{4,5},{5,6},{6,7},{11,8},{8,9},{9,10... | collective-permute-start | bytes 2359304 | tf_op jit(solution)/shard_map/while/body/eval_jaxpr/ppermute | solution.py:21
  101.3 20.2 %collective-permute-start.1 = (bf16[2,256,768]{1,2,0:T(8,128)(2,1)}, bf16[2,256,768]{1,2,0:T(8,128)(2,1)}, u32[]{:S(2)}, u32[]{:S(2)}) collective-permute-start(bf16[2,256,768]{1,2,0:T(8,128)(2,1)} %get-tuple-element.890), channel_id=1, source_target_pairs={{3,0},{0,1},{1,2},{2,3},{7,4},{4,5},{5,6},{6,7},{11,8},{8,9},{9,10... | collective-permute-start | bytes 2359304 | tf_op jit(solution)/shard_map/while/body/eval_jaxpr/ppermute | solution.py:21
  115.7 5.8 copy-start.6
  117.0 7.2 %copy-start.28 = (f32[2,12,256,1]{2,1,0,3:T(8,128)}, f32[2,12,256,1]{2,1,0,3:T(8,128)S(1)}, u32[]{:S(2)}) copy-start(f32[2,12,256,1]{2,1,0,3:T(8,128)S(1)} %bitcast_add_fusion.10) | copy-start | bytes 73732 | tf_op jit(solution)/shard_map/while
  128.9 11.7 %collective-permute-start = (bf16[2,256,768]{1,2,0:T(8,128)(2,1)}, bf16[2,256,768]{1,2,0:T(8,128)(2,1)}, u32[]{:S(2)}, u32[]{:S(2)}) collective-permute-start(bf16[2,256,768]{1,2,0:T(8,128)(2,1)} %get-tuple-element.889), channel_id=1, source_target_pairs={{3,0},{0,1},{1,2},{2,3},{7,4},{4,5},{5,6},{6,7},{11,8},{8,9},{9,10... | collective-permute-start | bytes 2359304 | tf_op jit(solution)/shard_map/while/body/eval_jaxpr/ppermute | solution.py:21
  128.9 20.2 %collective-permute-start.1 = (bf16[2,256,768]{1,2,0:T(8,128)(2,1)}, bf16[2,256,768]{1,2,0:T(8,128)(2,1)}, u32[]{:S(2)}, u32[]{:S(2)}) collective-permute-start(bf16[2,256,768]{1,2,0:T(8,128)(2,1)} %get-tuple-element.890), channel_id=1, source_target_pairs={{3,0},{0,1},{1,2},{2,3},{7,4},{4,5},{5,6},{6,7},{11,8},{8,9},{9,10... | collective-permute-start | bytes 2359304 | tf_op jit(solution)/shard_map/while/body/eval_jaxpr/ppermute | solution.py:21
  143.3 5.8 copy-start.6
  144.6 7.2 %copy-start.28 = (f32[2,12,256,1]{2,1,0,3:T(8,128)}, f32[2,12,256,1]{2,1,0,3:T(8,128)S(1)}, u32[]{:S(2)}) copy-start(f32[2,12,256,1]{2,1,0,3:T(8,128)S(1)} %bitcast_add_fusion.10) | copy-start | bytes 73732 | tf_op jit(solution)/shard_map/while
  161.9 6.7 slice-start.2
  162.8 28.4 %copy-start.16 = (f32[512,768]{1,0:T(8,128)}, f32[512,768]{1,0:T(8,128)S(1)}, u32[]{:S(2)}) copy-start(f32[512,768]{1,0:T(8,128)S(1)} %get-tuple-element.732) | copy-start | bytes 4718596
  162.9 28.3 %copy-start.51 = (f32[512]{0:T(512)}, f32[512]{0:T(512)S(1)}, u32[]{:S(2)}) copy-start(f32[512]{0:T(512)S(1)} %broadcast_multiply_fusion) | copy-start | bytes 6148
  163.2 28.0 %copy-start.57 = (f32[512]{0:T(512)}, f32[512]{0:T(512)S(1)}, u32[]{:S(2)}) copy-start(f32[512]{0:T(512)S(1)} %fusion.63) | copy-start | bytes 6148
  163.2 5.3 copy-start.13
  163.2 5.3 copy-start.42
  163.2 24.4 %slice-start = ((s8[4718592]{0:T(1024)(128)(4,1)}), s8[4194304]{0:T(1024)(128)(4,1)S(1)}, s32[]{:S(2)}) async-start(s8[4718592]{0:T(1024)(128)(4,1)} %bitcast.234), calls=%async_computation.11 | async-start | bytes 8388608
  168.5 19.1 %copy-start.17 = (f32[512,3072]{1,0:T(8,128)}, f32[512,3072]{1,0:T(8,128)S(1)}, u32[]{:S(2)}) copy-start(f32[512,3072]{1,0:T(8,128)S(1)} %fusion.76) | copy-start | bytes 18874372
  168.6 19.1 %slice-start.1 = ((s8[4718592]{0:T(1024)(128)(4,1)}), s8[524288]{0:T(1024)(128)(4,1)S(1)}, s32[]{:S(2)}) async-start(s8[4718592]{0:T(1024)(128)(4,1)} %bitcast.234), calls=%async_computation.12 | async-start | bytes 1048576
  196.6 224.5 %reduce-scatter.8.cloned.1.call-start = ((), (), s32[]{:S(2)}) async-start(), calls=%async_computation.5 | async-start | bytes 4423680 | tf_op jit(solution)/shard_map/reduce_scatter | solution.py:233
  202.9 7.9 %copy-start.41 = (pred[2,256]{1,0:T(4,128)(4,1)S(1)}, pred[2,256]{1,0:T(4,128)(4,1)}, u32[]{:S(2)}) copy-start(pred[2,256]{1,0:T(4,128)(4,1)} %copy-done.40) | copy-start | bytes 1540
  224.5 11.7 %collective-permute-start.2 = (bf16[2,256,768]{1,2,0:T(8,128)(2,1)}, bf16[2,256,768]{1,2,0:T(8,128)(2,1)}, u32[]{:S(2)}, u32[]{:S(2)}) collective-permute-start(bf16[2,256,768]{1,2,0:T(8,128)(2,1)} %get-tuple-element.934), channel_id=1, source_target_pairs={{3,0},{0,1},{1,2},{2,3},{7,4},{4,5},{5,6},{6,7},{11,8},{8,9},{9,10... | collective-permute-start | bytes 2359304 | tf_op jit(solution)/shard_map/while/body/eval_jaxpr/ppermute | solution.py:21
  224.5 20.2 %collective-permute-start.3 = (bf16[2,256,768]{1,2,0:T(8,128)(2,1)}, bf16[2,256,768]{1,2,0:T(8,128)(2,1)}, u32[]{:S(2)}, u32[]{:S(2)}) collective-permute-start(bf16[2,256,768]{1,2,0:T(8,128)(2,1)} %get-tuple-element.935), channel_id=1, source_target_pairs={{3,0},{0,1},{1,2},{2,3},{7,4},{4,5},{5,6},{6,7},{11,8},{8,9},{9,10... | collective-permute-start | bytes 2359304 | tf_op jit(solution)/shard_map/while/body/eval_jaxpr/ppermute | solution.py:21
  225.4 27.6 %collective-permute-start.5 = (bf16[2,256,768]{1,2,0:T(8,128)(2,1)}, bf16[2,256,768]{1,2,0:T(8,128)(2,1)}, u32[]{:S(2)}, u32[]{:S(2)}) collective-permute-start(bf16[2,256,768]{1,2,0:T(8,128)(2,1)} %get-tuple-element.933), channel_id=1, source_target_pairs={{3,0},{0,1},{1,2},{2,3},{7,4},{4,5},{5,6},{6,7},{11,8},{8,9},{9,10... | collective-permute-start | bytes 2359304 | tf_op jit(solution)/shard_map/while/body/eval_jaxpr/ppermute | solution.py:21
  225.5 37.9 %collective-permute-start.4 = (bf16[2,256,768]{1,2,0:T(8,128)(2,1)}, bf16[2,256,768]{1,2,0:T(8,128)(2,1)}, u32[]{:S(2)}, u32[]{:S(2)}) collective-permute-start(bf16[2,256,768]{1,2,0:T(8,128)(2,1)} %get-tuple-element.932), channel_id=1, source_target_pairs={{3,0},{0,1},{1,2},{2,3},{7,4},{4,5},{5,6},{6,7},{11,8},{8,9},{9,10... | collective-permute-start | bytes 2359304 | tf_op jit(solution)/shard_map/while/body/eval_jaxpr/ppermute | solution.py:21
  238.7 5.9 copy-start.30
  248.1 11.6 %copy-start.1 = (bf16[2,256,12,64]{1,3,2,0:T(8,128)(2,1)S(1)}, bf16[2,256,12,64]{1,3,2,0:T(8,128)(2,1)}, u32[]{:S(2)}) copy-start(bf16[2,256,12,64]{1,3,2,0:T(8,128)(2,1)} %get-tuple-element.955) | copy-start | bytes 2359300 | tf_op jit(solution)/shard_map/while
  266.2 11.7 %collective-permute-start.2 = (bf16[2,256,768]{1,2,0:T(8,128)(2,1)}, bf16[2,256,768]{1,2,0:T(8,128)(2,1)}, u32[]{:S(2)}, u32[]{:S(2)}) collective-permute-start(bf16[2,256,768]{1,2,0:T(8,128)(2,1)} %get-tuple-element.934), channel_id=1, source_target_pairs={{3,0},{0,1},{1,2},{2,3},{7,4},{4,5},{5,6},{6,7},{11,8},{8,9},{9,10... | collective-permute-start | bytes 2359304 | tf_op jit(solution)/shard_map/while/body/eval_jaxpr/ppermute | solution.py:21
  266.2 20.2 %collective-permute-start.3 = (bf16[2,256,768]{1,2,0:T(8,128)(2,1)}, bf16[2,256,768]{1,2,0:T(8,128)(2,1)}, u32[]{:S(2)}, u32[]{:S(2)}) collective-permute-start(bf16[2,256,768]{1,2,0:T(8,128)(2,1)} %get-tuple-element.935), channel_id=1, source_target_pairs={{3,0},{0,1},{1,2},{2,3},{7,4},{4,5},{5,6},{6,7},{11,8},{8,9},{9,10... | collective-permute-start | bytes 2359304 | tf_op jit(solution)/shard_map/while/body/eval_jaxpr/ppermute | solution.py:21
  267.1 27.6 %collective-permute-start.5 = (bf16[2,256,768]{1,2,0:T(8,128)(2,1)}, bf16[2,256,768]{1,2,0:T(8,128)(2,1)}, u32[]{:S(2)}, u32[]{:S(2)}) collective-permute-start(bf16[2,256,768]{1,2,0:T(8,128)(2,1)} %get-tuple-element.933), channel_id=1, source_target_pairs={{3,0},{0,1},{1,2},{2,3},{7,4},{4,5},{5,6},{6,7},{11,8},{8,9},{9,10... | collective-permute-start | bytes 2359304 | tf_op jit(solution)/shard_map/while/body/eval_jaxpr/ppermute | solution.py:21
  267.2 37.9 %collective-permute-start.4 = (bf16[2,256,768]{1,2,0:T(8,128)(2,1)}, bf16[2,256,768]{1,2,0:T(8,128)(2,1)}, u32[]{:S(2)}, u32[]{:S(2)}) collective-permute-start(bf16[2,256,768]{1,2,0:T(8,128)(2,1)} %get-tuple-element.932), channel_id=1, source_target_pairs={{3,0},{0,1},{1,2},{2,3},{7,4},{4,5},{5,6},{6,7},{11,8},{8,9},{9,10... | collective-permute-start | bytes 2359304 | tf_op jit(solution)/shard_map/while/body/eval_jaxpr/ppermute | solution.py:21
  280.4 5.9 copy-start.30
  289.8 11.6 %copy-start.1 = (bf16[2,256,12,64]{1,3,2,0:T(8,128)(2,1)S(1)}, bf16[2,256,12,64]{1,3,2,0:T(8,128)(2,1)}, u32[]{:S(2)}) copy-start(bf16[2,256,12,64]{1,3,2,0:T(8,128)(2,1)} %get-tuple-element.955) | copy-start | bytes 2359300 | tf_op jit(solution)/shard_map/while
  307.9 11.7 %collective-permute-start.2 = (bf16[2,256,768]{1,2,0:T(8,128)(2,1)}, bf16[2,256,768]{1,2,0:T(8,128)(2,1)}, u32[]{:S(2)}, u32[]{:S(2)}) collective-permute-start(bf16[2,256,768]{1,2,0:T(8,128)(2,1)} %get-tuple-element.934), channel_id=1, source_target_pairs={{3,0},{0,1},{1,2},{2,3},{7,4},{4,5},{5,6},{6,7},{11,8},{8,9},{9,10... | collective-permute-start | bytes 2359304 | tf_op jit(solution)/shard_map/while/body/eval_jaxpr/ppermute | solution.py:21
  307.9 20.2 %collective-permute-start.3 = (bf16[2,256,768]{1,2,0:T(8,128)(2,1)}, bf16[2,256,768]{1,2,0:T(8,128)(2,1)}, u32[]{:S(2)}, u32[]{:S(2)}) collective-permute-start(bf16[2,256,768]{1,2,0:T(8,128)(2,1)} %get-tuple-element.935), channel_id=1, source_target_pairs={{3,0},{0,1},{1,2},{2,3},{7,4},{4,5},{5,6},{6,7},{11,8},{8,9},{9,10... | collective-permute-start | bytes 2359304 | tf_op jit(solution)/shard_map/while/body/eval_jaxpr/ppermute | solution.py:21
  308.8 27.6 %collective-permute-start.5 = (bf16[2,256,768]{1,2,0:T(8,128)(2,1)}, bf16[2,256,768]{1,2,0:T(8,128)(2,1)}, u32[]{:S(2)}, u32[]{:S(2)}) collective-permute-start(bf16[2,256,768]{1,2,0:T(8,128)(2,1)} %get-tuple-element.933), channel_id=1, source_target_pairs={{3,0},{0,1},{1,2},{2,3},{7,4},{4,5},{5,6},{6,7},{11,8},{8,9},{9,10... | collective-permute-start | bytes 2359304 | tf_op jit(solution)/shard_map/while/body/eval_jaxpr/ppermute | solution.py:21
  308.9 37.9 %collective-permute-start.4 = (bf16[2,256,768]{1,2,0:T(8,128)(2,1)}, bf16[2,256,768]{1,2,0:T(8,128)(2,1)}, u32[]{:S(2)}, u32[]{:S(2)}) collective-permute-start(bf16[2,256,768]{1,2,0:T(8,128)(2,1)} %get-tuple-element.932), channel_id=1, source_target_pairs={{3,0},{0,1},{1,2},{2,3},{7,4},{4,5},{5,6},{6,7},{11,8},{8,9},{9,10... | collective-permute-start | bytes 2359304 | tf_op jit(solution)/shard_map/while/body/eval_jaxpr/ppermute | solution.py:21
  322.1 5.9 copy-start.30
  331.5 11.6 %copy-start.1 = (bf16[2,256,12,64]{1,3,2,0:T(8,128)(2,1)S(1)}, bf16[2,256,12,64]{1,3,2,0:T(8,128)(2,1)}, u32[]{:S(2)}) copy-start(bf16[2,256,12,64]{1,3,2,0:T(8,128)(2,1)} %get-tuple-element.955) | copy-start | bytes 2359300 | tf_op jit(solution)/shard_map/while
  351.9 11.7 %collective-permute-start.6 = (bf16[2,256,768]{2,1,0:T(8,128)(2,1)}, bf16[2,256,768]{2,1,0:T(8,128)(2,1)}, u32[]{:S(2)}, u32[]{:S(2)}) collective-permute-start(bf16[2,256,768]{2,1,0:T(8,128)(2,1)} %copy.120), channel_id=1, source_target_pairs={{3,0},{0,1},{1,2},{2,3},{7,4},{4,5},{5,6},{6,7},{11,8},{8,9},{9,10... | collective-permute-start | bytes 2359304 | tf_op jit(solution)/shard_map/ppermute | solution.py:21
  354.2 17.9 %collective-permute-start.7 = (bf16[2,256,768]{2,1,0:T(8,128)(2,1)}, bf16[2,256,768]{2,1,0:T(8,128)(2,1)}, u32[]{:S(2)}, u32[]{:S(2)}) collective-permute-start(bf16[2,256,768]{2,1,0:T(8,128)(2,1)} %copy.121), channel_id=1, source_target_pairs={{3,0},{0,1},{1,2},{2,3},{7,4},{4,5},{5,6},{6,7},{11,8},{8,9},{9,10... | collective-permute-start | bytes 2359304 | tf_op jit(solution)/shard_map/ppermute | solution.py:21
  380.0 91.5 %reduce-scatter.14.cloned.1.call-start = ((), (), s32[]{:S(2)}) async-start(), calls=%async_computation.8 | async-start | bytes 5898240 | tf_op jit(solution)/shard_map/reduce_scatter | solution.py:257
  380.7 7.9 %copy-start.14 = (bf16[2,1,256,768]{3,2,1,0:T(8,128)(2,1)S(1)}, bf16[2,1,256,768]{3,2,1,0:T(8,128)(2,1)}, u32[]{:S(2)}) copy-start(bf16[2,1,256,768]{3,2,1,0:T(8,128)(2,1)} %param.33) | copy-start | bytes 2359300
  392.9 129.0 %reduce-scatter.12.cloned.1.call-start = ((), (), s32[]{:S(2)}) async-start(), calls=%async_computation.7 | async-start | bytes 5898240 | tf_op jit(solution)/shard_map/reduce_scatter | solution.py:251
  401.0 125.3 %copy-start.63 = (bf16[768]{0:T(1024)(128)(2,1)S(1)}, bf16[768]{0:T(1024)(128)(2,1)}, u32[]{:S(2)}) copy-start(bf16[768]{0:T(1024)(128)(2,1)} %param.32) | copy-start | bytes 4612
  401.0 162.6 %reduce-scatter.16.cloned.1.call-start = ((), (), s32[]{:S(2)}) async-start(), calls=%async_computation.9 | async-start | bytes 245760
  403.3 286.4 %all-reduce.12.cloned.1.call-start = ((), (), s32[]{:S(2)}) async-start(), calls=%async_computation.10 | async-start | bytes 7077888 | tf_op jit(solution)/shard_map/psum | solution.py:267
  526.4 7.4 %copy-start.9 = (bf16[2,1,256,768]{3,2,1,0:T(8,128)(2,1)S(1)}, bf16[2,1,256,768]{3,2,1,0:T(8,128)(2,1)}, u32[]{:S(2)}) copy-start(bf16[2,1,256,768]{3,2,1,0:T(8,128)(2,1)} %param.19) | copy-start | bytes 2359300
  526.4 7.4 %copy-start.34 = (bf16[96,8,2,256]{3,1,2,0:T(8,128)(2,1)S(1)}, bf16[96,8,2,256]{3,1,2,0:T(8,128)(2,1)}, u32[]{:S(2)}) copy-start(bf16[96,8,2,256]{3,1,2,0:T(8,128)(2,1)} %copy.137) | copy-start | bytes 2359300
  526.4 7.4 %copy-start.35 = (bf16[512,768]{0,1:T(8,128)(2,1)S(1)}, bf16[512,768]{0,1:T(8,128)(2,1)}, u32[]{:S(2)}) copy-start(bf16[512,768]{0,1:T(8,128)(2,1)} %copy.122) | copy-start | bytes 2359300
  526.4 7.4 %copy-start.36 = (bf16[512,768]{0,1:T(8,128)(2,1)S(1)}, bf16[512,768]{0,1:T(8,128)(2,1)}, u32[]{:S(2)}) copy-start(bf16[512,768]{0,1:T(8,128)(2,1)} %copy.123) | copy-start | bytes 2359300
  526.4 7.4 %copy-start.39 = (f32[768]{0:T(1024)S(1)}, f32[768]{0:T(1024)}, u32[]{:S(2)}) copy-start(f32[768]{0:T(1024)} %copy-done.38) | copy-start | bytes 9220
  526.4 7.4 %copy-start.45 = (f32[1,2,2,128]{3,1,2,0:T(2,128)S(1)}, f32[1,2,2,128]{3,1,2,0:T(2,128)}, u32[]{:S(2)}) copy-start(f32[1,2,2,128]{3,1,2,0:T(2,128)} %copy-done.44) | copy-start | bytes 6148
  533.9 25.6 %copy-start.49 = (f32[512]{0:T(512)S(1)}, f32[512]{0:T(512)}, u32[]{:S(2)}) copy-start(f32[512]{0:T(512)} %copy-done.48) | copy-start | bytes 6148
  (54 other events, 150.2 us)
Sparse Core Ops, SparseCore 0:
  196.8 26.2 reduce-scatter.9
  380.1 40.9 reduce-scatter.7
  423.6 47.8 reduce-scatter.13
  474.1 47.7 reduce-scatter.11
  524.8 19.9 reduce-scatter.15
  548.5 141.1 all-reduce.11
where the time goes:
time: 717 us; the launch traced here: 705 us
  waiting for transfers between devices  321 us (45%)
  matrix products  128 us (18%)
  local copies, waits for them, and re-layouts  105 us (15%)
  other arithmetic  77.3 us (11%)
  blocking collectives  43.7 us (6%)
  between operations  16.6 us (2%)
  starting transfers between devices  11.2 us (2%)
    ppermute x20, waiting for transfers between devices, from_behind(): return lax.ppermute(block, axis, route)  110 us
    psum x1, waiting for transfers between devices, local(): lax.psum(shares[2].astype(jnp.bfloat16), 'clip').astype(jnp.float32)  93.4 us
    reduce_scatter x1, waiting for transfers between devices, local(): lax.psum_scatter(grad_reduce_weight.astype(jnp.bfloat16), 'frame', scatte...  50.4 us
    reduce_scatter x1, waiting for transfers between devices, local(): lax.psum_scatter(grad_expand_weight.astype(jnp.bfloat16), 'frame', scatte...  50.4 us
    while x81, local copies, waits for them, and re-layouts  31.1 us
    psum x1, blocking collectives, local(): lax.psum(shares[0].astype(jnp.bfloat16), 'clip').astype(jnp.float32)  23.9 us
    unnamed x135, local copies, waits for them, and re-layouts  22.8 us
    dot_general x1, matrix products, local(): jnp.dot(upstream_low, reduce_weight.T, preferred_element_type=jnp.float32)  19.1 us
  transfers between devices with their start and end apart: 26, of which 21 were waited for; matrix products, arithmetic and copies ran while one was open for 25% of the time, Pallas kernels for 0%

commit v1 on v0

--- a/solution.py
+++ b/solution.py
@@ -1,6 +1,9 @@
+import functools
 import jax
 import jax.numpy as jnp
 from jax import lax
+from jax.experimental import pallas as pl
+from jax.experimental.pallas import tpu as pltpu
 from jax.sharding import PartitionSpec as P
 
 D = 768
@@ -83,6 +86,280 @@
         preferred_element_type=jnp.float32,
     )
     return (grad_query, grad_keys.reshape(MICRO, BLOCK, D), grad_values.reshape(MICRO, BLOCK, D))
+
+
+MESH = pl.DeviceIdType.MESH
+K = 36
+QR = 384
+HR = 192
+
+
+class Place:
+    def __init__(self):
+        self.clip = lax.axis_index("clip")
+        self.frame = lax.axis_index("frame")
+        self.x = lax.rem(self.clip, 2)
+        self.z = self.clip // 2
+        self.core = lax.rem(self.frame, 2)
+        self.y = self.frame // 2
+        self.outer = jnp.logical_or(self.z == 0, self.z == 3)
+        self.inner = jnp.logical_not(self.outer)
+        self.to_core = (self.clip, self.y * 2 + (1 - self.core))
+        self.to_y = (self.clip, (1 - self.y) * 2 + self.core)
+        self.to_x = (self.z * 2 + (1 - self.x), self.frame)
+        mate = self.z + 1 - 2 * lax.rem(self.z, 2)
+        self.to_mate = (mate * 2 + self.x, self.frame)
+        self.to_inner = ((3 - self.z) * 2 + self.x, self.frame)
+
+
+def enter(place):
+    barrier = pltpu.get_barrier_semaphore()
+    for peer in (place.to_core, place.to_y, place.to_x, place.to_mate):
+        pl.semaphore_signal(barrier, inc=1, device_id=peer, device_id_type=MESH)
+
+    @pl.when(place.inner)
+    def _():
+        pl.semaphore_signal(barrier, inc=1, device_id=place.to_inner, device_id_type=MESH)
+
+    pl.semaphore_wait(barrier, jnp.where(place.inner, 5, 4))
+
+
+class Reduce:
+    def __init__(self, place, bufs, send, recv):
+        self.p = place
+        self.own, self.nbr, self.rc, self.ry, self.rx, self.r1, self.r2, self.ra = bufs
+        self.send, self.recv = send, recv
+
+    def copy(self, src, dst, stage, k, peer):
+        return pltpu.make_async_remote_copy(
+            src_ref=src,
+            dst_ref=dst,
+            send_sem=self.send.at[stage, k],
+            recv_sem=self.recv.at[stage, k],
+            device_id=peer,
+            device_id_type=MESH,
+        )
+
+    def half(self, k):
+        return self.own.at[k, self.p.y, pl.ds(pl.multiple_of(self.p.x * HR, HR), HR)]
+
+    def far_half(self, k):
+        start = pl.multiple_of((1 - self.p.x) * HR, HR)
+        return self.own.at[k, self.p.y, pl.ds(start, HR)]
+
+    def c_core(self, k):
+        return self.copy(self.nbr.at[k], self.rc.at[k], 0, k, self.p.to_core)
+
+    def c_y(self, k):
+        return self.copy(self.own.at[k, 1 - self.p.y], self.ry.at[k], 1, k, self.p.to_y)
+
+    def c_x(self, k):
+        return self.copy(self.far_half(k), self.rx.at[k], 2, k, self.p.to_x)
+
+    def c_in(self, k):
+        return self.copy(self.half(k), self.r1.at[k], 3, k, self.p.to_mate)
+
+    def c_mid(self, k):
+        return self.copy(self.half(k), self.r2.at[k], 4, k, self.p.to_inner)
+
+    def c_out(self, k):
+        return self.copy(self.r2.at[k], self.r1.at[k], 3, k, self.p.to_mate)
+
+    def c_gather(self, k, inner):
+        src = self.r2 if inner else self.r1
+        return self.copy(src.at[k], self.ra.at[k], 5, k, self.p.to_x)
+
+    def begin(self, k):
+        self.c_core(k).start()
+
+    def stage_core(self, k):
+        self.c_core(k).wait_recv()
+        self.own[k] = self.own[k] + self.rc[k]
+        self.c_y(k).start()
+
+    def stage_y(self, k):
+        self.c_y(k).wait_recv()
+        self.own[k, self.p.y] = self.own[k, self.p.y] + self.ry[k]
+        self.c_x(k).start()
+
+    def stage_x(self, k):
+        self.c_x(k).wait_recv()
+        half = self.half(k)
+        half[...] = half[...] + self.rx[k]
+
+        @pl.when(self.p.outer)
+        def _():
+            self.c_in(k).start()
+
+    def stage_in(self, k):
+        @pl.when(self.p.inner)
+        def _():
+            self.c_in(k).wait_recv()
+            half = self.half(k)
+            half[...] = half[...] + self.r1[k]
+            self.c_mid(k).start()
+
+    def stage_mid(self, k):
+        @pl.when(self.p.inner)
+        def _():
+            self.c_mid(k).wait_recv()
+            self.r2[k] = self.r2[k] + self.half(k)[...]
+            self.c_out(k).start()
+            self.c_gather(k, True).start()
+
+    def stage_out(self, k):
+        @pl.when(self.p.outer)
+        def _():
+            self.c_in(k).wait_recv()
+            self.c_gather(k, False).start()
+
+    def stage_done(self, k):
+        self.c_gather(k, True).wait_recv()
+        self.c_core(k).wait_send()
+        self.c_y(k).wait_send()
+        self.c_x(k).wait_send()
+        self.c_in(k).wait_send()
+        self.c_gather(k, True).wait_send()
+
+        @pl.when(self.p.inner)
+        def _():
+            self.c_mid(k).wait_send()
+
+        mine = jnp.where(self.p.outer, self.r1[k], self.r2[k]).astype(jnp.float32)
+        theirs = self.ra[k].astype(jnp.float32)
+        first = self.p.x == 0
+        return jnp.where(first, mine, theirs), jnp.where(first, theirs, mine)
+
+
+LAGS = (0, 2, 4, 5, 6, 7, 9)
+
+
+def reduce_kernel(own_ref, nbr_ref, out_ref, own, nbr, rc, ry, rx, r1, r2, ra, stage, send, recv, lsem, osem):
+    place = Place()
+    enter(place)
+    red = Reduce(place, (own, nbr, rc, ry, rx, r1, r2, ra), send, recv)
+
+    def load(k):
+        return (
+            pltpu.make_async_copy(own_ref.at[k], own.at[k], lsem.at[0, k]),
+            pltpu.make_async_copy(nbr_ref.at[k], nbr.at[k], lsem.at[1, k]),
+        )
+
+    def kick(k, _):
+        for one in load(k):
+            one.start()
+        return 0
+
+    lax.fori_loop(0, K, kick, 0)
+
+    def begin(k, _):
+        for one in load(k):
+            one.wait()
+        red.begin(k)
+        return 0
+
+    lax.fori_loop(0, K, begin, 0)
+
+    def store(k):
+        slot = lax.rem(k, 2)
+        return pltpu.make_async_copy(stage.at[slot], out_ref.at[k], osem.at[slot])
+
+    def finish(k):
+        @pl.when(k >= 2)
+        def _():
+            store(k - 2).wait()
+
+        one, two = red.stage_done(k)
+        slot = lax.rem(k, 2)
+        stage[slot, pl.ds(0, HR)] = one
+        stage[slot, pl.ds(HR, HR)] = two
+        store(k).start()
+
+    steps = (red.stage_core, red.stage_y, red.stage_x, red.stage_in, red.stage_mid, red.stage_out, finish)
+
+    def tick(t, _):
+        for lag, step in zip(LAGS, steps):
+            k = t - lag
+
+            @pl.when(jnp.logical_and(k >= 0, k < K))
+            def _():
+                step(k)
+
+        return 0
+
+    lax.fori_loop(0, K + LAGS[-1], tick, 0)
+    store(K - 2).wait()
+    store(K - 1).wait()
+
+
+def reduce_all(own, nbr):
+    bf = jnp.bfloat16
+    return pl.pallas_call(
+        reduce_kernel,
+        out_shape=jax.ShapeDtypeStruct((K, QR, 128), jnp.float32),
+        in_specs=[pl.BlockSpec(memory_space=pl.ANY)] * 2,
+        out_specs=pl.BlockSpec(memory_space=pl.ANY),
+        scratch_shapes=[
+            pltpu.VMEM((K, 2, QR, 128), bf),
+            pltpu.VMEM((K, 2, QR, 128), bf),
+            pltpu.VMEM((K, 2, QR, 128), bf),
+            pltpu.VMEM((K, QR, 128), bf),
+            pltpu.VMEM((K, HR, 128), bf),
+            pltpu.VMEM((K, HR, 128), bf),
+            pltpu.VMEM((K, HR, 128), bf),
+            pltpu.VMEM((K, HR, 128), bf),
+            pltpu.VMEM((2, QR, 128), jnp.float32),
+            pltpu.SemaphoreType.DMA((6, K)),
+            pltpu.SemaphoreType.DMA((6, K)),
+            pltpu.SemaphoreType.DMA((2, K)),
+            pltpu.SemaphoreType.DMA((2,)),
+        ],
+        compiler_params=pltpu.CompilerParams(
+            collective_id=0, has_side_effects=True, vmem_limit_bytes=60 << 20
+        ),
+    )(own, nbr)
+
+
+def pack_wide(grad):
+    n = grad.shape[1] // 256
+    parts = grad.reshape(4, 192, n, 2, 128)
+    return jnp.transpose(parts, (2, 0, 3, 1, 4)).reshape(n, 4, QR, 128)
+
+
+def unpack_wide(parts):
+    n = parts.shape[0]
+    return jnp.transpose(parts.reshape(n, 2, 192, 128), (2, 0, 1, 3)).reshape(192, n * 256)
+
+
+def pack_tall(grad):
+    parts = grad.reshape(4, 6, 128, 2, 3, 128)
+    return jnp.transpose(parts, (1, 3, 0, 4, 2, 5)).reshape(12, 4, QR, 128)
+
+
+def unpack_tall(parts):
+    parts = parts.reshape(6, 2, 3, 128, 128)
+    return jnp.transpose(parts, (0, 3, 1, 2, 4)).reshape(768, 768)
+
+
+def reduce_weights(in_w, out_w, exp_w, red_w):
+    packed = jnp.concatenate(
+        [
+            pack_tall(red_w.astype(jnp.bfloat16)),
+            pack_wide(exp_w.astype(jnp.bfloat16)),
+            pack_wide(out_w.astype(jnp.bfloat16)),
+            pack_wide(in_w.astype(jnp.bfloat16)),
+        ]
+    ).reshape(K, 2, 2, QR, 128)
+    core = lax.axis_index("frame") % 2
+    own = lax.dynamic_index_in_dim(packed, core, 2, keepdims=False)
+    nbr = lax.dynamic_index_in_dim(packed, 1 - core, 2, keepdims=False)
+    done = reduce_all(own, nbr)
+    return (
+        unpack_wide(done[27:36]),
+        unpack_wide(done[24:27]),
+        unpack_wide(done[12:24]),
+        unpack_tall(done[0:12]),
+    )
 
 
 def local(
@@ -293,9 +570,211 @@
     )
 
 
+def local_slice(
+    tokens,
+    counts,
+    first_gain,
+    first_bias,
+    input_weight,
+    input_bias,
+    output_weight,
+    output_bias,
+    second_gain,
+    second_bias,
+    expand_weight,
+    expand_bias,
+    reduce_weight,
+    reduce_bias,
+    cotangent,
+):
+    members = lax.axis_size("frame")
+    myself = lax.axis_index("frame")
+    total_rows = MICRO * BLOCK
+    seq_in = tokens.reshape(total_rows, D).astype(jnp.float32)
+    every_count = lax.all_gather(counts.reshape(MICRO, FRAME_DEV), "frame", axis=1, tiled=True)
+    gain_one = first_gain.astype(jnp.float32)
+    shift_one = first_bias.astype(jnp.float32)
+    gain_two = second_gain.astype(jnp.float32)
+    shift_two = second_bias.astype(jnp.float32)
+    qv_bias = input_bias.astype(jnp.float32)
+    first_low = norm_rows(seq_in, gain_one, shift_one).astype(jnp.bfloat16)
+    projected = jnp.dot(first_low, input_weight, preferred_element_type=jnp.float32)
+    query = (
+        ((projected[:, :D] + qv_bias[0]) * 0.125).astype(jnp.bfloat16).reshape(MICRO, BLOCK, H, HD)
+    )
+    keys = projected[:, D : 2 * D].astype(jnp.bfloat16).reshape(MICRO, BLOCK, D)
+    values = (projected[:, 2 * D :] + qv_bias[1]).astype(jnp.bfloat16).reshape(MICRO, BLOCK, D)
+    start = (
+        jnp.full((MICRO, H, BLOCK, 1), -1e30, jnp.float32),
+        jnp.zeros((MICRO, H, BLOCK, 1), jnp.float32),
+        jnp.zeros((MICRO, H, BLOCK, HD), jnp.float32),
+    )
+    state = absorb(start, query, keys, values, key_valid(every_count, myself))
+    stored = ()
+
+    def forward_hop(step, carry):
+        state_now, moving, kept = carry
+        moving = from_behind((moving[0], moving[1]), "frame", 1)
+        source = (myself - step) % members
+        state_now = absorb(state_now, query, moving[0], moving[1], key_valid(every_count, source))
+        return (state_now, moving, kept)
+
+    state, _, stored = lax.fori_loop(1, members, forward_hop, (state, (keys, values), stored))
+    top, total, summed = state
+    log_total = top + jnp.log(total)
+    attend_full = jnp.transpose(summed / total, (0, 2, 1, 3))
+    attend_low = attend_full.reshape(total_rows, D).astype(jnp.bfloat16)
+    middle = (
+        seq_in
+        + jnp.dot(attend_low, output_weight, preferred_element_type=jnp.float32)
+        + output_bias.astype(jnp.float32)
+    )
+    second_low = norm_rows(middle, gain_two, shift_two).astype(jnp.bfloat16)
+    before = jnp.dot(
+        second_low, expand_weight, preferred_element_type=jnp.float32
+    ) + expand_bias.astype(jnp.float32)
+    active_low = gelu_exact(before).astype(jnp.bfloat16)
+    result = (
+        middle
+        + jnp.dot(active_low, reduce_weight, preferred_element_type=jnp.float32)
+        + reduce_bias.astype(jnp.float32)
+    )
+    layer_out = result.astype(jnp.bfloat16).reshape(MICRO, 1, BLOCK, D)
+    upstream_low = cotangent.reshape(total_rows, D)
+    upstream = upstream_low.astype(jnp.float32)
+    grad_reduce_weight = jnp.dot(active_low.T, upstream_low, preferred_element_type=jnp.float32)
+    grad_reduce_bias = jnp.sum(upstream, axis=0)
+    grad_active = jnp.dot(upstream_low, reduce_weight.T, preferred_element_type=jnp.float32)
+    _, gelu_back = jax.vjp(gelu_exact, before)
+    grad_before = gelu_back(grad_active)[0].astype(jnp.bfloat16)
+    grad_expand_weight = jnp.dot(second_low.T, grad_before, preferred_element_type=jnp.float32)
+    grad_expand_bias = jnp.sum(grad_before.astype(jnp.float32), axis=0)
+    grad_second = jnp.dot(grad_before, expand_weight.T, preferred_element_type=jnp.float32)
+    _, second_back = jax.vjp(norm_rows, middle, gain_two, shift_two)
+    middle_part, grad_second_gain, grad_second_bias = second_back(grad_second)
+    grad_middle = upstream + middle_part
+    grad_branch = grad_middle.astype(jnp.bfloat16)
+    grad_output_weight = jnp.dot(attend_low.T, grad_branch, preferred_element_type=jnp.float32)
+    grad_output_bias = jnp.sum(grad_branch.astype(jnp.float32), axis=0)
+    grad_attend = jnp.dot(grad_branch, output_weight.T, preferred_element_type=jnp.float32).astype(
+        jnp.bfloat16
+    )
+    grad_heads = grad_attend.reshape(MICRO, BLOCK, H, HD)
+    delta = jnp.transpose(
+        jnp.sum(grad_heads.astype(jnp.float32) * attend_full, axis=-1), (0, 2, 1)
+    )[..., None]
+    first_terms = block_back(
+        query, keys, values, key_valid(every_count, myself), log_total, delta, grad_heads
+    )
+
+    def backward_hop(step, carry):
+        grad_query, running, moving = carry
+        running = (
+            from_behind(running[0].astype(jnp.bfloat16), "frame", 1).astype(jnp.float32),
+            from_behind(running[1].astype(jnp.bfloat16), "frame", 1).astype(jnp.float32),
+        )
+        current = from_behind((moving[0], moving[1]), "frame", 1)
+        source = (myself - step) % members
+        add_query, add_keys, add_values = block_back(
+            query,
+            current[0],
+            current[1],
+            key_valid(every_count, source),
+            log_total,
+            delta,
+            grad_heads,
+        )
+        return (grad_query + add_query, (running[0] + add_keys, running[1] + add_values), current)
+
+    grad_query, running, _ = lax.fori_loop(
+        1, members, backward_hop, (first_terms[0], (first_terms[1], first_terms[2]), (keys, values))
+    )
+    finished = (
+        from_behind(running[0].astype(jnp.bfloat16), "frame", 1).astype(jnp.float32),
+        from_behind(running[1].astype(jnp.bfloat16), "frame", 1).astype(jnp.float32),
+    )
+    query_low = grad_query.astype(jnp.bfloat16).reshape(total_rows, D) * 0.125
+    keys_low = finished[0].astype(jnp.bfloat16).reshape(total_rows, D)
+    values_low = finished[1].astype(jnp.bfloat16).reshape(total_rows, D)
+    grad_projected = jnp.concatenate([query_low, keys_low, values_low], axis=1)
+    grad_input_weight = jnp.dot(first_low.T, grad_projected, preferred_element_type=jnp.float32)
+    grad_input_bias = jnp.stack(
+        [
+            jnp.sum(query_low.astype(jnp.float32), axis=0),
+            jnp.sum(values_low.astype(jnp.float32), axis=0),
+        ]
+    )
+    grad_first = jnp.dot(grad_projected, input_weight.T, preferred_element_type=jnp.float32)
+    _, first_back = jax.vjp(norm_rows, seq_in, gain_one, shift_one)
+    input_part, grad_first_gain, grad_first_bias = first_back(grad_first)
+    grad_tokens = (grad_middle + input_part).reshape(MICRO, 1, BLOCK, D)
+    shares = (
+        lax.psum_scatter(
+            grad_first_gain.astype(jnp.bfloat16), "frame", scatter_dimension=0, tiled=True
+        ).astype(jnp.float32),
+        lax.psum_scatter(
+            grad_first_bias.astype(jnp.bfloat16), "frame", scatter_dimension=0, tiled=True
+        ).astype(jnp.float32),
+        None,
+        lax.psum_scatter(
+            grad_input_bias.astype(jnp.bfloat16), "frame", scatter_dimension=1, tiled=True
+        ).astype(jnp.float32),
+        None,
+        lax.psum_scatter(
+            grad_output_bias.astype(jnp.bfloat16), "frame", scatter_dimension=0, tiled=True
+        ).astype(jnp.float32),
+        lax.psum_scatter(
+            grad_second_gain.astype(jnp.bfloat16), "frame", scatter_dimension=0, tiled=True
+        ).astype(jnp.float32),
+        lax.psum_scatter(
+            grad_second_bias.astype(jnp.bfloat16), "frame", scatter_dimension=0, tiled=True
+        ).astype(jnp.float32),
+        None,
+        lax.psum_scatter(
+            grad_expand_bias.astype(jnp.bfloat16), "frame", scatter_dimension=0, tiled=True
+        ).astype(jnp.float32),
+        None,
+        lax.psum_scatter(
+            grad_reduce_bias.astype(jnp.bfloat16), "frame", scatter_dimension=0, tiled=True
+        ).astype(jnp.float32),
+    )
+    big = reduce_weights(grad_input_weight, grad_output_weight, grad_expand_weight, grad_reduce_weight)
+    totals = (
+        lax.psum(shares[0].astype(jnp.bfloat16), "clip").astype(jnp.float32),
+        lax.psum(shares[1].astype(jnp.bfloat16), "clip").astype(jnp.float32),
+        big[0],
+        lax.psum(shares[3].astype(jnp.bfloat16), "clip").astype(jnp.float32),
+        big[1],
+        lax.psum(shares[5].astype(jnp.bfloat16), "clip").astype(jnp.float32),
+        lax.psum(shares[6].astype(jnp.bfloat16), "clip").astype(jnp.float32),
+        lax.psum(shares[7].astype(jnp.bfloat16), "clip").astype(jnp.float32),
+        big[2],
+        lax.psum(shares[9].astype(jnp.bfloat16), "clip").astype(jnp.float32),
+        big[3],
+        lax.psum(shares[11].astype(jnp.bfloat16), "clip").astype(jnp.float32),
+    )
+    return (
+        layer_out,
+        grad_tokens,
+        totals[0],
+        totals[1],
+        totals[2],
+        totals[3],
+        totals[4],
+        totals[5],
+        totals[6],
+        totals[7],
+        totals[8],
+        totals[9],
+        totals[10],
+        totals[11],
+    )
+
+
 def solution(mesh):
+    fits = mesh.shape["clip"] == 8 and mesh.shape["frame"] == 4
     return jax.shard_map(
-        local,
+        local_slice if fits else local,
         mesh=mesh,
         in_specs=(
             P(None, "clip", "frame", None),

time: 717 us -> 719 us (level)
  waiting for transfers between devices: 321 us -> 98.8 us
  Pallas kernels: 0 us -> 120 us
  local copies, waits for them, and re-layouts: 105 us -> 212 us
    pallas_call x0 -> x1, Pallas kernels: none -> 120 us  [reduce_all(): pl.pallas_call(reduce_kernel, out_shape=jax.ShapeDtypeStruct((K, QR, 128)...]
    reduce_scatter x4 -> x0, waiting for transfers between devices: 118 us -> none  [the longest x1 50.4 us: local(): lax.psum_scatter(grad_reduce_weight.astype(jnp.bfloat16), 'frame', scatte...]
    psum x1 -> x0, waiting for transfers between devices: 93.4 us -> none  [local(): lax.psum(shares[2].astype(jnp.bfloat16), 'clip').astype(jnp.float32)]
    reshape x6 -> x17, local copies, waits for them, and re-layouts: 15.2 us -> 72.9 us  [the longest x6 34.2 us: pack_wide(): parts = grad.reshape(4, 192, n, 2, 128)]
    transpose x1 -> x5, local copies, waits for them, and re-layouts: 0.01 us -> 19.7 us  [the longest x3 11.3 us: unpack_wide(): jnp.transpose(parts.reshape(n, 2, 192, 128), (2, 0, 1, 3))]
    ppermute x20, waiting for transfers between devices: 110 us -> 98.7 us  [from_behind(): return lax.ppermute(block, axis, route)]
    slice x3 -> x6, local copies, waits for them, and re-layouts: 3.27 us -> 13.2 us  [the longest x1 5.16 us: reduce_weights(): done[0:12]]
    convert_element_type x24 -> x20, other arithmetic: 36.6 us -> 30 us  [the longest x1 6.18 us: local_slice(): active_low = gelu_exact(before).astype(jnp.bfloat16)]
  transfers between devices with their start and end apart: 26 -> 21, of which waited for: 21 -> 15; matrix products, arithmetic and copies ran while one was open for 25% -> 33% of each run, Pallas kernels for 0% -> 17%
where the time goes in v1:
time: 719 us; the launch traced here: 705 us
  local copies, waits for them, and re-layouts  212 us (29%)
  matrix products  129 us (18%)
  Pallas kernels  120 us (17%)
  waiting for transfers between devices  98.8 us (14%)
  other arithmetic  78.9 us (11%)
  blocking collectives  38.2 us (5%)
  between operations  16.3 us (2%)
  starting transfers between devices  10.5 us (1%)
    pallas_call x1, Pallas kernels, reduce_all(): pl.pallas_call(reduce_kernel, out_shape=jax.ShapeDtypeStruct((K, QR, 128)...  120 us
    ppermute x20, waiting for transfers between devices, from_behind(): return lax.ppermute(block, axis, route)  98.7 us
    reshape x6, local copies, waits for them, and re-layouts, pack_wide(): parts = grad.reshape(4, 192, n, 2, 128)  34.2 us
    while x81, local copies, waits for them, and re-layouts  31.1 us
    unnamed x155, local copies, waits for them, and re-layouts  28.6 us
    dot_general x1, matrix products, local_slice(): jnp.dot(upstream_low, reduce_weight.T, preferred_element_type=jnp.float32)  19.5 us
    psum x1, blocking collectives, local_slice(): lax.psum(shares[0].astype(jnp.bfloat16), 'clip').astype(jnp.float32)  19.4 us
    dot_general x7, matrix products, scores_of(): jnp.einsum('mqhd,mkhd->mhqk', query, key_heads, preferred_element_type=jn...  17.9 us
  transfers between devices with their start and end apart: 21, of which 15 were waited for; matrix products, arithmetic and copies ran while one was open for 33% of the time, Pallas kernels for 17%

profile of v1, /device:TPU:0, one launch (start us, length us, event | category | flops | bytes accessed | tf_op | source)
XLA Modules:
  0.0 705.2 jit_solution(5637213362844061462)
XLA Ops:
  18.0 8.0 %all-gather = s32[2,1,16]{0,1,2:T(1,128)} all-gather(s32[2,1,4]{0,1,2:T(1,128)} %copy.102), channel_id=2, replica_groups=mesh['clip'=8,'frame'=4] {'frame'}, dimensions={2}, use_global_device_ids=true | all-gather | bytes 160 | tf_op jit(solution)/shard_map/all_gather | solution.py:594
  42.3 2.9 reshape.385
  59.7 2.9 reshape_reshape.10
  62.6 2.9 reshape_reshape.4
  73.3 83.2 %while.46 = (s32[]{:T(128)}, f32[2,12,256,1]{2,1,0,3:T(8,128)}, f32[2,12,256,1]{2,1,0,3:T(8,128)}, f32[2,12,256,64]{2,3,1,0:T(8,128)}, bf16[2,256,768]{1,2,0:T(8...) while((s32[]{:T(128)}, f32[2,12,256,1]{2,1,0,3:T(8,128)}, ...), condition=%wide.region_7.8_spmd, body=%wide.region_4.7_spmd.sunk | while | flops 416041472 | bytes 47102572 | solution.py:622
  74.8 10.5 %collective-permute-done = bf16[2,256,768]{1,2,0:T(8,128)(2,1)} collective-permute-done((bf16[2,256,768]{1,2,0:T(8,128)(2,1)}, bf16[2,256,768]{1,2,0:T(8,128)(2,1)}, u32[]{:S(2)}, u32[]{:S(2)}) %collective-permute-start) | collective-permute-done | bytes 786464 | tf_op jit(solution)/shard_map/while/body/eval_jaxpr/ppermute | solution.py:24
  89.9 3.9 collective-permute-done.1
  102.5 10.5 %collective-permute-done = bf16[2,256,768]{1,2,0:T(8,128)(2,1)} collective-permute-done((bf16[2,256,768]{1,2,0:T(8,128)(2,1)}, bf16[2,256,768]{1,2,0:T(8,128)(2,1)}, u32[]{:S(2)}, u32[]{:S(2)}) %collective-permute-start) | collective-permute-done | bytes 786464 | tf_op jit(solution)/shard_map/while/body/eval_jaxpr/ppermute | solution.py:24
  117.5 3.9 collective-permute-done.1
  121.4 2.7 multiply_add_fusion.3
  130.1 10.5 %collective-permute-done = bf16[2,256,768]{1,2,0:T(8,128)(2,1)} collective-permute-done((bf16[2,256,768]{1,2,0:T(8,128)(2,1)}, bf16[2,256,768]{1,2,0:T(8,128)(2,1)}, u32[]{:S(2)}, u32[]{:S(2)}) %collective-permute-start) | collective-permute-done | bytes 786464 | tf_op jit(solution)/shard_map/while/body/eval_jaxpr/ppermute | solution.py:24
  145.2 3.9 collective-permute-done.1
  158.9 4.2 bitcast_convert_fusion
  164.7 5.5 fusion.76
  170.3 19.5 %fusion.79 = (bf16[3072]{0:T(1024)(128)(2,1)}, bf16[512,3072]{1,0:T(8,128)(2,1)S(1)}, f32[512,3072]{1,0:T(8,128)}) fusion(f32[512,3072]{1,0:T(8,128)S(1)} %fusion.76, f32[3072]{0:T(1024)S(1)} %copy-done.46, bf16[512,768]{1,0:T(8,128)(2,1)S(1)} %bitcast.249, bf16[3072,768]{1,0:T(8,128)(2,1)S(1)} %bitcast.283), kind=kOutput, calls=%fused_computation.149 | convolution fusion | flops 2532307968 | bytes 21252096 | tf_op jit(solution)/shard_map/dot_general | solution.py:647
  189.8 3.5 multiply_reduce_fusion
  201.0 2.9 reshape.390
  208.7 5.1 fusion.27
  213.8 4.2 multiply_convert_fusion.1
  222.3 125.0 %while.47 = (s32[]{:T(128)}, f32[2,256,12,64]{1,3,2,0:T(8,128)}, bf16[2,256,768]{1,2,0:T(8,128)(2,1)}, bf16[2,256,768]{1,2,0:T(8,128)(2,1)}, bf16[2,256,768]{1,2...) while((s32[]{:T(128)}, f32[2,256,12,64]{1,3,2,0:T(8,128)}, ...), condition=%wide.region_14.15_spmd, body=%wide.region_13.14_spmd.sunk | while | flops 1021968896 | bytes 81287400 | solution.py:689
  225.1 9.1 %collective-permute-done.2 = bf16[2,256,768]{1,2,0:T(8,128)(2,1)} collective-permute-done((bf16[2,256,768]{1,2,0:T(8,128)(2,1)}, bf16[2,256,768]{1,2,0:T(8,128)(2,1)}, u32[]{:S(2)}, u32[]{:S(2)}) %collective-permute-start.2) | collective-permute-done | bytes 786464 | tf_op jit(solution)/shard_map/while/body/eval_jaxpr/ppermute | solution.py:24
  238.3 4.4 collective-permute-done.3
  242.7 3.4 multiply_convert_fusion.4
  246.2 5.0 collective-permute-done.5
  261.3 2.8 bitcast_add_fusion.12
  266.7 9.1 %collective-permute-done.2 = bf16[2,256,768]{1,2,0:T(8,128)(2,1)} collective-permute-done((bf16[2,256,768]{1,2,0:T(8,128)(2,1)}, bf16[2,256,768]{1,2,0:T(8,128)(2,1)}, u32[]{:S(2)}, u32[]{:S(2)}) %collective-permute-start.2) | collective-permute-done | bytes 786464 | tf_op jit(solution)/shard_map/while/body/eval_jaxpr/ppermute | solution.py:24
  279.9 4.4 collective-permute-done.3
  284.3 3.4 multiply_convert_fusion.4
  287.7 5.0 collective-permute-done.5
  302.9 2.8 bitcast_add_fusion.12
  308.3 9.1 %collective-permute-done.2 = bf16[2,256,768]{1,2,0:T(8,128)(2,1)} collective-permute-done((bf16[2,256,768]{1,2,0:T(8,128)(2,1)}, bf16[2,256,768]{1,2,0:T(8,128)(2,1)}, u32[]{:S(2)}, u32[]{:S(2)}) %collective-permute-start.2) | collective-permute-done | bytes 786464 | tf_op jit(solution)/shard_map/while/body/eval_jaxpr/ppermute | solution.py:24
  321.4 4.4 collective-permute-done.3
  325.9 3.4 multiply_convert_fusion.4
  329.3 5.0 collective-permute-done.5
  344.5 2.8 bitcast_add_fusion.12
  352.9 7.5 %convolution_convert_fusion.1 = bf16[768,3072]{1,0:T(8,128)(2,1)} fusion(bf16[512,3072]{1,0:T(8,128)(2,1)} %copy-done.74, f32[512,768]{1,0:T(8,128)} %copy-done.19, f32[768]{0:T(1024)S(1)} %copy-done.67, f32[768]{0:T(1024)S(1)} %copy-done.58, f32[512]{0:T(512)S(1)} %copy-done.63, f32[512]{0:T(512)S(1)} %copy-done.55), kind=kOutput, calls=%fused_computation.56 | convolution fusion | flops 2420244480 | bytes 9447424 | tf_op jit(solution)/shard_map/dot_general | solution.py:650
  367.2 6.2 multiply_convert_fusion.2
  375.1 4.7 convolution_convert_fusion.2
  379.8 6.7 copy.138
  386.5 10.4 %reshape.396 = bf16[4,6,128,2,3,128]{2,1,0,5,4,3:T(8,128)(2,1)} reshape(bf16[3072,768]{0,1:T(8,128)(2,1)} %copy.138) | data formatting | bytes 9437184 | tf_op jit(solution)/shard_map/reshape | solution.py:335
  396.9 8.4 %copy.139 = bf16[6,2,4,3,128,128]{5,4,3,2,1,0:T(8,128)(2,1)} copy(bf16[6,2,4,3,128,128]{4,0,2,5,3,1:T(8,128)(2,1)} %bitcast.236) | data formatting | bytes 9437184 | tf_op jit(solution)/shard_map/transpose | solution.py:336
  405.3 11.6 %reshape.397 = bf16[4,192,12,2,128]{4,3,2,1,0:T(2,128)(2,1)} reshape(bf16[768,3072]{1,0:T(8,128)(2,1)} %convolution_convert_fusion.1) | data formatting | bytes 9437184 | tf_op jit(solution)/shard_map/reshape | solution.py:325
  416.9 5.7 copy.140
  422.6 3.5 reshape.398
  433.0 7.2 %add_convert_fusion.1 = bf16[512,768]{1,0:T(8,128)(2,1)} fusion(f32[512,768]{1,0:T(8,128)} %copy-done.19, bf16[512,3072]{1,0:T(8,128)(2,1)} %copy-done.29, bf16[3072,768]{1,0:T(8,128)(2,1)} %param.31, f32[768]{0:T(1024)S(1)} %copy-done.69), kind=kOutput, calls=%fused_computation.101 | convolution fusion | flops 2417098752 | bytes 10226688 | tf_op jit(solution)/shard_map/dot_general | solution.py:639
  444.8 5.9 fusion.77
  450.7 3.9 convolution_convert_fusion
  460.0 2.9 fusion.48
  463.5 7.7 %reshape.399 = bf16[4,192,9,2,128]{4,3,2,1,0:T(2,128)(2,1)} reshape(bf16[768,2304]{1,0:T(8,128)(2,1)} %convolution_convert_fusion) | data formatting | bytes 7077888 | tf_op jit(solution)/shard_map/reshape | solution.py:325
  471.2 3.0 copy.142
  474.2 7.1 %pad_maximum_fusion = bf16[36,2,2,384,128]{4,3,2,1,0:T(8,128)(2,1)S(1)} fusion(bf16[9,2,2,384,128]{4,3,2,1,0:T(8,128)(2,1)S(1)} %bitcast.241, bf16[3,2,2,384,128]{4,3,2,1,0:T(8,128)(2,1)S(1)} %bitcast.255, bf16[12,2,2,384,128]{4,3,2,1,0:T(8,128)(2,1)} %bitcast.239, bf16[12,2,2,384,128]{4,3,2,1,0:T(8,128)(2,1)} %bitcast.240), kind=kLoop, calls=%fused_computation.29 | loop fusion | flops 21233664 | bytes 28311552 | tf_op jit(solution)/shard_map/concatenate | solution.py:345
  481.3 5.3 dynamic-slice_bitcast_fusion
  486.6 120.4 %shard_map.254 = f32[36,384,128]{2,1,0:T(8,128)} custom-call(bf16[36,2,384,128]{3,2,1,0:T(8,128)(2,1)} %get-tuple-element.719.own_ref, bf16[36,2,384,128]{3,2,1,0:T(8,128)(2,1)} %get-tuple-element.718.nbr_ref), custom_call_target="tpu_custom_call" | custom-call | tf_op jit(solution)/shard_map/pallas_call | solution.py:297
  607.0 5.2 fusion.84
  616.0 2.8 slice.33
  618.8 10.9 %all-reduce.8 = (bf16[768]{0:T(1024)(128)(2,1)}, bf16[768]{0:T(1024)(128)(2,1)}, bf16[768]{0:T(1024)(128)(2,1)}, bf16[768]{0:T(1024)(128)(2,1)}, bf16[768]{0:T(1...) all-reduce(bf16[768]{0:T(1024)(128)(2,1)S(1)} %copy-done.65, ...), channel_id=3, replica_groups=mesh['clip'=8,'frame'=4] {'frame'}, use_global_device_ids=true, to_apply=%region_18.19.clone | all-reduce | flops 7680 | bytes 30720
  641.8 4.9 copy.145
  646.7 4.1 reshape.405
  650.9 4.1 copy.143
  654.9 3.5 reshape.401
  658.5 3.4 copy.146
  661.9 3.9 copy.186
  665.7 3.0 copy.149
  670.4 19.4 %all-reduce.7 = (bf16[192]{0:T(256)(128)(2,1)}, bf16[192]{0:T(256)(128)(2,1)}, bf16[2,192]{1,0:T(2,128)(2,1)S(1)}, bf16[192]{0:T(256)(128)(2,1)}, bf16[192]{0:T(...) all-reduce(bf16[192]{0:T(256)(128)(2,1)} %dynamic-slice.2, ...), channel_id=1, replica_groups=mesh['clip'=8,'frame'=4] {'clip'}, use_global_device_ids=true, to_apply=%region_19.20 | all-reduce | flops 2304 | bytes 9216 | tf_op jit(solution)/shard_map/psum | solution.py:743
  (411 shorter events, 213.1 us)
Async XLA Ops:
  7.2 28.4 %copy-start = (bf16[768,2304]{1,0:T(8,128)(2,1)S(1)}, bf16[768,2304]{1,0:T(8,128)(2,1)}, u32[]{:S(2)}) copy-start(bf16[768,2304]{1,0:T(8,128)(2,1)} %param.23) | copy-start | bytes 10616836
  7.2 662.3 %reduce-scatter.4.cloned.1.call-start = ((), (), s32[]{:S(2)}) async-start(), calls=%async_computation.1 | async-start | bytes 245760
  10.7 26.9 %copy-start.48 = (f32[1,2,2,128]{3,1,2,0:T(2,128)}, f32[1,2,2,128]{3,1,2,0:T(2,128)S(1)}, u32[]{:S(2)}) copy-start(f32[1,2,2,128]{3,1,2,0:T(2,128)S(1)} %copy.158) | copy-start | bytes 6148
  12.2 5.8 copy-start.56
  12.3 25.4 %copy-start.50 = (f32[512]{0:T(512)}, f32[512]{0:T(512)S(1)}, u32[]{:S(2)}) copy-start(f32[512]{0:T(512)S(1)} %rsqrt.22) | copy-start | bytes 6148
  12.9 24.7 %copy-start.42 = (f32[768]{0:T(1024)}, f32[768]{0:T(1024)S(1)}, u32[]{:S(2)}) copy-start(f32[768]{0:T(1024)S(1)} %convert_element_type.247) | copy-start | bytes 9220
  56.7 8.9 %copy-start.64 = (s32[2,256]{1,0:T(2,128)S(1)}, s32[2,256]{1,0:T(2,128)}, u32[]{:S(2)}) copy-start(s32[2,256]{1,0:T(2,128)} %lt.186) | copy-start | bytes 6148
  56.7 8.9 %copy-start.70 = (s32[256]{0:T(256)S(1)}, s32[256]{0:T(256)}, u32[]{:S(2)}) copy-start(s32[256]{0:T(256)} %lt.182) | copy-start | bytes 3076
  73.5 11.8 %collective-permute-start = (bf16[2,256,768]{1,2,0:T(8,128)(2,1)}, bf16[2,256,768]{1,2,0:T(8,128)(2,1)}, u32[]{:S(2)}, u32[]{:S(2)}) collective-permute-start(bf16[2,256,768]{1,2,0:T(8,128)(2,1)} %get-tuple-element.889), channel_id=1, source_target_pairs={{3,0},{0,1},{1,2},{2,3},{7,4},{4,5},{5,6},{6,7},{11,8},{8,9},{9,10... | collective-permute-start | bytes 2359304 | tf_op jit(solution)/shard_map/while/body/eval_jaxpr/ppermute | solution.py:24
  73.9 19.9 %collective-permute-start.1 = (bf16[2,256,768]{1,2,0:T(8,128)(2,1)}, bf16[2,256,768]{1,2,0:T(8,128)(2,1)}, u32[]{:S(2)}, u32[]{:S(2)}) collective-permute-start(bf16[2,256,768]{1,2,0:T(8,128)(2,1)} %get-tuple-element.890), channel_id=1, source_target_pairs={{3,0},{0,1},{1,2},{2,3},{7,4},{4,5},{5,6},{6,7},{11,8},{8,9},{9,10... | collective-permute-start | bytes 2359304 | tf_op jit(solution)/shard_map/while/body/eval_jaxpr/ppermute | solution.py:24
  88.0 5.8 copy-start.7
  89.2 7.2 %copy-start.31 = (f32[2,12,256,1]{2,1,0,3:T(8,128)}, f32[2,12,256,1]{2,1,0,3:T(8,128)S(1)}, u32[]{:S(2)}) copy-start(f32[2,12,256,1]{2,1,0,3:T(8,128)S(1)} %bitcast_add_fusion.10) | copy-start | bytes 73732 | tf_op jit(solution)/shard_map/while
  101.3 11.7 %collective-permute-start = (bf16[2,256,768]{1,2,0:T(8,128)(2,1)}, bf16[2,256,768]{1,2,0:T(8,128)(2,1)}, u32[]{:S(2)}, u32[]{:S(2)}) collective-permute-start(bf16[2,256,768]{1,2,0:T(8,128)(2,1)} %get-tuple-element.889), channel_id=1, source_target_pairs={{3,0},{0,1},{1,2},{2,3},{7,4},{4,5},{5,6},{6,7},{11,8},{8,9},{9,10... | collective-permute-start | bytes 2359304 | tf_op jit(solution)/shard_map/while/body/eval_jaxpr/ppermute | solution.py:24
  101.3 20.2 %collective-permute-start.1 = (bf16[2,256,768]{1,2,0:T(8,128)(2,1)}, bf16[2,256,768]{1,2,0:T(8,128)(2,1)}, u32[]{:S(2)}, u32[]{:S(2)}) collective-permute-start(bf16[2,256,768]{1,2,0:T(8,128)(2,1)} %get-tuple-element.890), channel_id=1, source_target_pairs={{3,0},{0,1},{1,2},{2,3},{7,4},{4,5},{5,6},{6,7},{11,8},{8,9},{9,10... | collective-permute-start | bytes 2359304 | tf_op jit(solution)/shard_map/while/body/eval_jaxpr/ppermute | solution.py:24
  115.7 5.8 copy-start.7
  116.9 7.2 %copy-start.31 = (f32[2,12,256,1]{2,1,0,3:T(8,128)}, f32[2,12,256,1]{2,1,0,3:T(8,128)S(1)}, u32[]{:S(2)}) copy-start(f32[2,12,256,1]{2,1,0,3:T(8,128)S(1)} %bitcast_add_fusion.10) | copy-start | bytes 73732 | tf_op jit(solution)/shard_map/while
  128.9 11.7 %collective-permute-start = (bf16[2,256,768]{1,2,0:T(8,128)(2,1)}, bf16[2,256,768]{1,2,0:T(8,128)(2,1)}, u32[]{:S(2)}, u32[]{:S(2)}) collective-permute-start(bf16[2,256,768]{1,2,0:T(8,128)(2,1)} %get-tuple-element.889), channel_id=1, source_target_pairs={{3,0},{0,1},{1,2},{2,3},{7,4},{4,5},{5,6},{6,7},{11,8},{8,9},{9,10... | collective-permute-start | bytes 2359304 | tf_op jit(solution)/shard_map/while/body/eval_jaxpr/ppermute | solution.py:24
  128.9 20.2 %collective-permute-start.1 = (bf16[2,256,768]{1,2,0:T(8,128)(2,1)}, bf16[2,256,768]{1,2,0:T(8,128)(2,1)}, u32[]{:S(2)}, u32[]{:S(2)}) collective-permute-start(bf16[2,256,768]{1,2,0:T(8,128)(2,1)} %get-tuple-element.890), channel_id=1, source_target_pairs={{3,0},{0,1},{1,2},{2,3},{7,4},{4,5},{5,6},{6,7},{11,8},{8,9},{9,10... | collective-permute-start | bytes 2359304 | tf_op jit(solution)/shard_map/while/body/eval_jaxpr/ppermute | solution.py:24
  143.3 5.8 copy-start.7
  144.6 7.2 %copy-start.31 = (f32[2,12,256,1]{2,1,0,3:T(8,128)}, f32[2,12,256,1]{2,1,0,3:T(8,128)S(1)}, u32[]{:S(2)}) copy-start(f32[2,12,256,1]{2,1,0,3:T(8,128)S(1)} %bitcast_add_fusion.10) | copy-start | bytes 73732 | tf_op jit(solution)/shard_map/while
  156.6 6.7 copy-start.9
  156.6 6.7 copy-start.68
  156.6 6.7 copy-start.73
  163.3 6.9 slice-start.2
  164.3 29.0 %copy-start.19 = (f32[512,768]{1,0:T(8,128)}, f32[512,768]{1,0:T(8,128)S(1)}, u32[]{:S(2)}) copy-start(f32[512,768]{1,0:T(8,128)S(1)} %get-tuple-element.732) | copy-start | bytes 4718596
  164.3 29.0 %copy-start.54 = (f32[512]{0:T(512)}, f32[512]{0:T(512)S(1)}, u32[]{:S(2)}) copy-start(f32[512]{0:T(512)S(1)} %broadcast_multiply_fusion) | copy-start | bytes 6148
  164.7 28.7 %copy-start.62 = (f32[512]{0:T(512)}, f32[512]{0:T(512)S(1)}, u32[]{:S(2)}) copy-start(f32[512]{0:T(512)S(1)} %fusion.63) | copy-start | bytes 6148
  164.7 25.1 %slice-start = ((s8[4718592]{0:T(1024)(128)(4,1)}), s8[4194304]{0:T(1024)(128)(4,1)S(1)}, s32[]{:S(2)}) async-start(s8[4718592]{0:T(1024)(128)(4,1)} %bitcast.280), calls=%async_computation.2 | async-start | bytes 8388608
  170.2 19.5 %copy-start.20 = (f32[512,3072]{1,0:T(8,128)}, f32[512,3072]{1,0:T(8,128)S(1)}, u32[]{:S(2)}) copy-start(f32[512,3072]{1,0:T(8,128)S(1)} %fusion.76) | copy-start | bytes 18874372
  170.3 19.5 %slice-start.1 = ((s8[4718592]{0:T(1024)(128)(4,1)}), s8[524288]{0:T(1024)(128)(4,1)S(1)}, s32[]{:S(2)}) async-start(s8[4718592]{0:T(1024)(128)(4,1)} %bitcast.280), calls=%async_computation.3 | async-start | bytes 1048576
  201.0 7.6 %copy-start.45 = (pred[2,256]{1,0:T(4,128)(4,1)S(1)}, pred[2,256]{1,0:T(4,128)(4,1)}, u32[]{:S(2)}) copy-start(pred[2,256]{1,0:T(4,128)(4,1)} %copy-done.44) | copy-start | bytes 1540
  222.5 11.8 %collective-permute-start.2 = (bf16[2,256,768]{1,2,0:T(8,128)(2,1)}, bf16[2,256,768]{1,2,0:T(8,128)(2,1)}, u32[]{:S(2)}, u32[]{:S(2)}) collective-permute-start(bf16[2,256,768]{1,2,0:T(8,128)(2,1)} %get-tuple-element.934), channel_id=1, source_target_pairs={{3,0},{0,1},{1,2},{2,3},{7,4},{4,5},{5,6},{6,7},{11,8},{8,9},{9,10... | collective-permute-start | bytes 2359304 | tf_op jit(solution)/shard_map/while/body/eval_jaxpr/ppermute | solution.py:24
  222.5 20.1 %collective-permute-start.3 = (bf16[2,256,768]{1,2,0:T(8,128)(2,1)}, bf16[2,256,768]{1,2,0:T(8,128)(2,1)}, u32[]{:S(2)}, u32[]{:S(2)}) collective-permute-start(bf16[2,256,768]{1,2,0:T(8,128)(2,1)} %get-tuple-element.935), channel_id=1, source_target_pairs={{3,0},{0,1},{1,2},{2,3},{7,4},{4,5},{5,6},{6,7},{11,8},{8,9},{9,10... | collective-permute-start | bytes 2359304 | tf_op jit(solution)/shard_map/while/body/eval_jaxpr/ppermute | solution.py:24
  223.4 27.7 %collective-permute-start.5 = (bf16[2,256,768]{1,2,0:T(8,128)(2,1)}, bf16[2,256,768]{1,2,0:T(8,128)(2,1)}, u32[]{:S(2)}, u32[]{:S(2)}) collective-permute-start(bf16[2,256,768]{1,2,0:T(8,128)(2,1)} %get-tuple-element.933), channel_id=1, source_target_pairs={{3,0},{0,1},{1,2},{2,3},{7,4},{4,5},{5,6},{6,7},{11,8},{8,9},{9,10... | collective-permute-start | bytes 2359304 | tf_op jit(solution)/shard_map/while/body/eval_jaxpr/ppermute | solution.py:24
  223.5 37.8 %collective-permute-start.4 = (bf16[2,256,768]{1,2,0:T(8,128)(2,1)}, bf16[2,256,768]{1,2,0:T(8,128)(2,1)}, u32[]{:S(2)}, u32[]{:S(2)}) collective-permute-start(bf16[2,256,768]{1,2,0:T(8,128)(2,1)} %get-tuple-element.932), channel_id=1, source_target_pairs={{3,0},{0,1},{1,2},{2,3},{7,4},{4,5},{5,6},{6,7},{11,8},{8,9},{9,10... | collective-permute-start | bytes 2359304 | tf_op jit(solution)/shard_map/while/body/eval_jaxpr/ppermute | solution.py:24
  236.8 5.9 copy-start.32
  246.1 11.5 %copy-start.1 = (bf16[2,256,12,64]{1,3,2,0:T(8,128)(2,1)S(1)}, bf16[2,256,12,64]{1,3,2,0:T(8,128)(2,1)}, u32[]{:S(2)}) copy-start(bf16[2,256,12,64]{1,3,2,0:T(8,128)(2,1)} %get-tuple-element.955) | copy-start | bytes 2359300 | tf_op jit(solution)/shard_map/while
  264.1 11.7 %collective-permute-start.2 = (bf16[2,256,768]{1,2,0:T(8,128)(2,1)}, bf16[2,256,768]{1,2,0:T(8,128)(2,1)}, u32[]{:S(2)}, u32[]{:S(2)}) collective-permute-start(bf16[2,256,768]{1,2,0:T(8,128)(2,1)} %get-tuple-element.934), channel_id=1, source_target_pairs={{3,0},{0,1},{1,2},{2,3},{7,4},{4,5},{5,6},{6,7},{11,8},{8,9},{9,10... | collective-permute-start | bytes 2359304 | tf_op jit(solution)/shard_map/while/body/eval_jaxpr/ppermute | solution.py:24
  264.1 20.2 %collective-permute-start.3 = (bf16[2,256,768]{1,2,0:T(8,128)(2,1)}, bf16[2,256,768]{1,2,0:T(8,128)(2,1)}, u32[]{:S(2)}, u32[]{:S(2)}) collective-permute-start(bf16[2,256,768]{1,2,0:T(8,128)(2,1)} %get-tuple-element.935), channel_id=1, source_target_pairs={{3,0},{0,1},{1,2},{2,3},{7,4},{4,5},{5,6},{6,7},{11,8},{8,9},{9,10... | collective-permute-start | bytes 2359304 | tf_op jit(solution)/shard_map/while/body/eval_jaxpr/ppermute | solution.py:24
  265.0 27.7 %collective-permute-start.5 = (bf16[2,256,768]{1,2,0:T(8,128)(2,1)}, bf16[2,256,768]{1,2,0:T(8,128)(2,1)}, u32[]{:S(2)}, u32[]{:S(2)}) collective-permute-start(bf16[2,256,768]{1,2,0:T(8,128)(2,1)} %get-tuple-element.933), channel_id=1, source_target_pairs={{3,0},{0,1},{1,2},{2,3},{7,4},{4,5},{5,6},{6,7},{11,8},{8,9},{9,10... | collective-permute-start | bytes 2359304 | tf_op jit(solution)/shard_map/while/body/eval_jaxpr/ppermute | solution.py:24
  265.0 37.9 %collective-permute-start.4 = (bf16[2,256,768]{1,2,0:T(8,128)(2,1)}, bf16[2,256,768]{1,2,0:T(8,128)(2,1)}, u32[]{:S(2)}, u32[]{:S(2)}) collective-permute-start(bf16[2,256,768]{1,2,0:T(8,128)(2,1)} %get-tuple-element.932), channel_id=1, source_target_pairs={{3,0},{0,1},{1,2},{2,3},{7,4},{4,5},{5,6},{6,7},{11,8},{8,9},{9,10... | collective-permute-start | bytes 2359304 | tf_op jit(solution)/shard_map/while/body/eval_jaxpr/ppermute | solution.py:24
  278.3 5.9 copy-start.32
  287.7 11.5 %copy-start.1 = (bf16[2,256,12,64]{1,3,2,0:T(8,128)(2,1)S(1)}, bf16[2,256,12,64]{1,3,2,0:T(8,128)(2,1)}, u32[]{:S(2)}) copy-start(bf16[2,256,12,64]{1,3,2,0:T(8,128)(2,1)} %get-tuple-element.955) | copy-start | bytes 2359300 | tf_op jit(solution)/shard_map/while
  305.7 11.7 %collective-permute-start.2 = (bf16[2,256,768]{1,2,0:T(8,128)(2,1)}, bf16[2,256,768]{1,2,0:T(8,128)(2,1)}, u32[]{:S(2)}, u32[]{:S(2)}) collective-permute-start(bf16[2,256,768]{1,2,0:T(8,128)(2,1)} %get-tuple-element.934), channel_id=1, source_target_pairs={{3,0},{0,1},{1,2},{2,3},{7,4},{4,5},{5,6},{6,7},{11,8},{8,9},{9,10... | collective-permute-start | bytes 2359304 | tf_op jit(solution)/shard_map/while/body/eval_jaxpr/ppermute | solution.py:24
  305.7 20.2 %collective-permute-start.3 = (bf16[2,256,768]{1,2,0:T(8,128)(2,1)}, bf16[2,256,768]{1,2,0:T(8,128)(2,1)}, u32[]{:S(2)}, u32[]{:S(2)}) collective-permute-start(bf16[2,256,768]{1,2,0:T(8,128)(2,1)} %get-tuple-element.935), channel_id=1, source_target_pairs={{3,0},{0,1},{1,2},{2,3},{7,4},{4,5},{5,6},{6,7},{11,8},{8,9},{9,10... | collective-permute-start | bytes 2359304 | tf_op jit(solution)/shard_map/while/body/eval_jaxpr/ppermute | solution.py:24
  306.6 27.7 %collective-permute-start.5 = (bf16[2,256,768]{1,2,0:T(8,128)(2,1)}, bf16[2,256,768]{1,2,0:T(8,128)(2,1)}, u32[]{:S(2)}, u32[]{:S(2)}) collective-permute-start(bf16[2,256,768]{1,2,0:T(8,128)(2,1)} %get-tuple-element.933), channel_id=1, source_target_pairs={{3,0},{0,1},{1,2},{2,3},{7,4},{4,5},{5,6},{6,7},{11,8},{8,9},{9,10... | collective-permute-start | bytes 2359304 | tf_op jit(solution)/shard_map/while/body/eval_jaxpr/ppermute | solution.py:24
  306.6 37.9 %collective-permute-start.4 = (bf16[2,256,768]{1,2,0:T(8,128)(2,1)}, bf16[2,256,768]{1,2,0:T(8,128)(2,1)}, u32[]{:S(2)}, u32[]{:S(2)}) collective-permute-start(bf16[2,256,768]{1,2,0:T(8,128)(2,1)} %get-tuple-element.932), channel_id=1, source_target_pairs={{3,0},{0,1},{1,2},{2,3},{7,4},{4,5},{5,6},{6,7},{11,8},{8,9},{9,10... | collective-permute-start | bytes 2359304 | tf_op jit(solution)/shard_map/while/body/eval_jaxpr/ppermute | solution.py:24
  319.9 5.9 copy-start.32
  329.3 11.5 %copy-start.1 = (bf16[2,256,12,64]{1,3,2,0:T(8,128)(2,1)S(1)}, bf16[2,256,12,64]{1,3,2,0:T(8,128)(2,1)}, u32[]{:S(2)}) copy-start(bf16[2,256,12,64]{1,3,2,0:T(8,128)(2,1)} %get-tuple-element.955) | copy-start | bytes 2359300 | tf_op jit(solution)/shard_map/while
  347.3 5.6 copy-start.55
  347.3 5.6 copy-start.58
  347.3 5.6 copy-start.63
  349.7 90.5 %collective-permute-start.6 = (bf16[2,256,768]{2,1,0:T(8,128)(2,1)}, bf16[2,256,768]{2,1,0:T(8,128)(2,1)}, u32[]{:S(2)}, u32[]{:S(2)}) collective-permute-start(bf16[2,256,768]{2,1,0:T(8,128)(2,1)} %copy.134), channel_id=1, source_target_pairs={{3,0},{0,1},{1,2},{2,3},{7,4},{4,5},{5,6},{6,7},{11,8},{8,9},{9,10... | collective-permute-start | bytes 2359304 | tf_op jit(solution)/shard_map/ppermute | solution.py:24
  352.0 90.5 %collective-permute-start.7 = (bf16[2,256,768]{2,1,0:T(8,128)(2,1)}, bf16[2,256,768]{2,1,0:T(8,128)(2,1)}, u32[]{:S(2)}, u32[]{:S(2)}) collective-permute-start(bf16[2,256,768]{2,1,0:T(8,128)(2,1)} %copy.135), channel_id=1, source_target_pairs={{3,0},{0,1},{1,2},{2,3},{7,4},{4,5},{5,6},{6,7},{11,8},{8,9},{9,10... | collective-permute-start | bytes 2359304 | tf_op jit(solution)/shard_map/ppermute | solution.py:24
  352.9 7.5 %copy-start.36 = (bf16[96,8,2,256]{3,1,2,0:T(8,128)(2,1)S(1)}, bf16[96,8,2,256]{3,1,2,0:T(8,128)(2,1)}, u32[]{:S(2)}) copy-start(bf16[96,8,2,256]{3,1,2,0:T(8,128)(2,1)} %copy-done.35) | copy-start | bytes 2359300
  352.9 7.5 %copy-start.41 = (bf16[512,768]{1,0:T(8,128)(2,1)S(1)}, bf16[512,768]{1,0:T(8,128)(2,1)}, u32[]{:S(2)}) copy-start(bf16[512,768]{1,0:T(8,128)(2,1)} %copy-done.40) | copy-start | bytes 2359300
  360.4 6.2 copy-start.71
  360.4 6.8 copy-start.47
  367.2 7.9 %copy-start.16 = (bf16[2,1,256,768]{3,2,1,0:T(8,128)(2,1)S(1)}, bf16[2,1,256,768]{3,2,1,0:T(8,128)(2,1)}, u32[]{:S(2)}) copy-start(bf16[2,1,256,768]{3,2,1,0:T(8,128)(2,1)} %param.33) | copy-start | bytes 2359300
  444.8 5.9 copy-start.34
  444.8 5.9 copy-start.37
  444.8 5.9 copy-start.38
  444.8 5.9 copy-start.39
  450.7 9.3 %copy-start.51 = (f32[512]{0:T(512)S(1)}, f32[512]{0:T(512)}, u32[]{:S(2)}) copy-start(f32[512]{0:T(512)} %copy-done.50) | copy-start | bytes 6148
  (58 other events, 195.4 us)
Sparse Core Ops, SparseCore 0:
  459.4 20.6 reduce-scatter.3

commit v2 on v0

--- a/solution.py
+++ b/solution.py
@@ -1,6 +1,8 @@
 import jax
 import jax.numpy as jnp
 from jax import lax
+from jax.experimental import pallas as pl
+from jax.experimental.pallas import tpu as pltpu
 from jax.sharding import PartitionSpec as P
 
 D = 768
@@ -293,9 +295,815 @@
     )
 
 
+MESH = pl.DeviceIdType.MESH
+BF = jnp.bfloat16
+F32 = jnp.float32
+K = 36
+QR = 384
+HR = 192
+SLOT_COUNT = 8
+ROWS = 512
+PART = 256
+FF = 3072
+LOW = -1e30
+LAGS = (0, 2, 4, 5, 6, 7, 9)
+
+
+def dot_nn(a, b):
+    return lax.dot_general(a, b, (((1,), (0,)), ((), ())), preferred_element_type=F32)
+
+
+def dot_nt(a, b):
+    return lax.dot_general(a, b, (((1,), (1,)), ((), ())), preferred_element_type=F32)
+
+
+def dot_tn(a, b):
+    return lax.dot_general(a, b, (((0,), (0,)), ((), ())), preferred_element_type=F32)
+
+
+def at128(index):
+    return pl.ds(pl.multiple_of(index, 128), 128)
+
+
+def at256(index):
+    return pl.ds(pl.multiple_of(index, 256), 256)
+
+
+def loop(low, high, body):
+    def step(i, carry):
+        body(i)
+        return carry
+
+    lax.fori_loop(low, high, step, 0)
+
+
+class Place:
+    def __init__(self):
+        self.clip = lax.axis_index("clip")
+        self.frame = lax.axis_index("frame")
+        self.x = lax.rem(self.clip, 2)
+        self.z = self.clip // 2
+        self.core = lax.rem(self.frame, 2)
+        self.y = self.frame // 2
+        self.outer = jnp.logical_or(self.z == 0, self.z == 3)
+        self.inner = jnp.logical_not(self.outer)
+        self.to_core = (self.clip, self.y * 2 + (1 - self.core))
+        self.to_y = (self.clip, (1 - self.y) * 2 + self.core)
+        self.to_x = (self.z * 2 + (1 - self.x), self.frame)
+        mate = self.z + 1 - 2 * lax.rem(self.z, 2)
+        self.to_mate = (mate * 2 + self.x, self.frame)
+        self.to_inner = ((3 - self.z) * 2 + self.x, self.frame)
+
+    def seat(self, quarter):
+        yy, cc = quarter // 2, quarter % 2
+        return yy + 2 * (self.core if cc == 0 else 1 - self.core)
+
+
+def enter(place):
+    barrier = pltpu.get_barrier_semaphore()
+    for peer in (place.to_core, place.to_y, place.to_x, place.to_mate):
+        pl.semaphore_signal(barrier, inc=1, device_id=peer, device_id_type=MESH)
+
+    @pl.when(place.inner)
+    def _():
+        pl.semaphore_signal(barrier, inc=1, device_id=place.to_inner, device_id_type=MESH)
+
+    pl.semaphore_wait(barrier, jnp.where(place.inner, 5, 4))
+
+
+def remote(src, dst, send, recv, peer):
+    return pltpu.make_async_remote_copy(
+        src_ref=src, dst_ref=dst, send_sem=send, recv_sem=recv, device_id=peer, device_id_type=MESH
+    )
+
+
+class Reduce:
+    def __init__(self, place, bufs, tot, send, recv, tsem):
+        self.p = place
+        self.own, self.nbr, self.rc, self.ry, self.rx, self.r1, self.r2 = bufs
+        self.tot, self.send, self.recv, self.tsem = tot, send, recv, tsem
+
+    def copy(self, src, dst, stage, k, peer):
+        return remote(src, dst, self.send.at[stage, k], self.recv.at[stage, k], peer)
+
+    def my_half(self):
+        return pl.ds(pl.multiple_of(self.p.x * HR, HR), HR)
+
+    def half(self, k):
+        return self.own.at[k, self.p.y, self.my_half()]
+
+    def c_core(self, k):
+        return self.copy(self.nbr.at[lax.rem(k, SLOT_COUNT)], self.rc.at[k], 0, k, self.p.to_core)
+
+    def c_y(self, k):
+        return self.copy(self.own.at[k, 1 - self.p.y], self.ry.at[k], 1, k, self.p.to_y)
+
+    def c_x(self, k):
+        start = pl.multiple_of((1 - self.p.x) * HR, HR)
+        far = self.own.at[k, self.p.y, pl.ds(start, HR)]
+        return self.copy(far, self.rx.at[k], 2, k, self.p.to_x)
+
+    def c_in(self, k):
+        return self.copy(self.half(k), self.r1.at[k], 3, k, self.p.to_mate)
+
+    def c_mid(self, k):
+        return self.copy(self.half(k), self.r2.at[k], 4, k, self.p.to_inner)
+
+    def c_out(self, k):
+        return self.copy(self.r2.at[k], self.r1.at[k], 3, k, self.p.to_mate)
+
+    def c_gather(self, k, inner):
+        src = self.r2 if inner else self.r1
+        return self.copy(src.at[k], self.tot.at[k, self.my_half()], 5, k, self.p.to_x)
+
+    def c_keep(self, k, inner):
+        src = self.r2 if inner else self.r1
+        return pltpu.make_async_copy(src.at[k], self.tot.at[k, self.my_half()], self.tsem.at[k])
+
+    def slot(self, k):
+        @pl.when(k >= SLOT_COUNT)
+        def _():
+            self.c_core(k - SLOT_COUNT).wait_send()
+
+        return lax.rem(k, SLOT_COUNT)
+
+    def emit_wide(self, k, grad):
+        slot = self.slot(k)
+        for yy in range(2):
+            for side in range(2):
+                rows = slice(side * HR, (side + 1) * HR)
+                cols = slice(side * 128, (side + 1) * 128)
+                self.own[k, yy, rows] = grad[yy * HR : (yy + 1) * HR, cols]
+                self.nbr[slot, yy, rows] = grad[QR + yy * HR : QR + (yy + 1) * HR, cols]
+        self.c_core(k).start()
+
+    def emit_tall(self, k, grad, first):
+        slot = self.slot(k)
+        for yy in range(2):
+            for i in range(3):
+                rows = slice(i * 128, (i + 1) * 128)
+                cols = slice(first + i * 128, first + (i + 1) * 128)
+                self.own[k, yy, rows] = grad[yy * 128 : (yy + 1) * 128, cols]
+                self.nbr[slot, yy, rows] = grad[256 + yy * 128 : 256 + (yy + 1) * 128, cols]
+        self.c_core(k).start()
+
+    def stage_core(self, k):
+        self.c_core(k).wait_recv()
+        self.own[k] = self.own[k] + self.rc[k]
+        self.c_y(k).start()
+
+    def stage_y(self, k):
+        self.c_y(k).wait_recv()
+        self.own[k, self.p.y] = self.own[k, self.p.y] + self.ry[k]
+        self.c_x(k).start()
+
+    def stage_x(self, k):
+        self.c_x(k).wait_recv()
+        half = self.half(k)
+        half[...] = half[...] + self.rx[k]
+
+        @pl.when(self.p.outer)
+        def _():
+            self.c_in(k).start()
+
+    def stage_in(self, k):
+        @pl.when(self.p.inner)
+        def _():
+            self.c_in(k).wait_recv()
+            half = self.half(k)
+            half[...] = half[...] + self.r1[k]
+            self.c_mid(k).start()
+
+    def stage_mid(self, k):
+        @pl.when(self.p.inner)
+        def _():
+            self.c_mid(k).wait_recv()
+            self.r2[k] = self.r2[k] + self.half(k)[...]
+            self.c_out(k).start()
+            self.c_gather(k, True).start()
+            self.c_keep(k, True).start()
+
+    def stage_out(self, k):
+        @pl.when(self.p.outer)
+        def _():
+            self.c_in(k).wait_recv()
+            self.c_gather(k, False).start()
+            self.c_keep(k, False).start()
+
+    def stage_done(self, k):
+        self.c_gather(k, True).wait_recv()
+        self.c_y(k).wait_send()
+        self.c_x(k).wait_send()
+        self.c_in(k).wait_send()
+        self.c_gather(k, True).wait_send()
+        self.c_keep(k, True).wait()
+
+        @pl.when(k >= K - SLOT_COUNT)
+        def _():
+            self.c_core(k).wait_send()
+
+        @pl.when(self.p.inner)
+        def _():
+            self.c_mid(k).wait_send()
+
+    def tick(self, t):
+        stages = (
+            self.stage_core,
+            self.stage_y,
+            self.stage_x,
+            self.stage_in,
+            self.stage_mid,
+            self.stage_out,
+            self.stage_done,
+        )
+        for lag, stage in zip(LAGS, stages):
+            k = t - lag
+            if isinstance(k, int):
+                if 0 <= k < K:
+                    stage(k)
+            else:
+
+                @pl.when(jnp.logical_and(k >= 0, k < K))
+                def _(stage=stage, k=k):
+                    stage(k)
+
+
+def norm_parts(values):
+    mean = jnp.mean(values, axis=-1, keepdims=True)
+    centred = values - mean
+    spread = jnp.mean(centred * centred, axis=-1, keepdims=True)
+    scale = lax.rsqrt(spread + epsilon)
+    return centred * scale, scale
+
+
+def norm_back(hat, scale, gain, grad):
+    lifted = grad * gain
+    level = jnp.mean(lifted, axis=-1, keepdims=True)
+    slope = jnp.mean(lifted * hat, axis=-1, keepdims=True)
+    return scale * (lifted - level - hat * slope)
+
+
+def three_parts(values):
+    high = values.astype(BF).astype(F32)
+    rest = values - high
+    middle = rest.astype(BF).astype(F32)
+    return high, middle, rest - middle
+
+
+def layer_kernel(
+    tok_ref, cot_ref, cnt_ref, vec, wi_ref, wo_ref, we_ref, wr_ref,
+    tot_ref, vs, lo_ref, gto_ref, gtr_ref,
+    own, nbr, rc, ry, rx, r1, r2,
+    tokx, dyx, w1, wo, wr, qkv, kvr, rowb, kaug, qaug, att, mid, low2, turned, g_t, du_t, y_sum, h_sum,
+    d_out, dp, dkv_own, dkv_send, dkv_recv, lo, gts, vr,
+    send, recv, tsem, lsem, xsend, xrecv, ksend, krecv, vsend, vrecv,
+):
+    p = Place()
+    loads = [
+        pltpu.make_async_copy(tok_ref.at[p.y, 0], tokx.at[pl.ds(0, PART)], lsem.at[0]),
+        pltpu.make_async_copy(wi_ref, w1.at[:, pl.ds(0, 2304)], lsem.at[1]),
+        pltpu.make_async_copy(cot_ref.at[p.y, 0], dyx.at[pl.ds(0, PART)], lsem.at[2]),
+        pltpu.make_async_copy(wo_ref, wo, lsem.at[3]),
+        pltpu.make_async_copy(wr_ref, wr, lsem.at[4]),
+    ]
+    for one in loads:
+        one.start()
+    enter(p)
+    red = Reduce(p, (own, nbr, rc, ry, rx, r1, r2), tot_ref, send, recv, tsem)
+
+    def swap(index, src, dst, peer):
+        return remote(src, dst, xsend.at[index], xrecv.at[index], peer)
+
+    c_tok = swap(0, tok_ref.at[1 - p.y, 0], tokx.at[pl.ds(PART, PART)], p.to_y)
+    c_cot = swap(1, cot_ref.at[1 - p.y, 0], dyx.at[pl.ds(PART, PART)], p.to_y)
+    c_row = swap(2, rowb.at[2], rowb.at[1], p.to_y)
+    c_aug = swap(3, kaug.at[pl.ds(0, ROWS)], kaug.at[pl.ds(ROWS, ROWS)], p.to_core)
+    c_kv = [
+        swap(4 + r, qkv.at[pl.ds(r * PART, PART), pl.ds(768, 1536)], kvr.at[pl.ds(r * PART, PART)], p.to_core)
+        for r in range(2)
+    ]
+    c_tok.start()
+
+    lane = lax.broadcasted_iota(jnp.int32, (16, PART), 1)
+
+    def bias_row(m):
+        frame = lane // SLOTS
+        kept = jnp.zeros_like(lane)
+        for j in range(FRAME_DEV):
+            kept = jnp.where(frame == j, cnt_ref[m, 0, j], kept)
+        return jnp.where(lane - frame * SLOTS < kept, 0.0, LOW).astype(BF)
+
+    rowb[0] = bias_row(p.y)
+    rowb[2] = bias_row(1 - p.y)
+    c_row.start()
+    pick = jnp.where(
+        jnp.logical_and(
+            lax.broadcasted_iota(jnp.int32, (16, 128), 0) == 0,
+            lax.broadcasted_iota(jnp.int32, (16, 128), 1) == 0,
+        ),
+        1.0,
+        0.0,
+    ).astype(BF)
+    kaug[pl.ds(0, PART)] = dot_tn(rowb[0], pick).astype(BF)
+    lane_q = lax.broadcasted_iota(jnp.int32, (PART, 128), 1)
+    lane_row = lax.broadcasted_iota(jnp.int32, (1, 128), 1)
+    head_mask = [
+        jnp.where((lane_row < 64) == (h == 0), 1.0, 0.0).astype(BF) for h in range(2)
+    ]
+    qaug[...] = jnp.where(lax.broadcasted_iota(jnp.int32, (ROWS, 128), 1) == 0, 1.0, 0.0)
+    vs[...] = jnp.zeros_like(vs)
+
+    def project(r):
+        rows = pl.ds(r * PART, PART)
+        hat, _ = norm_parts(tokx[rows].astype(F32))
+        low2[rows] = (hat * vec[0:1] + vec[1:2]).astype(BF)
+
+        def column(j):
+            col = pl.multiple_of(j * 256, 256)
+            part = lax.rem(j, 3) * 256
+            shift = jnp.where(
+                j < 3, vec[2:3, at256(part)], jnp.where(j >= 6, vec[3:4, at256(part)], 0.0)
+            )
+            value = dot_nn(low2[rows], w1[:, pl.ds(col, 256)]) + shift
+            qkv[rows, pl.ds(col, 256)] = (value * jnp.where(j < 3, 0.125, 1.0)).astype(BF)
+
+        loop(3, 9, column)
+        c_kv[r].start()
+        loop(0, 3, column)
+
+    loads[0].wait()
+    loads[1].wait()
+    project(0)
+    c_tok.wait_recv()
+    c_row.wait_recv()
+    c_cot.start()
+    kaug[pl.ds(PART, PART)] = dot_tn(rowb[1], pick).astype(BF)
+    c_aug.start()
+    project(1)
+    load_we = pltpu.make_async_copy(we_ref, w1, lsem.at[5])
+    load_we.start()
+    c_kv[0].wait_recv()
+    c_kv[1].wait_recv()
+    c_aug.wait_recv()
+
+    def attend(pair):
+        col = pl.multiple_of(pair * 128, 128)
+        ones = jnp.ones((ROWS, 128), BF)
+        first = jnp.where(lane_q == 0, 1.0, 0.0).astype(BF)
+        k_here = jnp.concatenate([qkv[:, at128(768 + col)], kaug[pl.ds(0, ROWS)]], axis=1)
+        k_there = jnp.concatenate([kvr[:, at128(col)], kaug[pl.ds(ROWS, ROWS)]], axis=1)
+        v_here = jnp.concatenate([qkv[:, at128(1536 + col)], ones], axis=1)
+        v_there = jnp.concatenate([kvr[:, at128(768 + col)], ones], axis=1)
+        for block in range(2):
+            rows = pl.ds(block * PART, PART)
+            query = qkv[rows, at128(col)]
+            extra = qaug[rows]
+            outs = []
+            for h in range(2):
+                lifted = jnp.concatenate([query * head_mask[h], first], axis=1)
+                s_here = dot_nt(lifted, k_here)
+                s_there = dot_nt(lifted, k_there)
+                top = jnp.maximum(
+                    jnp.max(s_here, axis=-1, keepdims=True), jnp.max(s_there, axis=-1, keepdims=True)
+                )
+                e_here = jnp.exp(s_here - top).astype(BF)
+                e_there = jnp.exp(s_there - top).astype(BF)
+                both = dot_nn(e_here, v_here) + dot_nn(e_there, v_there)
+                total = both[:, 128:]
+                outs.append(both[:, :128] / total)
+                parts = three_parts(top + jnp.log(total))
+                base = 1 + 3 * (2 * pair + h)
+                for i in range(3):
+                    extra = jnp.where(lane_q == base + i, -parts[i], extra)
+            qaug[rows] = extra
+            att[rows, at128(col)] = jnp.where(lane_q < 64, outs[0], outs[1]).astype(BF)
+
+    loop(0, 6, attend)
+
+    def turn(rows, block):
+        flipped = block.T
+        for quarter in range(4):
+            seat = pl.multiple_of(p.seat(quarter) * HR, HR)
+            turned[pl.ds(seat, HR), rows] = flipped[quarter * HR : (quarter + 1) * HR]
+
+    loads[3].wait()
+
+    def middle(i):
+        rows = at256(i * PART)
+        value = tokx[rows].astype(F32) + dot_nn(att[rows], wo[...]) + vec[4:5]
+        mid[rows] = value
+        hat, _ = norm_parts(value)
+        block = (hat * vec[5:6] + vec[6:7]).astype(BF)
+        low2[rows] = block
+        turn(rows, block)
+
+    loop(0, 2, middle)
+    loads[2].wait()
+    loads[4].wait()
+    load_we.wait()
+    c_cot.wait_recv()
+    y_sum[...] = jnp.zeros_like(y_sum)
+    h_sum[...] = jnp.zeros_like(h_sum)
+
+    def feed(t):
+        starts = []
+        for side in range(2):
+            cc = p.core if side == 0 else 1 - p.core
+            for yy in range(2):
+                starts.append((yy * 2 + cc) * 768 + t * 128)
+        w_up = jnp.concatenate([w1[:, at128(s)] for s in starts], axis=1)
+        shifts = vec[8:12, at128(t * 128)]
+        zeroth = p.core == 0
+        shift = jnp.concatenate(
+            [
+                jnp.where(zeroth, shifts[yy * 2 + s : yy * 2 + s + 1], shifts[yy * 2 + 1 - s : yy * 2 + 2 - s])
+                for s in range(2)
+                for yy in range(2)
+            ],
+            axis=1,
+        )
+        before = dot_nn(low2[...], w_up) + shift
+        half = 0.5 + 0.5 * lax.erf(before * 0.7071067811865476)
+        active = (before * half).astype(BF)
+        slope = half + before * (jnp.exp(before * before * -0.5) * 0.3989422804014327)
+        g_t[...] = active
+        w_down = jnp.concatenate([wr[at128(s), :] for s in starts], axis=0)
+        du_t[...] = (dot_nt(dyx[...], w_down) * slope).astype(BF)
+        tall = dot_nn(g_t[...].T, dyx[...]).astype(BF)
+        red.emit_tall(4 * t, tall, 0)
+        red.emit_tall(4 * t + 1, tall, QR)
+        for e in range(2):
+            seats = [e + 2 * (p.core if cc == 0 else 1 - p.core) for cc in range(2)]
+            right = jnp.concatenate([du_t[:, at128(s * 128)] for s in seats], axis=1)
+            red.emit_wide(4 * t + 2 + e, dot_nn(turned[...], right).astype(BF))
+        sums = jnp.sum(du_t[...].astype(F32), axis=0, keepdims=True)
+        seat = [sums[:, i * 128 : (i + 1) * 128] for i in range(4)]
+        vs[8:12, at128(t * 128)] = jnp.concatenate(
+            [
+                jnp.where(zeroth, seat[yy + 2 * cc], seat[yy + 2 - 2 * cc])
+                for yy in range(2)
+                for cc in range(2)
+            ],
+            axis=0,
+        )
+        red.tick(2 * t)
+        y_sum[...] += dot_nn(g_t[...], w_down)
+        h_sum[...] += dot_nt(du_t[...], w_up)
+        red.tick(2 * t + 1)
+
+    loop(0, 6, feed)
+    reload_wi = pltpu.make_async_copy(wi_ref, w1.at[:, pl.ds(0, 2304)], lsem.at[6])
+    reload_wi.start()
+
+    def second(i):
+        rows = at256(i * PART)
+        value = mid[rows]
+        lo[rows] = (value + y_sum[rows] + vec[7:8]).astype(BF)
+        hat, scale = norm_parts(value)
+        grad = h_sum[rows]
+        upstream = dyx[rows].astype(F32)
+        vs[5:6] += jnp.sum(grad * hat, axis=0, keepdims=True)
+        vs[6:7] += jnp.sum(grad, axis=0, keepdims=True)
+        vs[7:8] += jnp.sum(upstream, axis=0, keepdims=True)
+        total = upstream + norm_back(hat, scale, vec[5:6], grad)
+        mid[rows] = total
+        block = total.astype(BF)
+        low2[rows] = block
+        vs[4:5] += jnp.sum(block.astype(F32), axis=0, keepdims=True)
+        d_out[rows] = dot_nt(block, wo[...]).astype(BF)
+        turn(rows, att[rows])
+
+    loop(0, 2, second)
+    red.tick(12)
+
+    def out_grad(n):
+        red.emit_wide(24 + n, dot_nn(turned[...], low2[:, at256(n * 256)]).astype(BF))
+
+    loop(0, 3, out_grad)
+    red.tick(13)
+
+    def c_dkv(pair):
+        return remote(
+            dkv_send.at[lax.rem(pair, 2)], dkv_recv.at[pair], ksend.at[pair], krecv.at[pair], p.to_core
+        )
+
+    def settle(pair):
+        c_dkv(pair).wait_recv()
+        slot = lax.rem(pair, 2)
+        for i in range(2):
+            total = dkv_own[slot, i] + dkv_recv[pair, i].astype(F32)
+            dp[:, at128(768 * (i + 1) + pair * 128)] = total.astype(BF)
+
+    lane_k = lax.broadcasted_iota(jnp.int32, (ROWS, 128), 1)
+
+    def attend_back(pair):
+        col = pl.multiple_of(pair * 128, 128)
+        slot = lax.rem(pair, 2)
+        query = qkv[:, at128(col)]
+        extra_q = qaug[...].astype(BF)
+        grads = d_out[:, at128(col)]
+        outs = att[:, at128(col)].astype(F32)
+        three = jnp.where(lane_k < 3, 1.0, 0.0).astype(BF)
+        dq = jnp.zeros((128, ROWS), F32)
+        dk = [jnp.zeros((ROWS, 128), F32)] * 2
+        dv = [jnp.zeros((ROWS, 128), F32)] * 2
+        for h in range(2):
+            q_h = query * head_mask[h]
+            g_h = grads * head_mask[h]
+            parts = three_parts(jnp.sum(g_h.astype(F32) * outs, axis=-1, keepdims=True))
+            extra_g = jnp.zeros((ROWS, 128), F32)
+            for i in range(3):
+                extra_g = jnp.where(lane_k == i, -parts[i], extra_g)
+            q_wide = jnp.concatenate([q_h, extra_q], axis=1)
+            g_wide = jnp.concatenate([g_h, extra_g.astype(BF)], axis=1)
+            base = 1 + 3 * (2 * pair + h)
+            mark = jnp.where(
+                jnp.logical_and(lane_k >= base, lane_k < base + 3), 1.0, 0.0
+            ).astype(BF)
+            for side in range(2):
+                if side == 0:
+                    key, value = qkv[:, at128(768 + col)], qkv[:, at128(1536 + col)]
+                else:
+                    key, value = kvr[:, at128(col)], kvr[:, at128(768 + col)]
+                k_wide = jnp.concatenate([key, kaug[pl.ds(side * ROWS, ROWS)] + mark], axis=1)
+                v_wide = jnp.concatenate([value, three], axis=1)
+                weight = jnp.exp(dot_nt(k_wide, q_wide))
+                slope = (weight * dot_nt(v_wide, g_wide)).astype(BF)
+                dv[side] = dv[side] + dot_nn(weight.astype(BF), g_h)
+                dk[side] = dk[side] + dot_nn(slope, q_h)
+                dq = dq + dot_nn((key * head_mask[h]).T, slope)
+        dp[:, at128(col)] = (dq.T.astype(BF).astype(F32) * 0.125).astype(BF)
+
+        @pl.when(pair >= 1)
+        def _():
+            settle(pair - 1)
+
+        @pl.when(pair >= 2)
+        def _():
+            c_dkv(pair - 2).wait_send()
+
+        dkv_own[slot, 0] = dk[0]
+        dkv_own[slot, 1] = dv[0]
+        dkv_send[slot, 0] = dk[1].astype(BF)
+        dkv_send[slot, 1] = dv[1].astype(BF)
+        c_dkv(pair).start()
+        red.tick(14 + 2 * pair)
+        red.tick(15 + 2 * pair)
+
+    loop(0, 6, attend_back)
+    settle(5)
+    c_dkv(4).wait_send()
+    c_dkv(5).wait_send()
+
+    def turn_first(i):
+        rows = at256(i * PART)
+        hat, _ = norm_parts(tokx[rows].astype(F32))
+        turn(rows, (hat * vec[0:1] + vec[1:2]).astype(BF))
+
+    loop(0, 2, turn_first)
+
+    def in_grad(n):
+        red.emit_wide(27 + n, dot_nn(turned[...], dp[:, at256(n * 256)]).astype(BF))
+        red.tick(26 + n)
+
+    loop(0, 9, in_grad)
+    vs[2:3] = jnp.sum(dp[:, 0:768].astype(F32), axis=0, keepdims=True)
+    vs[3:4] = jnp.sum(dp[:, 1536:2304].astype(F32), axis=0, keepdims=True)
+    reload_wi.wait()
+    c_lo = swap(6, lo.at[pl.ds(PART, PART)], lo_ref.at[p.y], p.to_y)
+    keep_lo = pltpu.make_async_copy(lo.at[pl.ds(0, PART)], lo_ref.at[p.y], lsem.at[7])
+    c_lo.start()
+    keep_lo.start()
+
+    def first_back(i):
+        rows = at256(i * PART)
+        grad = dot_nt(dp[rows], w1[:, pl.ds(0, 2304)])
+        hat, scale = norm_parts(tokx[rows].astype(F32))
+        vs[0:1] += jnp.sum(grad * hat, axis=0, keepdims=True)
+        vs[1:2] += jnp.sum(grad, axis=0, keepdims=True)
+        y_sum[rows] = mid[rows] + norm_back(hat, scale, vec[0:1], grad)
+
+    loop(0, 2, first_back)
+    gts[...] = y_sum[pl.ds(PART, PART)].astype(BF)
+    c_gt = swap(7, gts, gtr_ref, p.to_y)
+    keep_gt = pltpu.make_async_copy(y_sum.at[pl.ds(0, PART)], gto_ref, lsem.at[8])
+    c_gt.start()
+    keep_gt.start()
+
+    def c_vec(stage, peer):
+        return remote(vr.at[2 * stage], vr.at[2 * stage + 1], vsend.at[stage], vrecv.at[stage], peer)
+
+    def vec_pair(stage, peer):
+        vr[2 * stage] = vs[...]
+        c_vec(stage, peer).start()
+
+    def vec_take(stage, peer):
+        c_vec(stage, peer).wait()
+        vs[...] += vr[2 * stage + 1]
+
+    vec_pair(0, p.to_core)
+    red.tick(35)
+    vec_take(0, p.to_core)
+    vec_pair(1, p.to_y)
+    red.tick(36)
+    vec_take(1, p.to_y)
+    vec_pair(2, p.to_x)
+    red.tick(37)
+    vec_take(2, p.to_x)
+
+    @pl.when(p.outer)
+    def _():
+        vec_pair(3, p.to_mate)
+
+    red.tick(38)
+
+    @pl.when(p.inner)
+    def _():
+        c_vec(3, p.to_mate).wait_recv()
+        vs[...] += vr[7]
+        vec_pair(4, p.to_inner)
+
+    red.tick(39)
+
+    @pl.when(p.inner)
+    def _():
+        vec_take(4, p.to_inner)
+        vec_pair(3, p.to_mate)
+
+    red.tick(40)
+
+    @pl.when(p.outer)
+    def _():
+        c_vec(3, p.to_mate).wait_recv()
+        vs[...] = vr[7]
+
+    c_vec(3, p.to_mate).wait_send()
+
+    def drain(t):
+        red.tick(t)
+
+    loop(41, K + LAGS[-1], drain)
+    c_tok.wait_send()
+    c_row.wait_send()
+    c_cot.wait_send()
+    c_aug.wait_send()
+    c_kv[0].wait_send()
+    c_kv[1].wait_send()
+    c_lo.wait()
+    c_gt.wait()
+    keep_lo.wait()
+    keep_gt.wait()
+
+
+def finish_kernel(tot, vs, lo_in, gto, gtr, lo_out, gt, g0, g1, wi, g2, wo, g4, g5, g6, we, g8, wr, g7):
+    y = lax.axis_index("frame") // 2
+    frame = lax.axis_index("frame")
+    lo_out[...] = lo_in[...].reshape(2, 1, PART, D)
+    gt[y, 0] = gto[...]
+    gt[1 - y, 0] = gtr[...].astype(F32)
+    for t in range(6):
+        for hh in range(2):
+            for i in range(3):
+                col = (3 * hh + i) * 128
+                wr[t * 128 : (t + 1) * 128, col : col + 128] = tot[4 * t + hh, i * 128 : (i + 1) * 128].astype(F32)
+        for j in range(4):
+            col = j * 768 + t * 128
+            side = j % 2
+            we[:, col : col + 128] = tot[4 * t + 2 + j // 2, side * HR : (side + 1) * HR].astype(F32)
+    for out, base, count in ((wo, 24, 3), (wi, 27, 9)):
+        for n in range(count):
+            for side in range(2):
+                col = n * 256 + side * 128
+                out[:, col : col + 128] = tot[base + n, side * HR : (side + 1) * HR].astype(F32)
+    own = [jnp.zeros((16, HR), F32)]
+    for f in range(4):
+        own.append(jnp.where(frame == f, vs[:, f * HR : (f + 1) * HR], own[-1]))
+    mine = own[-1]
+    g0[...] = mine[0]
+    g1[...] = mine[1]
+    g2[...] = mine[2:4]
+    g4[...] = mine[4]
+    g5[...] = mine[5]
+    g6[...] = mine[6]
+    g7[...] = mine[7]
+    row = vs[8:9]
+    for f in range(1, 4):
+        row = jnp.where(frame == f, vs[8 + f : 9 + f], row)
+    g8[...] = row[0]
+
+
+def local_slice(
+    tokens,
+    counts,
+    first_gain,
+    first_bias,
+    input_weight,
+    input_bias,
+    output_weight,
+    output_bias,
+    second_gain,
+    second_bias,
+    expand_weight,
+    expand_bias,
+    reduce_weight,
+    reduce_bias,
+    cotangent,
+):
+    rows = [first_gain, first_bias, input_bias[0], input_bias[1], output_bias, second_gain, second_bias, reduce_bias]
+    vec = jnp.concatenate([jnp.stack(rows), expand_bias.reshape(4, D), jnp.zeros((4, D), BF)]).astype(F32)
+    anywhere = pl.BlockSpec(memory_space=pl.ANY)
+    vmem = pl.BlockSpec(memory_space=pltpu.VMEM)
+    smem = pl.BlockSpec(memory_space=pltpu.SMEM)
+    shape = jax.ShapeDtypeStruct
+    dma = pltpu.SemaphoreType.DMA
+    tot, vs, lo, gto, gtr = pl.pallas_call(
+        layer_kernel,
+        out_shape=(
+            shape((K, QR, 128), BF),
+            shape((16, D), F32),
+            shape((2, PART, D), BF),
+            shape((PART, D), F32),
+            shape((PART, D), BF),
+        ),
+        in_specs=[anywhere, anywhere, smem, vmem] + [anywhere] * 4,
+        out_specs=(anywhere, vmem, anywhere, anywhere, anywhere),
+        scratch_shapes=[
+            pltpu.VMEM((K, 2, QR, 128), BF),
+            pltpu.VMEM((SLOT_COUNT, 2, QR, 128), BF),
+            pltpu.VMEM((K, 2, QR, 128), BF),
+            pltpu.VMEM((K, QR, 128), BF),
+            pltpu.VMEM((K, HR, 128), BF),
+            pltpu.VMEM((K, HR, 128), BF),
+            pltpu.VMEM((K, HR, 128), BF),
+            pltpu.VMEM((ROWS, D), BF),
+            pltpu.VMEM((ROWS, D), BF),
+            pltpu.VMEM((D, FF), BF),
+            pltpu.VMEM((D, D), BF),
+            pltpu.VMEM((FF, D), BF),
+            pltpu.VMEM((ROWS, 3 * D), BF),
+            pltpu.VMEM((ROWS, 2 * D), BF),
+            pltpu.VMEM((3, 16, PART), BF),
+            pltpu.VMEM((2 * ROWS, 128), BF),
+            pltpu.VMEM((ROWS, 128), F32),
+            pltpu.VMEM((ROWS, D), BF),
+            pltpu.VMEM((ROWS, D), F32),
+            pltpu.VMEM((ROWS, D), BF),
+            pltpu.VMEM((D, ROWS), BF),
+            pltpu.VMEM((ROWS, ROWS), BF),
+            pltpu.VMEM((ROWS, ROWS), BF),
+            pltpu.VMEM((ROWS, D), F32),
+            pltpu.VMEM((ROWS, D), F32),
+            pltpu.VMEM((ROWS, D), BF),
+            pltpu.VMEM((ROWS, 3 * D), BF),
+            pltpu.VMEM((2, 2, ROWS, 128), F32),
+            pltpu.VMEM((2, 2, ROWS, 128), BF),
+            pltpu.VMEM((6, 2, ROWS, 128), BF),
+            pltpu.VMEM((ROWS, D), BF),
+            pltpu.VMEM((PART, D), BF),
+            pltpu.VMEM((10, 16, D), F32),
+            dma((6, K)),
+            dma((6, K)),
+            dma((K,)),
+            dma((9,)),
+            dma((8,)),
+            dma((8,)),
+            dma((6,)),
+            dma((6,)),
+            dma((5,)),
+            dma((5,)),
+        ],
+        compiler_params=pltpu.CompilerParams(
+            collective_id=0, has_side_effects=True, vmem_limit_bytes=62 << 20
+        ),
+    )(tokens, cotangent, counts, vec, input_weight, output_weight, expand_weight, reduce_weight)
+    return pl.pallas_call(
+        finish_kernel,
+        out_shape=(
+            shape((MICRO, 1, PART, D), BF),
+            shape((MICRO, 1, PART, D), F32),
+            shape((HR,), F32),
+            shape((HR,), F32),
+            shape((HR, 3 * D), F32),
+            shape((2, HR), F32),
+            shape((HR, D), F32),
+            shape((HR,), F32),
+            shape((HR,), F32),
+            shape((HR,), F32),
+            shape((HR, FF), F32),
+            shape((D,), F32),
+            shape((D, D), F32),
+            shape((HR,), F32),
+        ),
+        in_specs=[vmem] * 5,
+        out_specs=(vmem,) * 14,
+        compiler_params=pltpu.CompilerParams(vmem_limit_bytes=40 << 20),
+    )(tot, vs, lo, gto, gtr)
+
+
 def solution(mesh):
+    fits = mesh.shape["clip"] == 8 and mesh.shape["frame"] == 4
     return jax.shard_map(
-        local,
+        local_slice if fits else local,
         mesh=mesh,
         in_specs=(
             P(None, "clip", "frame", None),

time: 717 us -> 199 us (0.28); the launches traced: 705 us -> 198 us
  waiting for transfers between devices: 321 us -> 0 us
  Pallas kernels: 0 us -> 185 us
  matrix products: 128 us -> 0 us
  local copies, waits for them, and re-layouts: 105 us -> 11.6 us
  other arithmetic: 77.3 us -> 0.63 us
  blocking collectives: 43.7 us -> 0 us
  between operations: 16.6 us -> 0.83 us
  starting transfers between devices: 11.2 us -> 0 us
    pallas_call x0 -> x2, Pallas kernels: none -> 185 us  [the longest x1 181 us: local_slice(): pl.pallas_call(layer_kernel, out_shape=(shape((K, QR, 128), BF), shape((1...]
    dot_general x39 -> x0, matrix products: 128 us -> none  [the longest x1 19.1 us: local(): jnp.dot(upstream_low, reduce_weight.T, preferred_element_type=jnp.float32)]
    reduce_scatter x4 -> x0, waiting for transfers between devices: 118 us -> none  [the longest x1 50.4 us: local(): lax.psum_scatter(grad_reduce_weight.astype(jnp.bfloat16), 'frame', scatte...]
    ppermute x20 -> x0, waiting for transfers between devices: 110 us -> none  [from_behind(): return lax.ppermute(block, axis, route)]
    psum x1 -> x0, waiting for transfers between devices: 93.4 us -> none  [local(): lax.psum(shares[2].astype(jnp.bfloat16), 'clip').astype(jnp.float32)]
    while x86 -> x0, local copies, waits for them, and re-layouts: 41.1 us -> none
    convert_element_type x24 -> x1, other arithmetic: 36.6 us -> 0.63 us  [local_slice(): jnp.concatenate([jnp.stack(rows), expand_bias.reshape(4, D), jnp.zeros((4...]
    psum x1 -> x0, blocking collectives: 23.9 us -> none  [local(): lax.psum(shares[0].astype(jnp.bfloat16), 'clip').astype(jnp.float32)]
  transfers between devices with their start and end apart: 26 -> 0, of which waited for: 21 -> 0; matrix products, arithmetic and copies ran while one was open for 25% -> 0% of each run, Pallas kernels for 0% -> 0%
where the time goes in v2:
time: 199 us; the launch traced here: 198 us
  Pallas kernels  185 us (93%)
  local copies, waits for them, and re-layouts  11.6 us (6%)
    pallas_call x1, Pallas kernels, local_slice(): pl.pallas_call(layer_kernel, out_shape=(shape((K, QR, 128), BF), shape((1...  181 us
    unnamed x10, local copies, waits for them, and re-layouts  6.05 us
    another operation x6, local copies, waits for them, and re-layouts, local_slice(): jnp.stack(rows)  4.11 us

profile of v2, /device:TPU:0, one launch (start us, length us, event | category | flops | bytes accessed | tf_op | source)
XLA Modules:
  0.0 198.1 jit_solution(7609138767444979695)
XLA Ops:
  0.6 0.7 stack.18
  1.3 0.7 stack.19
  2.0 0.7 stack.20
  2.7 0.7 stack.21
  3.4 0.7 stack.22
  4.1 0.7 stack.23
  4.8 0.7 reshape.31
  5.5 0.7 concatenate.4
  6.2 0.6 convert_element_type.3.vec
  6.8 181.0 %shard_map.254 = (bf16[36,384,128]{2,1,0:T(8,128)(2,1)}, f32[16,768]{1,0:T(8,128)}, bf16[2,256,768]{2,1,0:T(8,128)(2,1)}, f32[256,768]{1,0:T(8,128)}, bf16[256,768]{1,0:T(8,128)(2,1)}) custom-call(bf16[2,1,256,768]{3,2,1,0:T(8,128)(2,1)} %tok_ref.1, bf16[2,1,256,768]{3,2,1,0:T(8,128)(2,1)} %cot_ref.1, s32[2,1,4]{2,1,0:T(1,128)} %cnt_ref.1, ...), custom_call_target="tpu_custom_call" | custom-call | tf_op jit(solution)/shard_map/pallas_call | solution.py:1019
  187.9 0.0 copy-start
  187.9 2.0 %copy-done = bf16[36,384,128]{2,1,0:T(8,128)(2,1)S(1)} copy-done((bf16[36,384,128]{2,1,0:T(8,128)(2,1)S(1)}, bf16[36,384,128]{2,1,0:T(8,128)(2,1)}, u32[]{:S(2)}) %copy-start) | copy-done | bytes 3538968
  189.9 0.0 copy-start.1
  189.9 1.1 copy-done.1
  191.0 0.0 copy-start.2
  191.0 1.1 copy-done.2
  192.2 0.0 copy-start.3
  192.2 1.0 copy-done.3
  193.1 0.0 copy-start.4
  193.1 0.8 copy-done.4
  193.9 4.0 %shard_map.255 = (bf16[2,1,256,768]{3,2,1,0:T(8,128)(2,1)}, f32[2,1,256,768]{3,2,1,0:T(8,128)}, f32[192]{0:T(256)}, f32[192]{0:T(256)}, f32[192,2304]{1,0:T(8,12...) custom-call(bf16[36,384,128]{2,1,0:T(8,128)(2,1)S(1)} %copy-done, ...), custom_call_target="tpu_custom_call" | custom-call | tf_op jit(solution)/shard_map/pallas_call | solution.py:1079
  (1 shorter events, 0.0 us)
Async XLA Ops:
  187.9 2.0 %copy-start = (bf16[36,384,128]{2,1,0:T(8,128)(2,1)S(1)}, bf16[36,384,128]{2,1,0:T(8,128)(2,1)}, u32[]{:S(2)}) copy-start(bf16[36,384,128]{2,1,0:T(8,128)(2,1)} %get-tuple-element.19.tot) | copy-start | bytes 10616836
  189.9 1.1 copy-start.1
  191.0 1.1 copy-start.2
  192.2 1.0 copy-start.3
  193.1 0.8 copy-start.4

commit v3 on v2

--- a/solution.py
+++ b/solution.py
@@ -306,7 +306,9 @@
 PART = 256
 FF = 3072
 LOW = -1e30
-LAGS = (0, 2, 4, 5, 6, 7, 9)
+LAGS = (0, 6, 12, 15, 18, 21, 24)
+WAYS = "acbacabca"
+TALL = ((0, 0, 0, 0, 128), (0, 128, 1, 0, 64), (1, 0, 1, 64, 128), (1, 64, 2, 0, 128))
 
 
 def dot_nn(a, b):
@@ -352,7 +354,8 @@
         self.to_x = (self.z * 2 + (1 - self.x), self.frame)
         mate = self.z + 1 - 2 * lax.rem(self.z, 2)
         self.to_mate = (mate * 2 + self.x, self.frame)
-        self.to_inner = ((3 - self.z) * 2 + self.x, self.frame)
+        self.to_far = ((3 - self.z) * 2 + self.x, self.frame)
+        self.h = jnp.where(self.inner, 1, 0)
 
     def seat(self, quarter):
         yy, cc = quarter // 2, quarter % 2
@@ -361,14 +364,9 @@
 
 def enter(place):
     barrier = pltpu.get_barrier_semaphore()
-    for peer in (place.to_core, place.to_y, place.to_x, place.to_mate):
+    for peer in (place.to_core, place.to_y, place.to_x, place.to_mate, place.to_far):
         pl.semaphore_signal(barrier, inc=1, device_id=peer, device_id_type=MESH)
-
-    @pl.when(place.inner)
-    def _():
-        pl.semaphore_signal(barrier, inc=1, device_id=place.to_inner, device_id_type=MESH)
-
-    pl.semaphore_wait(barrier, jnp.where(place.inner, 5, 4))
+    pl.semaphore_wait(barrier, 5)
 
 
 def remote(src, dst, send, recv, peer):
@@ -386,39 +384,95 @@
     def copy(self, src, dst, stage, k, peer):
         return remote(src, dst, self.send.at[stage, k], self.recv.at[stage, k], peer)
 
-    def my_half(self):
-        return pl.ds(pl.multiple_of(self.p.x * HR, HR), HR)
-
-    def half(self, k):
-        return self.own.at[k, self.p.y, self.my_half()]
+    def keep(self, src, dst, k):
+        return pltpu.make_async_copy(src, dst, self.tsem.at[k])
+
+    def part(self, far):
+        return pl.ds(pl.multiple_of((1 - self.p.x if far else self.p.x) * 96, 96), 96)
 
     def c_core(self, k):
         return self.copy(self.nbr.at[lax.rem(k, SLOT_COUNT)], self.rc.at[k], 0, k, self.p.to_core)
 
-    def c_y(self, k):
+    def a_y(self, k):
         return self.copy(self.own.at[k, 1 - self.p.y], self.ry.at[k], 1, k, self.p.to_y)
 
-    def c_x(self, k):
-        start = pl.multiple_of((1 - self.p.x) * HR, HR)
-        far = self.own.at[k, self.p.y, pl.ds(start, HR)]
-        return self.copy(far, self.rx.at[k], 2, k, self.p.to_x)
-
-    def c_in(self, k):
+    def a_x(self, k):
+        return self.copy(self.own.at[k, self.p.y, 1 - self.p.x], self.rx.at[k], 2, k, self.p.to_x)
+
+    def b_x(self, k):
+        return self.copy(self.own.at[k, :, 1 - self.p.x], self.ry.at[k], 1, k, self.p.to_x)
+
+    def b_y(self, k):
+        return self.copy(self.own.at[k, 1 - self.p.y, self.p.x], self.rx.at[k], 2, k, self.p.to_y)
+
+    def half(self, k):
+        return self.own.at[k, self.p.y, self.p.x]
+
+    def l_in(self, k):
         return self.copy(self.half(k), self.r1.at[k], 3, k, self.p.to_mate)
 
-    def c_mid(self, k):
-        return self.copy(self.half(k), self.r2.at[k], 4, k, self.p.to_inner)
-
-    def c_out(self, k):
+    def l_mid(self, k):
+        return self.copy(self.half(k), self.r2.at[k], 4, k, self.p.to_far)
+
+    def l_out(self, k):
         return self.copy(self.r2.at[k], self.r1.at[k], 3, k, self.p.to_mate)
 
-    def c_gather(self, k, inner):
+    def l_gather(self, k, inner):
         src = self.r2 if inner else self.r1
-        return self.copy(src.at[k], self.tot.at[k, self.my_half()], 5, k, self.p.to_x)
-
-    def c_keep(self, k, inner):
+        return self.copy(src.at[k], self.tot.at[k, self.p.x], 5, k, self.p.to_x)
+
+    def l_keep(self, k, inner):
         src = self.r2 if inner else self.r1
-        return pltpu.make_async_copy(src.at[k], self.tot.at[k, self.my_half()], self.tsem.at[k])
+        return self.keep(src.at[k], self.tot.at[k, self.p.x], k)
+
+    def q_pair(self, k):
+        return self.copy(self.own.at[k, :, 1 - self.p.h], self.ry.at[k], 1, k, self.p.to_mate)
+
+    def q_y(self, k):
+        return self.copy(self.own.at[k, 1 - self.p.y, self.p.h], self.rx.at[k], 2, k, self.p.to_y)
+
+    def q_x(self, k):
+        src = self.own.at[k, self.p.y, self.p.h, self.part(True)]
+        return self.copy(src, self.r1.at[k, pl.ds(0, 96)], 3, k, self.p.to_x)
+
+    def q_far(self, k):
+        src = self.own.at[k, self.p.y, self.p.h, self.part(False)]
+        return self.copy(src, self.r1.at[k, pl.ds(96, 96)], 4, k, self.p.to_far)
+
+    def q_gather(self, k):
+        both = self.r2.at[k, self.part(False)]
+        return self.copy(both, both, 5, k, self.p.to_x)
+
+    def q_spread(self, k):
+        return self.copy(self.r2.at[k], self.tot.at[k, self.p.h], 6, k, self.p.to_mate)
+
+    def q_keep(self, k):
+        return self.keep(self.r2.at[k], self.tot.at[k, self.p.h], k)
+
+    def kinds(self, k):
+        if isinstance(k, int):
+            return WAYS[k % len(WAYS)]
+        m = lax.rem(k, len(WAYS))
+        out = {}
+        for way in "abc":
+            hit = m < 0
+            for i, one in enumerate(WAYS):
+                if one == way:
+                    hit = jnp.logical_or(hit, m == i)
+            out[way] = hit
+        return out
+
+    def split(self, k, a, b, c):
+        kinds = self.kinds(k)
+        if isinstance(kinds, str):
+            {"a": a, "b": b, "c": c}[kinds](k)
+            return
+        if a is b:
+            pl.when(jnp.logical_not(kinds["c"]))(lambda: a(k))
+        else:
+            pl.when(kinds["a"])(lambda: a(k))
+            pl.when(kinds["b"])(lambda: b(k))
+        pl.when(kinds["c"])(lambda: c(k))
 
     def slot(self, k):
         @pl.when(k >= SLOT_COUNT)
@@ -431,101 +485,142 @@
         slot = self.slot(k)
         for yy in range(2):
             for side in range(2):
-                rows = slice(side * HR, (side + 1) * HR)
                 cols = slice(side * 128, (side + 1) * 128)
-                self.own[k, yy, rows] = grad[yy * HR : (yy + 1) * HR, cols]
-                self.nbr[slot, yy, rows] = grad[QR + yy * HR : QR + (yy + 1) * HR, cols]
+                self.own[k, yy, side] = grad[yy * HR : (yy + 1) * HR, cols]
+                self.nbr[slot, yy, side] = grad[QR + yy * HR : QR + (yy + 1) * HR, cols]
         self.c_core(k).start()
 
     def emit_tall(self, k, grad, first):
         slot = self.slot(k)
         for yy in range(2):
-            for i in range(3):
-                rows = slice(i * 128, (i + 1) * 128)
-                cols = slice(first + i * 128, first + (i + 1) * 128)
-                self.own[k, yy, rows] = grad[yy * 128 : (yy + 1) * 128, cols]
-                self.nbr[slot, yy, rows] = grad[256 + yy * 128 : 256 + (yy + 1) * 128, cols]
+            for side, to, block, low, high in TALL:
+                cols = slice(first + block * 128, first + (block + 1) * 128)
+                rows = slice(to, to + high - low)
+                self.own[k, yy, side, rows] = grad[yy * 128 + low : yy * 128 + high, cols]
+                self.nbr[slot, yy, side, rows] = grad[256 + yy * 128 + low : 256 + yy * 128 + high, cols]
         self.c_core(k).start()
 
-    def stage_core(self, k):
+    def stage_1(self, k):
         self.c_core(k).wait_recv()
         self.own[k] = self.own[k] + self.rc[k]
-        self.c_y(k).start()
-
-    def stage_y(self, k):
-        self.c_y(k).wait_recv()
-        self.own[k, self.p.y] = self.own[k, self.p.y] + self.ry[k]
-        self.c_x(k).start()
-
-    def stage_x(self, k):
-        self.c_x(k).wait_recv()
-        half = self.half(k)
-        half[...] = half[...] + self.rx[k]
-
-        @pl.when(self.p.outer)
-        def _():
-            self.c_in(k).start()
-
-    def stage_in(self, k):
-        @pl.when(self.p.inner)
-        def _():
-            self.c_in(k).wait_recv()
-            half = self.half(k)
-            half[...] = half[...] + self.r1[k]
-            self.c_mid(k).start()
-
-    def stage_mid(self, k):
-        @pl.when(self.p.inner)
-        def _():
-            self.c_mid(k).wait_recv()
-            self.r2[k] = self.r2[k] + self.half(k)[...]
-            self.c_out(k).start()
-            self.c_gather(k, True).start()
-            self.c_keep(k, True).start()
-
-    def stage_out(self, k):
-        @pl.when(self.p.outer)
-        def _():
-            self.c_in(k).wait_recv()
-            self.c_gather(k, False).start()
-            self.c_keep(k, False).start()
-
-    def stage_done(self, k):
-        self.c_gather(k, True).wait_recv()
-        self.c_y(k).wait_send()
-        self.c_x(k).wait_send()
-        self.c_in(k).wait_send()
-        self.c_gather(k, True).wait_send()
-        self.c_keep(k, True).wait()
+        self.split(
+            k,
+            lambda k: self.a_y(k).start(),
+            lambda k: self.b_x(k).start(),
+            lambda k: self.q_pair(k).start(),
+        )
+
+    def stage_2(self, k):
+        self.a_y(k).wait_recv()
+
+        def a(k):
+            self.own[k, self.p.y] = self.own[k, self.p.y] + self.ry[k]
+            self.a_x(k).start()
+
+        def b(k):
+            self.own[k, :, self.p.x] = self.own[k, :, self.p.x] + self.ry[k]
+            self.b_y(k).start()
+
+        def c(k):
+            self.own[k, :, self.p.h] = self.own[k, :, self.p.h] + self.ry[k]
+            self.q_y(k).start()
+
+        self.split(k, a, b, c)
+
+    def stage_3(self, k):
+        self.a_x(k).wait_recv()
+
+        def line(k):
+            self.own[k, self.p.y, self.p.x] = self.own[k, self.p.y, self.p.x] + self.rx[k]
+            pl.when(self.p.outer)(lambda: self.l_in(k).start())
+
+        def c(k):
+            self.own[k, self.p.y, self.p.h] = self.own[k, self.p.y, self.p.h] + self.rx[k]
+            self.q_x(k).start()
+
+        self.split(k, line, line, c)
+
+    def stage_4(self, k):
+        def line(k):
+            @pl.when(self.p.inner)
+            def _():
+                self.l_in(k).wait_recv()
+                self.own[k, self.p.y, self.p.x] = self.own[k, self.p.y, self.p.x] + self.r1[k]
+                self.l_mid(k).start()
+
+        def c(k):
+            self.q_x(k).wait_recv()
+            mine = self.own.at[k, self.p.y, self.p.h, self.part(False)]
+            mine[...] = mine[...] + self.r1[k, pl.ds(0, 96)]
+            self.q_far(k).start()
+
+        self.split(k, line, line, c)
+
+    def stage_5(self, k):
+        def line(k):
+            @pl.when(self.p.inner)
+            def _():
+                self.l_mid(k).wait_recv()
+                self.r2[k] = self.r2[k] + self.own[k, self.p.y, self.p.x]
+                self.l_out(k).start()
+                self.l_gather(k, True).start()
+                self.l_keep(k, True).start()
+
+        def c(k):
+            self.q_far(k).wait_recv()
+            mine = self.own.at[k, self.p.y, self.p.h, self.part(False)]
+            self.r2[k, self.part(False)] = mine[...] + self.r1[k, pl.ds(96, 96)]
+            self.q_gather(k).start()
+
+        self.split(k, line, line, c)
+
+    def stage_6(self, k):
+        def line(k):
+            @pl.when(self.p.outer)
+            def _():
+                self.l_in(k).wait_recv()
+                self.l_gather(k, False).start()
+                self.l_keep(k, False).start()
+
+        def c(k):
+            self.q_gather(k).wait_recv()
+            self.q_spread(k).start()
+            self.q_keep(k).start()
+
+        self.split(k, line, line, c)
+
+    def stage_7(self, k):
+        self.a_y(k).wait_send()
+        self.a_x(k).wait_send()
 
         @pl.when(k >= K - SLOT_COUNT)
         def _():
             self.c_core(k).wait_send()
 
-        @pl.when(self.p.inner)
-        def _():
-            self.c_mid(k).wait_send()
+        def line(k):
+            self.l_gather(k, True).wait()
+            self.l_in(k).wait_send()
+            self.l_keep(k, True).wait()
+            pl.when(self.p.inner)(lambda: self.l_mid(k).wait_send())
+
+        def c(k):
+            self.q_spread(k).wait()
+            self.q_x(k).wait_send()
+            self.q_far(k).wait_send()
+            self.q_gather(k).wait_send()
+            self.q_keep(k).wait()
+
+        self.split(k, line, line, c)
 
     def tick(self, t):
-        stages = (
-            self.stage_core,
-            self.stage_y,
-            self.stage_x,
-            self.stage_in,
-            self.stage_mid,
-            self.stage_out,
-            self.stage_done,
-        )
+        stages = (self.stage_1, self.stage_2, self.stage_3, self.stage_4, self.stage_5, self.stage_6, self.stage_7)
         for lag, stage in zip(LAGS, stages):
             k = t - lag
             if isinstance(k, int):
                 if 0 <= k < K:
                     stage(k)
             else:
-
-                @pl.when(jnp.logical_and(k >= 0, k < K))
-                def _(stage=stage, k=k):
-                    stage(k)
+                pl.when(jnp.logical_and(k >= 0, k < K))(lambda stage=stage, k=k: stage(k))
 
 
 def norm_parts(values):
@@ -551,9 +646,10 @@
 
 
 def layer_kernel(
-    tok_ref, cot_ref, cnt_ref, vec, wi_ref, wo_ref, we_ref, wr_ref,
+    tok_ref, cot_ref, cnt_ref, fg_ref, fb_ref, ib_ref, ob_ref, sg_ref, sb_ref, eb_ref, rb_ref,
+    wi_ref, wo_ref, we_ref, wr_ref,
     tot_ref, vs, lo_ref, gto_ref, gtr_ref,
-    own, nbr, rc, ry, rx, r1, r2,
+    own, nbr, rc, ry, rx, r1, r2, vec,
     tokx, dyx, w1, wo, wr, qkv, kvr, rowb, kaug, qaug, att, mid, low2, turned, g_t, du_t, y_sum, h_sum,
     d_out, dp, dkv_own, dkv_send, dkv_recv, lo, gts, vr,
     send, recv, tsem, lsem, xsend, xrecv, ksend, krecv, vsend, vrecv,
@@ -583,6 +679,12 @@
         for r in range(2)
     ]
     c_tok.start()
+
+    for row, ref in ((0, fg_ref), (1, fb_ref), (4, ob_ref), (5, sg_ref), (6, sb_ref), (7, rb_ref)):
+        vec[row : row + 1] = ref[...].astype(F32).reshape(1, D)
+    vec[2:4] = ib_ref[...].astype(F32)
+    for f in range(4):
+        vec[8 + f : 9 + f] = eb_ref[f * D : (f + 1) * D].astype(F32).reshape(1, D)
 
     lane = lax.broadcasted_iota(jnp.int32, (16, PART), 1)
 
@@ -872,7 +974,6 @@
     reload_wi.wait()
     c_lo = swap(6, lo.at[pl.ds(PART, PART)], lo_ref.at[p.y], p.to_y)
     keep_lo = pltpu.make_async_copy(lo.at[pl.ds(0, PART)], lo_ref.at[p.y], lsem.at[7])
-    c_lo.start()
     keep_lo.start()
 
     def first_back(i):
@@ -887,7 +988,6 @@
     gts[...] = y_sum[pl.ds(PART, PART)].astype(BF)
     c_gt = swap(7, gts, gtr_ref, p.to_y)
     keep_gt = pltpu.make_async_copy(y_sum.at[pl.ds(0, PART)], gto_ref, lsem.at[8])
-    c_gt.start()
     keep_gt.start()
 
     def c_vec(stage, peer):
@@ -921,13 +1021,13 @@
     def _():
         c_vec(3, p.to_mate).wait_recv()
         vs[...] += vr[7]
-        vec_pair(4, p.to_inner)
+        vec_pair(4, p.to_far)
 
     red.tick(39)
 
     @pl.when(p.inner)
     def _():
-        vec_take(4, p.to_inner)
+        vec_take(4, p.to_far)
         vec_pair(3, p.to_mate)
 
     red.tick(40)
@@ -938,6 +1038,8 @@
         vs[...] = vr[7]
 
     c_vec(3, p.to_mate).wait_send()
+    c_lo.start()
+    c_gt.start()
 
     def drain(t):
         red.tick(t)
@@ -955,30 +1057,69 @@
     keep_gt.wait()
 
 
-def finish_kernel(tot, vs, lo_in, gto, gtr, lo_out, gt, g0, g1, wi, g2, wo, g4, g5, g6, we, g8, wr, g7):
+def finish_kernel(
+    tot_ref, vs, lo_in, gto, gtr_ref,
+    lo_out, gt, g0, g1, wi_out, g2, wo_out, g4, g5, g6, we_out, g8, wr_out, g7,
+    tot, gtr, gt_s, lo_s, wi, wo, we, wr, in_sem, out_sem,
+):
     y = lax.axis_index("frame") // 2
     frame = lax.axis_index("frame")
-    lo_out[...] = lo_in[...].reshape(2, 1, PART, D)
-    gt[y, 0] = gto[...]
-    gt[1 - y, 0] = gtr[...].astype(F32)
+    spans = [(4 * t, 4) for t in range(6)] + [(24, 3)] + [(27 + 3 * i, 3) for i in range(3)]
+    loads = [
+        pltpu.make_async_copy(tot_ref.at[pl.ds(k, n)], tot.at[pl.ds(k, n)], in_sem.at[i])
+        for i, (k, n) in enumerate(spans)
+    ]
+    loads += [
+        pltpu.make_async_copy(gtr_ref, gtr, in_sem.at[10]),
+        pltpu.make_async_copy(gto, gt_s.at[0], in_sem.at[11]),
+        pltpu.make_async_copy(lo_in, lo_s, in_sem.at[12]),
+    ]
+    for one in loads:
+        one.start()
+    outs = []
+
+    def leave(src, dst):
+        one = pltpu.make_async_copy(src, dst, out_sem.at[len(outs)])
+        one.start()
+        outs.append(one)
+
     for t in range(6):
+        loads[t].wait()
         for hh in range(2):
-            for i in range(3):
-                col = (3 * hh + i) * 128
-                wr[t * 128 : (t + 1) * 128, col : col + 128] = tot[4 * t + hh, i * 128 : (i + 1) * 128].astype(F32)
+            for side, to, block, low, high in TALL:
+                col = (3 * hh + block) * 128
+                wr[t * 128 + low : t * 128 + high, col : col + 128] = tot[
+                    4 * t + hh, side, to : to + high - low
+                ].astype(F32)
+        rows = pl.ds(t * 128, 128)
+        leave(wr.at[rows], wr_out.at[rows])
         for j in range(4):
-            col = j * 768 + t * 128
-            side = j % 2
-            we[:, col : col + 128] = tot[4 * t + 2 + j // 2, side * HR : (side + 1) * HR].astype(F32)
-    for out, base, count in ((wo, 24, 3), (wi, 27, 9)):
-        for n in range(count):
+            cols = pl.ds(j * 768 + t * 128, 128)
+            we[:, cols] = tot[4 * t + 2 + j // 2, j % 2].astype(F32)
+    leave(we, we_out)
+    for i, (src, dst) in enumerate([(wo, wo_out)] + [(wi, wi_out)] * 3):
+        loads[6 + i].wait()
+        base = 24 + 3 * i
+        start = 768 * max(i - 1, 0)
+        for n in range(3):
             for side in range(2):
-                col = n * 256 + side * 128
-                out[:, col : col + 128] = tot[base + n, side * HR : (side + 1) * HR].astype(F32)
-    own = [jnp.zeros((16, HR), F32)]
-    for f in range(4):
-        own.append(jnp.where(frame == f, vs[:, f * HR : (f + 1) * HR], own[-1]))
-    mine = own[-1]
+                col = start + n * 256 + side * 128
+                src[:, col : col + 128] = tot[base + n, side].astype(F32)
+        cols = pl.ds(start, 768)
+        leave(src.at[:, cols], dst.at[:, cols])
+    loads[10].wait()
+    gt_s[1] = gtr[...].astype(F32)
+    leave(gt_s.at[1], gt.at[1 - y, 0])
+    loads[11].wait()
+    leave(gt_s.at[0], gt.at[y, 0])
+    loads[12].wait()
+    leave(lo_s.at[0], lo_out.at[0, 0])
+    leave(lo_s.at[1], lo_out.at[1, 0])
+    mine = vs[0:8, 0:HR]
+    row = vs[8:9]
+    for f in range(1, 4):
+        mine = jnp.where(frame == f, vs[0:8, f * HR : (f + 1) * HR], mine)
+        row = jnp.where(frame == f, vs[8 + f : 9 + f], row)
     g0[...] = mine[0]
     g1[...] = mine[1]
     g2[...] = mine[2:4]
@@ -986,10 +1127,9 @@
     g5[...] = mine[5]
     g6[...] = mine[6]
     g7[...] = mine[7]
-    row = vs[8:9]
-    for f in range(1, 4):
-        row = jnp.where(frame == f, vs[8 + f : 9 + f], row)
     g8[...] = row[0]
+    for one in outs:
+        one.wait()
 
 
 def local_slice(
@@ -1009,8 +1149,6 @@
     reduce_bias,
     cotangent,
 ):
-    rows = [first_gain, first_bias, input_bias[0], input_bias[1], output_bias, second_gain, second_bias, reduce_bias]
-    vec = jnp.concatenate([jnp.stack(rows), expand_bias.reshape(4, D), jnp.zeros((4, D), BF)]).astype(F32)
     anywhere = pl.BlockSpec(memory_space=pl.ANY)
     vmem = pl.BlockSpec(memory_space=pltpu.VMEM)
     smem = pl.BlockSpec(memory_space=pltpu.SMEM)
@@ -1019,22 +1157,23 @@
     tot, vs, lo, gto, gtr = pl.pallas_call(
         layer_kernel,
         out_shape=(
-            shape((K, QR, 128), BF),
+            shape((K, 2, HR, 128), BF),
             shape((16, D), F32),
             shape((2, PART, D), BF),
             shape((PART, D), F32),
             shape((PART, D), BF),
         ),
-        in_specs=[anywhere, anywhere, smem, vmem] + [anywhere] * 4,
+        in_specs=[anywhere, anywhere, smem] + [vmem] * 8 + [anywhere] * 4,
         out_specs=(anywhere, vmem, anywhere, anywhere, anywhere),
         scratch_shapes=[
-            pltpu.VMEM((K, 2, QR, 128), BF),
-            pltpu.VMEM((SLOT_COUNT, 2, QR, 128), BF),
-            pltpu.VMEM((K, 2, QR, 128), BF),
-            pltpu.VMEM((K, QR, 128), BF),
+            pltpu.VMEM((K, 2, 2, HR, 128), BF),
+            pltpu.VMEM((SLOT_COUNT, 2, 2, HR, 128), BF),
+            pltpu.VMEM((K, 2, 2, HR, 128), BF),
+            pltpu.VMEM((K, 2, HR, 128), BF),
             pltpu.VMEM((K, HR, 128), BF),
             pltpu.VMEM((K, HR, 128), BF),
             pltpu.VMEM((K, HR, 128), BF),
+            pltpu.VMEM((12, D), F32),
             pltpu.VMEM((ROWS, D), BF),
             pltpu.VMEM((ROWS, D), BF),
             pltpu.VMEM((D, FF), BF),
@@ -1061,8 +1200,8 @@
             pltpu.VMEM((ROWS, D), BF),
             pltpu.VMEM((PART, D), BF),
             pltpu.VMEM((10, 16, D), F32),
-            dma((6, K)),
-            dma((6, K)),
+            dma((7, K)),
+            dma((7, K)),
             dma((K,)),
             dma((9,)),
             dma((8,)),
@@ -1075,7 +1214,23 @@
         compiler_params=pltpu.CompilerParams(
             collective_id=0, has_side_effects=True, vmem_limit_bytes=62 << 20
         ),
-    )(tokens, cotangent, counts, vec, input_weight, output_weight, expand_weight, reduce_weight)
+    )(
+        tokens,
+        cotangent,
+        counts,
+        first_gain,
+        first_bias,
+        input_bias,
+        output_bias,
+        second_gain,
+        second_bias,
+        expand_bias,
+        reduce_bias,
+        input_weight,
+        output_weight,
+        expand_weight,
+        reduce_weight,
+    )
     return pl.pallas_call(
         finish_kernel,
         out_shape=(
@@ -1094,9 +1249,21 @@
             shape((D, D), F32),
             shape((HR,), F32),
         ),
-        in_specs=[vmem] * 5,
-        out_specs=(vmem,) * 14,
-        compiler_params=pltpu.CompilerParams(vmem_limit_bytes=40 << 20),
+        in_specs=[anywhere, vmem, anywhere, anywhere, anywhere],
+        out_specs=tuple(anywhere if i in (0, 1, 4, 6, 10, 12) else vmem for i in range(14)),
+        scratch_shapes=[
+            pltpu.VMEM((K, 2, HR, 128), BF),
+            pltpu.VMEM((PART, D), BF),
+            pltpu.VMEM((2, PART, D), F32),
+            pltpu.VMEM((2, PART, D), BF),
+            pltpu.VMEM((HR, 3 * D), F32),
+            pltpu.VMEM((HR, D), F32),
+            pltpu.VMEM((HR, FF), F32),
+            pltpu.VMEM((D, D), F32),
+            dma((13,)),
+            dma((16,)),
+        ],
+        compiler_params=pltpu.CompilerParams(vmem_limit_bytes=62 << 20),
     )(tot, vs, lo, gto, gtr)
 
 

time: 199 us -> 160 us (0.80)
  Pallas kernels: 185 us -> 159 us
  local copies, waits for them, and re-layouts: 11.6 us -> 0 us
    pallas_call x1, Pallas kernels: 181 us -> 152 us  [local_slice(): pl.pallas_call(layer_kernel, out_shape=(shape((K, 2, HR, 128), BF), shape...]
    unnamed x10 -> x0, local copies, waits for them, and re-layouts: 6.05 us -> none
    another operation x6 -> x0, local copies, waits for them, and re-layouts: 4.11 us -> none  [local_slice(): jnp.stack(rows)]
    pallas_call x1, Pallas kernels: 3.97 us -> 6.61 us  [local_slice(): pl.pallas_call(finish_kernel, out_shape=(shape((MICRO, 1, PART, D), BF),...]
where the time goes in v3:
time: 160 us; the launch traced here: 159 us
  Pallas kernels  159 us (99%)
    pallas_call x1, Pallas kernels, local_slice(): pl.pallas_call(layer_kernel, out_shape=(shape((K, 2, HR, 128), BF), shape...  152 us
    pallas_call x1, Pallas kernels, local_slice(): pl.pallas_call(finish_kernel, out_shape=(shape((MICRO, 1, PART, D), BF),...  6.61 us

profile of v3, /device:TPU:0, one launch (start us, length us, event | category | flops | bytes accessed | tf_op | source)
XLA Modules:
  0.0 159.3 jit_solution(11666376881856361775)
XLA Ops:
  0.7 151.9 %shard_map.254 = (bf16[36,2,192,128]{3,2,1,0:T(8,128)(2,1)}, f32[16,768]{1,0:T(8,128)}, bf16[2,256,768]{2,1,0:T(8,128)(2,1)}, f32[256,768]{1,0:T(8,128)}, bf16[256,768]{1,0:T(8,128)(2,1)}) custom-call(bf16[2,1,256,768]{3,2,1,0:T(8,128)(2,1)} %tok_ref.1, bf16[2,1,256,768]{3,2,1,0:T(8,128)(2,1)} %cot_ref.1, s32[2,1,4]{2,1,0:T(1,128)} %cnt_ref.1, ...), custom_call_target="tpu_custom_call" | custom-call | tf_op jit(solution)/shard_map/pallas_call | solution.py:1157
  152.6 6.6 %shard_map.255 = (bf16[2,1,256,768]{3,2,1,0:T(8,128)(2,1)}, f32[2,1,256,768]{3,2,1,0:T(8,128)}, f32[192]{0:T(256)}, f32[192]{0:T(256)}, f32[192,2304]{1,0:T(8,12...) custom-call(bf16[36,2,192,128]{3,2,1,0:T(8,128)(2,1)} %get-tuple-ele, ...), custom_call_target="tpu_custom_call" | custom-call | tf_op jit(solution)/shard_map/pallas_call | solution.py:1234

commit v4 on v3

--- a/solution.py
+++ b/solution.py
@@ -298,17 +298,24 @@
 MESH = pl.DeviceIdType.MESH
 BF = jnp.bfloat16
 F32 = jnp.float32
-K = 36
-QR = 384
-HR = 192
-SLOT_COUNT = 8
+K = 18
+QR = 768
+HR = 384
+CR = 192
+SLOT_COUNT = 4
 ROWS = 512
 PART = 256
 FF = 3072
 LOW = -1e30
-LAGS = (0, 6, 12, 15, 18, 21, 24)
-WAYS = "acbacabca"
-TALL = ((0, 0, 0, 0, 128), (0, 128, 1, 0, 64), (1, 0, 1, 64, 128), (1, 64, 2, 0, 128))
+COLUMNS = (0, 1, 2, 3, 4, 5, 0, 1, 6, 7, 12, 13, 2, 3, 8, 9, 14, 15, 4, 5, 10, 11, 16, 17)
+WAYS = "accbabbccbabccbaaa"
+FEED_STEPS = (((), (), (101, 102), (104,), (200, 106), (203, 108, 204, 109)), ((), (100,), (103,), (105,), (201, 107), (202,)))
+NORM_STEPS = ((301, 205, 110), (111,))
+OUT_STEPS = (300, 303, 207)
+ATTEND_STEPS = (((302,), (208,), (403,), (503, 308, 212, 405, 211), (505, 406, 408), (504, 309, 213)), ((), (304,), (307, 209), (402,), (502,), ()), ((112,), (400,), (401,), (600, 404, 113, 114), (), (312, 605, 410, 601, 506, 214, 115)), ((305, 206), (210,), (500, 306), (501, 310, 603, 407), (), (507, 311, 508)))
+PROJECT_STEPS = (602, 604, 313)
+LAST_STEPS = ((510, 409, 412, 314, 116), (606, 607, 608, 411, 117))
+DRAIN_STEPS = (215, 509, 610, 0, 413, 512, 216, 414, 1, 511, 315, 2, 217, 514, 609, 3, 612, 513, 415, 316, 4, 611, 317, 5, 614, 515, 416, 613, 417, 615, 516, 517, 616, 617)
 
 
 def dot_nn(a, b):
@@ -376,129 +383,107 @@
 
 
 class Reduce:
-    def __init__(self, place, bufs, tot, send, recv, tsem):
+    def __init__(self, place, bufs, tot, csend, send, recv):
         self.p = place
         self.own, self.nbr, self.rc, self.ry, self.rx, self.r1, self.r2 = bufs
-        self.tot, self.send, self.recv, self.tsem = tot, send, recv, tsem
-
-    def copy(self, src, dst, stage, k, peer):
-        return remote(src, dst, self.send.at[stage, k], self.recv.at[stage, k], peer)
-
-    def keep(self, src, dst, k):
-        return pltpu.make_async_copy(src, dst, self.tsem.at[k])
+        self.tot, self.csend, self.send, self.recv = tot, csend, send, recv
+
+    def copy(self, src, dst, kind, stage, k, peer):
+        return remote(src, dst, self.send.at[kind], self.recv.at[stage, k], peer)
+
+    def last(self, src, dst, kind, end, peer):
+        return remote(src, dst, self.send.at[kind], self.send.at[end], peer)
 
     def part(self, far):
-        return pl.ds(pl.multiple_of((1 - self.p.x if far else self.p.x) * 96, 96), 96)
+        return pl.ds(pl.multiple_of((1 - self.p.x if far else self.p.x) * CR, CR), CR)
 
     def c_core(self, k):
-        return self.copy(self.nbr.at[lax.rem(k, SLOT_COUNT)], self.rc.at[k], 0, k, self.p.to_core)
+        slot = self.seat(k)
+        return remote(self.nbr.at[slot], self.rc.at[k], self.csend.at[slot], self.recv.at[0, k], self.p.to_core)
 
     def a_y(self, k):
-        return self.copy(self.own.at[k, 1 - self.p.y], self.ry.at[k], 1, k, self.p.to_y)
+        return self.copy(self.own.at[k, 1 - self.p.y], self.ry.at[k], 0, 1, k, self.p.to_y)
 
     def a_x(self, k):
-        return self.copy(self.own.at[k, self.p.y, 1 - self.p.x], self.rx.at[k], 2, k, self.p.to_x)
+        return self.copy(self.own.at[k, self.p.y, 1 - self.p.x], self.rx.at[k], 1, 2, k, self.p.to_x)
 
     def b_x(self, k):
-        return self.copy(self.own.at[k, :, 1 - self.p.x], self.ry.at[k], 1, k, self.p.to_x)
+        return self.copy(self.own.at[k, :, 1 - self.p.x], self.ry.at[k], 0, 1, k, self.p.to_x)
 
     def b_y(self, k):
-        return self.copy(self.own.at[k, 1 - self.p.y, self.p.x], self.rx.at[k], 2, k, self.p.to_y)
+        return self.copy(self.own.at[k, 1 - self.p.y, self.p.x], self.rx.at[k], 1, 2, k, self.p.to_y)
 
     def half(self, k):
         return self.own.at[k, self.p.y, self.p.x]
 
     def l_in(self, k):
-        return self.copy(self.half(k), self.r1.at[k], 3, k, self.p.to_mate)
+        return self.copy(self.half(k), self.r1.at[k], 2, 3, k, self.p.to_mate)
 
     def l_mid(self, k):
-        return self.copy(self.half(k), self.r2.at[k], 4, k, self.p.to_far)
+        return self.copy(self.half(k), self.r2.at[k], 3, 4, k, self.p.to_far)
 
     def l_out(self, k):
-        return self.copy(self.r2.at[k], self.r1.at[k], 3, k, self.p.to_mate)
-
-    def l_gather(self, k, inner):
+        return self.copy(self.r2.at[k], self.r1.at[k], 2, 3, k, self.p.to_mate)
+
+    def l_leave(self, k, inner):
         src = self.r2 if inner else self.r1
-        return self.copy(src.at[k], self.tot.at[k, self.p.x], 5, k, self.p.to_x)
-
-    def l_keep(self, k, inner):
-        src = self.r2 if inner else self.r1
-        return self.keep(src.at[k], self.tot.at[k, self.p.x], k)
+        self.last(src.at[k], self.tot.at[k, self.p.x], 4, 5, self.p.to_x).start()
+        self.keep(src.at[k], self.tot.at[k, self.p.x]).start()
 
     def q_pair(self, k):
-        return self.copy(self.own.at[k, :, 1 - self.p.h], self.ry.at[k], 1, k, self.p.to_mate)
+        return self.copy(self.own.at[k, :, 1 - self.p.h], self.ry.at[k], 0, 1, k, self.p.to_mate)
 
     def q_y(self, k):
-        return self.copy(self.own.at[k, 1 - self.p.y, self.p.h], self.rx.at[k], 2, k, self.p.to_y)
+        return self.copy(self.own.at[k, 1 - self.p.y, self.p.h], self.rx.at[k], 1, 2, k, self.p.to_y)
 
     def q_x(self, k):
         src = self.own.at[k, self.p.y, self.p.h, self.part(True)]
-        return self.copy(src, self.r1.at[k, pl.ds(0, 96)], 3, k, self.p.to_x)
+        return self.copy(src, self.r1.at[k, pl.ds(0, CR)], 6, 3, k, self.p.to_x)
 
     def q_far(self, k):
         src = self.own.at[k, self.p.y, self.p.h, self.part(False)]
-        return self.copy(src, self.r1.at[k, pl.ds(96, 96)], 4, k, self.p.to_far)
+        return self.copy(src, self.r1.at[k, pl.ds(CR, CR)], 7, 4, k, self.p.to_far)
 
     def q_gather(self, k):
         both = self.r2.at[k, self.part(False)]
-        return self.copy(both, both, 5, k, self.p.to_x)
-
-    def q_spread(self, k):
-        return self.copy(self.r2.at[k], self.tot.at[k, self.p.h], 6, k, self.p.to_mate)
-
-    def q_keep(self, k):
-        return self.keep(self.r2.at[k], self.tot.at[k, self.p.h], k)
-
-    def kinds(self, k):
+        return self.copy(both, both, 8, 5, k, self.p.to_x)
+
+    def q_leave(self, k):
+        self.last(self.r2.at[k], self.tot.at[k, self.p.h], 9, 10, self.p.to_mate).start()
+        self.keep(self.r2.at[k], self.tot.at[k, self.p.h]).start()
+
+    def keep(self, src, dst):
+        return pltpu.make_async_copy(src, dst, self.send.at[11])
+
+    def split(self, k, a, b, c):
+        {"a": a, "b": b, "c": c}[WAYS[k]](k)
+
+    def seat(self, k):
+        return k % SLOT_COUNT if isinstance(k, int) else lax.rem(k, SLOT_COUNT)
+
+    def slot(self, k):
         if isinstance(k, int):
-            return WAYS[k % len(WAYS)]
-        m = lax.rem(k, len(WAYS))
-        out = {}
-        for way in "abc":
-            hit = m < 0
-            for i, one in enumerate(WAYS):
-                if one == way:
-                    hit = jnp.logical_or(hit, m == i)
-            out[way] = hit
-        return out
-
-    def split(self, k, a, b, c):
-        kinds = self.kinds(k)
-        if isinstance(kinds, str):
-            {"a": a, "b": b, "c": c}[kinds](k)
-            return
-        if a is b:
-            pl.when(jnp.logical_not(kinds["c"]))(lambda: a(k))
+            self.c_core(k - SLOT_COUNT).wait_send()
         else:
-            pl.when(kinds["a"])(lambda: a(k))
-            pl.when(kinds["b"])(lambda: b(k))
-        pl.when(kinds["c"])(lambda: c(k))
-
-    def slot(self, k):
-        @pl.when(k >= SLOT_COUNT)
-        def _():
-            self.c_core(k - SLOT_COUNT).wait_send()
-
-        return lax.rem(k, SLOT_COUNT)
-
-    def emit_wide(self, k, grad):
-        slot = self.slot(k)
+            pl.when(k >= SLOT_COUNT)(lambda: self.c_core(k - SLOT_COUNT).wait_send())
+
+    def put_wide(self, k, side, grad):
+        slot = self.seat(k)
         for yy in range(2):
-            for side in range(2):
-                cols = slice(side * 128, (side + 1) * 128)
-                self.own[k, yy, side] = grad[yy * HR : (yy + 1) * HR, cols]
-                self.nbr[slot, yy, side] = grad[QR + yy * HR : QR + (yy + 1) * HR, cols]
-        self.c_core(k).start()
-
-    def emit_tall(self, k, grad, first):
-        slot = self.slot(k)
+            for i in range(2):
+                rows = slice(i * CR, (i + 1) * CR)
+                cols = slice(i * 128, (i + 1) * 128)
+                self.own[k, yy, side, rows] = grad[yy * CR : (yy + 1) * CR, cols]
+                self.nbr[slot, yy, side, rows] = grad[(2 + yy) * CR : (3 + yy) * CR, cols]
+
+    def put_tall(self, k, grad):
+        slot = self.seat(k)
         for yy in range(2):
-            for side, to, block, low, high in TALL:
-                cols = slice(first + block * 128, first + (block + 1) * 128)
-                rows = slice(to, to + high - low)
-                self.own[k, yy, side, rows] = grad[yy * 128 + low : yy * 128 + high, cols]
-                self.nbr[slot, yy, side, rows] = grad[256 + yy * 128 + low : 256 + yy * 128 + high, cols]
-        self.c_core(k).start()
+            for i in range(6):
+                rows = slice(i % 3 * 128, (i % 3 + 1) * 128)
+                cols = slice(i * 128, (i + 1) * 128)
+                self.own[k, yy, i // 3, rows] = grad[yy * 128 : (yy + 1) * 128, cols]
+                self.nbr[slot, yy, i // 3, rows] = grad[(2 + yy) * 128 : (3 + yy) * 128, cols]
 
     def stage_1(self, k):
         self.c_core(k).wait_recv()
@@ -551,7 +536,7 @@
         def c(k):
             self.q_x(k).wait_recv()
             mine = self.own.at[k, self.p.y, self.p.h, self.part(False)]
-            mine[...] = mine[...] + self.r1[k, pl.ds(0, 96)]
+            mine[...] = mine[...] + self.r1[k, pl.ds(0, CR)]
             self.q_far(k).start()
 
         self.split(k, line, line, c)
@@ -563,13 +548,12 @@
                 self.l_mid(k).wait_recv()
                 self.r2[k] = self.r2[k] + self.own[k, self.p.y, self.p.x]
                 self.l_out(k).start()
-                self.l_gather(k, True).start()
-                self.l_keep(k, True).start()
+                self.l_leave(k, True)
 
         def c(k):
             self.q_far(k).wait_recv()
             mine = self.own.at[k, self.p.y, self.p.h, self.part(False)]
-            self.r2[k, self.part(False)] = mine[...] + self.r1[k, pl.ds(96, 96)]
+            self.r2[k, self.part(False)] = mine[...] + self.r1[k, pl.ds(CR, CR)]
             self.q_gather(k).start()
 
         self.split(k, line, line, c)
@@ -579,48 +563,51 @@
             @pl.when(self.p.outer)
             def _():
                 self.l_in(k).wait_recv()
-                self.l_gather(k, False).start()
-                self.l_keep(k, False).start()
+                self.l_leave(k, False)
 
         def c(k):
             self.q_gather(k).wait_recv()
-            self.q_spread(k).start()
-            self.q_keep(k).start()
+            self.q_leave(k)
 
         self.split(k, line, line, c)
 
-    def stage_7(self, k):
-        self.a_y(k).wait_send()
-        self.a_x(k).wait_send()
-
-        @pl.when(k >= K - SLOT_COUNT)
-        def _():
+    def close(self):
+        rest = WAYS.count("c")
+        line = K - rest
+        peer = self.p.to_x
+
+        def whole(ref, count, kind):
+            span = ref.at[pl.ds(0, count)]
+            return remote(span, span, self.send.at[kind], self.send.at[kind], peer)
+
+        def parts(kind):
+            span = self.r1.at[pl.ds(0, rest), pl.ds(0, CR)]
+            return remote(span, span, self.send.at[kind], self.send.at[kind], peer)
+
+        for k in range(K - SLOT_COUNT, K):
             self.c_core(k).wait_send()
-
-        def line(k):
-            self.l_gather(k, True).wait()
-            self.l_in(k).wait_send()
-            self.l_keep(k, True).wait()
-            pl.when(self.p.inner)(lambda: self.l_mid(k).wait_send())
-
-        def c(k):
-            self.q_spread(k).wait()
-            self.q_x(k).wait_send()
-            self.q_far(k).wait_send()
-            self.q_gather(k).wait_send()
-            self.q_keep(k).wait()
-
-        self.split(k, line, line, c)
-
-    def tick(self, t):
-        stages = (self.stage_1, self.stage_2, self.stage_3, self.stage_4, self.stage_5, self.stage_6, self.stage_7)
-        for lag, stage in zip(LAGS, stages):
-            k = t - lag
-            if isinstance(k, int):
-                if 0 <= k < K:
-                    stage(k)
-            else:
-                pl.when(jnp.logical_and(k >= 0, k < K))(lambda stage=stage, k=k: stage(k))
+        whole(self.ry, K, 0).wait_send()
+        whole(self.rx, K, 1).wait_send()
+        whole(self.r1, line, 2).wait_send()
+        pl.when(self.p.inner)(lambda: whole(self.r1, line, 3).wait_send())
+        whole(self.r1, line, 4).wait_send()
+        whole(self.r1, line, 5).wait_recv()
+        parts(6).wait_send()
+        parts(7).wait_send()
+        parts(8).wait_send()
+        whole(self.r1, rest, 9).wait_send()
+        whole(self.r1, rest, 10).wait_recv()
+        pltpu.make_async_copy(self.r1, self.r2, self.send.at[11]).wait()
+
+    def run(self, steps):
+        stages = (self.stage_1, self.stage_2, self.stage_3, self.stage_4, self.stage_5, self.stage_6)
+        for step in steps:
+            stages[step // 100 - 1](step % 100)
+
+    def run_at(self, index, table):
+        for i, steps in enumerate(table):
+            if steps:
+                pl.when(index == i)(lambda steps=steps: self.run(steps))
 
 
 def norm_parts(values):
@@ -651,8 +638,8 @@
     tot_ref, vs, lo_ref, gto_ref, gtr_ref,
     own, nbr, rc, ry, rx, r1, r2, vec,
     tokx, dyx, w1, wo, wr, qkv, kvr, rowb, kaug, qaug, att, mid, low2, turned, g_t, du_t, y_sum, h_sum,
-    d_out, dp, dkv_own, dkv_send, dkv_recv, lo, gts, vr,
-    send, recv, tsem, lsem, xsend, xrecv, ksend, krecv, vsend, vrecv,
+    d_out, dp, dq_sum, dkv_own, dkv_far, dkv_send, dkv_recv, lo, gts, vr,
+    csend, send, recv, lsem, xsend, xrecv, ksend, krecv, vsend, vrecv,
 ):
     p = Place()
     loads = [
@@ -665,7 +652,7 @@
     for one in loads:
         one.start()
     enter(p)
-    red = Reduce(p, (own, nbr, rc, ry, rx, r1, r2), tot_ref, send, recv, tsem)
+    red = Reduce(p, (own, nbr, rc, ry, rx, r1, r2), tot_ref, csend, send, recv)
 
     def swap(index, src, dst, peer):
         return remote(src, dst, xsend.at[index], xrecv.at[index], peer)
@@ -785,8 +772,8 @@
     def turn(rows, block):
         flipped = block.T
         for quarter in range(4):
-            seat = pl.multiple_of(p.seat(quarter) * HR, HR)
-            turned[pl.ds(seat, HR), rows] = flipped[quarter * HR : (quarter + 1) * HR]
+            seat = pl.multiple_of(p.seat(quarter) * CR, CR)
+            turned[pl.ds(seat, CR), rows] = flipped[quarter * CR : (quarter + 1) * CR]
 
     loads[3].wait()
 
@@ -832,12 +819,15 @@
         w_down = jnp.concatenate([wr[at128(s), :] for s in starts], axis=0)
         du_t[...] = (dot_nt(dyx[...], w_down) * slope).astype(BF)
         tall = dot_nn(g_t[...].T, dyx[...]).astype(BF)
-        red.emit_tall(4 * t, tall, 0)
-        red.emit_tall(4 * t + 1, tall, QR)
+        red.slot(2 * t)
+        red.put_tall(2 * t, tall)
+        red.c_core(2 * t).start()
+        red.slot(2 * t + 1)
         for e in range(2):
             seats = [e + 2 * (p.core if cc == 0 else 1 - p.core) for cc in range(2)]
             right = jnp.concatenate([du_t[:, at128(s * 128)] for s in seats], axis=1)
-            red.emit_wide(4 * t + 2 + e, dot_nn(turned[...], right).astype(BF))
+            red.put_wide(2 * t + 1, e, dot_nn(turned[...], right).astype(BF))
+        red.c_core(2 * t + 1).start()
         sums = jnp.sum(du_t[...].astype(F32), axis=0, keepdims=True)
         seat = [sums[:, i * 128 : (i + 1) * 128] for i in range(4)]
         vs[8:12, at128(t * 128)] = jnp.concatenate(
@@ -848,10 +838,10 @@
             ],
             axis=0,
         )
-        red.tick(2 * t)
+        red.run_at(t, FEED_STEPS[0])
         y_sum[...] += dot_nn(g_t[...], w_down)
         h_sum[...] += dot_nt(du_t[...], w_up)
-        red.tick(2 * t + 1)
+        red.run_at(t, FEED_STEPS[1])
 
     loop(0, 6, feed)
     reload_wi = pltpu.make_async_copy(wi_ref, w1.at[:, pl.ds(0, 2304)], lsem.at[6])
@@ -874,15 +864,37 @@
         vs[4:5] += jnp.sum(block.astype(F32), axis=0, keepdims=True)
         d_out[rows] = dot_nt(block, wo[...]).astype(BF)
         turn(rows, att[rows])
+        red.run_at(i, NORM_STEPS)
 
     loop(0, 2, second)
-    red.tick(12)
-
-    def out_grad(n):
-        red.emit_wide(24 + n, dot_nn(turned[...], low2[:, at256(n * 256)]).astype(BF))
-
-    loop(0, 3, out_grad)
-    red.tick(13)
+    c_lo = swap(6, lo.at[pl.ds(PART, PART)], lo_ref.at[p.y], p.to_y)
+    keep_lo = pltpu.make_async_copy(lo.at[pl.ds(0, PART)], lo_ref.at[p.y], lsem.at[7])
+    keep_lo.start()
+
+    red.slot(12)
+    red.slot(13)
+    for k, side, first in ((12, 0, 0), (12, 1, 256), (13, 0, 512)):
+        red.put_wide(k, side, dot_nn(turned[...], low2[:, first : first + 256]).astype(BF))
+    red.c_core(12).start()
+    red.run(OUT_STEPS)
+
+    def turn_first(i):
+        rows = at256(i * PART)
+        hat, _ = norm_parts(tokx[rows].astype(F32))
+        turn(rows, (hat * vec[0:1] + vec[1:2]).astype(BF))
+
+    loop(0, 2, turn_first)
+
+    def in_grads(group):
+        def one(i):
+            at = 3 * group + i + 1
+            k, side = 13 + at // 2, lax.rem(at, 2)
+            pl.when(side == 0)(lambda: red.slot(k))
+            cols = at256(i * 768 + group * 256)
+            red.put_wide(k, side, dot_nn(turned[...], dp[:, cols]).astype(BF))
+            pl.when(side == 1)(lambda: red.c_core(k).start())
+
+        loop(0, 3, one)
 
     def c_dkv(pair):
         return remote(
@@ -906,9 +918,11 @@
         grads = d_out[:, at128(col)]
         outs = att[:, at128(col)].astype(F32)
         three = jnp.where(lane_k < 3, 1.0, 0.0).astype(BF)
-        dq = jnp.zeros((128, ROWS), F32)
-        dk = [jnp.zeros((ROWS, 128), F32)] * 2
-        dv = [jnp.zeros((ROWS, 128), F32)] * 2
+
+        @pl.when(pair >= 1)
+        def _():
+            settle(pair - 1)
+
         for h in range(2):
             q_h = query * head_mask[h]
             g_h = grads * head_mask[h]
@@ -931,50 +945,41 @@
                 v_wide = jnp.concatenate([value, three], axis=1)
                 weight = jnp.exp(dot_nt(k_wide, q_wide))
                 slope = (weight * dot_nt(v_wide, g_wide)).astype(BF)
-                dv[side] = dv[side] + dot_nn(weight.astype(BF), g_h)
-                dk[side] = dk[side] + dot_nn(slope, q_h)
-                dq = dq + dot_nn((key * head_mask[h]).T, slope)
-        dp[:, at128(col)] = (dq.T.astype(BF).astype(F32) * 0.125).astype(BF)
-
-        @pl.when(pair >= 1)
-        def _():
-            settle(pair - 1)
+                add_k, add_v = dot_nn(slope, q_h), dot_nn(weight.astype(BF), g_h)
+                add_q = dot_nn((key * head_mask[h]).T, slope)
+                if h == 0 and side == 0:
+                    dq_sum[...] = add_q
+                else:
+                    dq_sum[...] += add_q
+                sums = dkv_own.at[slot] if side == 0 else dkv_far
+                if h == 0:
+                    sums[0] = add_k
+                    sums[1] = add_v
+                else:
+                    sums[0] += add_k
+                    sums[1] += add_v
+                red.run_at(pair, ATTEND_STEPS[2 * h + side])
+        dp[:, at128(col)] = (dq_sum[...].T.astype(BF).astype(F32) * 0.125).astype(BF)
 
         @pl.when(pair >= 2)
         def _():
             c_dkv(pair - 2).wait_send()
 
-        dkv_own[slot, 0] = dk[0]
-        dkv_own[slot, 1] = dv[0]
-        dkv_send[slot, 0] = dk[1].astype(BF)
-        dkv_send[slot, 1] = dv[1].astype(BF)
+        dkv_send[slot] = dkv_far[...].astype(BF)
         c_dkv(pair).start()
-        red.tick(14 + 2 * pair)
-        red.tick(15 + 2 * pair)
+        pl.when(jnp.logical_and(pair >= 2, lax.rem(pair, 2) == 0))(lambda: in_grads(pair // 2 - 1))
+        pl.when(pair == 1)(lambda: c_lo.start())
 
     loop(0, 6, attend_back)
     settle(5)
     c_dkv(4).wait_send()
     c_dkv(5).wait_send()
 
-    def turn_first(i):
-        rows = at256(i * PART)
-        hat, _ = norm_parts(tokx[rows].astype(F32))
-        turn(rows, (hat * vec[0:1] + vec[1:2]).astype(BF))
-
-    loop(0, 2, turn_first)
-
-    def in_grad(n):
-        red.emit_wide(27 + n, dot_nn(turned[...], dp[:, at256(n * 256)]).astype(BF))
-        red.tick(26 + n)
-
-    loop(0, 9, in_grad)
+    in_grads(2)
+    red.run(PROJECT_STEPS)
     vs[2:3] = jnp.sum(dp[:, 0:768].astype(F32), axis=0, keepdims=True)
     vs[3:4] = jnp.sum(dp[:, 1536:2304].astype(F32), axis=0, keepdims=True)
     reload_wi.wait()
-    c_lo = swap(6, lo.at[pl.ds(PART, PART)], lo_ref.at[p.y], p.to_y)
-    keep_lo = pltpu.make_async_copy(lo.at[pl.ds(0, PART)], lo_ref.at[p.y], lsem.at[7])
-    keep_lo.start()
 
     def first_back(i):
         rows = at256(i * PART)
@@ -983,11 +988,13 @@
         vs[0:1] += jnp.sum(grad * hat, axis=0, keepdims=True)
         vs[1:2] += jnp.sum(grad, axis=0, keepdims=True)
         y_sum[rows] = mid[rows] + norm_back(hat, scale, vec[0:1], grad)
+        red.run_at(i, LAST_STEPS)
 
     loop(0, 2, first_back)
     gts[...] = y_sum[pl.ds(PART, PART)].astype(BF)
     c_gt = swap(7, gts, gtr_ref, p.to_y)
     keep_gt = pltpu.make_async_copy(y_sum.at[pl.ds(0, PART)], gto_ref, lsem.at[8])
+    c_gt.start()
     keep_gt.start()
 
     def c_vec(stage, peer):
@@ -1001,50 +1008,50 @@
         c_vec(stage, peer).wait()
         vs[...] += vr[2 * stage + 1]
 
+    def vec_0():
+        vec_take(0, p.to_core)
+        vec_pair(1, p.to_y)
+
+    def vec_1():
+        vec_take(1, p.to_y)
+        vec_pair(2, p.to_x)
+
+    def vec_2():
+        vec_take(2, p.to_x)
+
+        @pl.when(p.outer)
+        def _():
+            vec_pair(3, p.to_mate)
+
+    def vec_3():
+        @pl.when(p.inner)
+        def _():
+            c_vec(3, p.to_mate).wait_recv()
+            vs[...] += vr[7]
+            vec_pair(4, p.to_far)
+
+    def vec_4():
+        @pl.when(p.inner)
+        def _():
+            vec_take(4, p.to_far)
+            vec_pair(3, p.to_mate)
+
+    def vec_5():
+        @pl.when(p.outer)
+        def _():
+            c_vec(3, p.to_mate).wait_recv()
+            vs[...] = vr[7]
+
+        c_vec(3, p.to_mate).wait_send()
+
     vec_pair(0, p.to_core)
-    red.tick(35)
-    vec_take(0, p.to_core)
-    vec_pair(1, p.to_y)
-    red.tick(36)
-    vec_take(1, p.to_y)
-    vec_pair(2, p.to_x)
-    red.tick(37)
-    vec_take(2, p.to_x)
-
-    @pl.when(p.outer)
-    def _():
-        vec_pair(3, p.to_mate)
-
-    red.tick(38)
-
-    @pl.when(p.inner)
-    def _():
-        c_vec(3, p.to_mate).wait_recv()
-        vs[...] += vr[7]
-        vec_pair(4, p.to_far)
-
-    red.tick(39)
-
-    @pl.when(p.inner)
-    def _():
-        vec_take(4, p.to_far)
-        vec_pair(3, p.to_mate)
-
-    red.tick(40)
-
-    @pl.when(p.outer)
-    def _():
-        c_vec(3, p.to_mate).wait_recv()
-        vs[...] = vr[7]
-
-    c_vec(3, p.to_mate).wait_send()
-    c_lo.start()
-    c_gt.start()
-
-    def drain(t):
-        red.tick(t)
-
-    loop(41, K + LAGS[-1], drain)
+    vec_steps = (vec_0, vec_1, vec_2, vec_3, vec_4, vec_5)
+    for step in DRAIN_STEPS:
+        if step < 100:
+            vec_steps[step]()
+        else:
+            red.run((step,))
+    red.close()
     c_tok.wait_send()
     c_row.wait_send()
     c_cot.wait_send()
@@ -1064,15 +1071,15 @@
 ):
     y = lax.axis_index("frame") // 2
     frame = lax.axis_index("frame")
-    spans = [(4 * t, 4) for t in range(6)] + [(24, 3)] + [(27 + 3 * i, 3) for i in range(3)]
+    spans = [(2 * t, 2) for t in range(6)] + [(12, 2), (14, 2), (16, 2)]
     loads = [
         pltpu.make_async_copy(tot_ref.at[pl.ds(k, n)], tot.at[pl.ds(k, n)], in_sem.at[i])
         for i, (k, n) in enumerate(spans)
     ]
     loads += [
-        pltpu.make_async_copy(gtr_ref, gtr, in_sem.at[10]),
-        pltpu.make_async_copy(gto, gt_s.at[0], in_sem.at[11]),
-        pltpu.make_async_copy(lo_in, lo_s, in_sem.at[12]),
+        pltpu.make_async_copy(gtr_ref, gtr, in_sem.at[9]),
+        pltpu.make_async_copy(gto, gt_s.at[0], in_sem.at[10]),
+        pltpu.make_async_copy(lo_in, lo_s, in_sem.at[11]),
     ]
     for one in loads:
         one.start()
@@ -1085,40 +1092,40 @@
 
     for t in range(6):
         loads[t].wait()
-        for hh in range(2):
-            for side, to, block, low, high in TALL:
-                col = (3 * hh + block) * 128
-                wr[t * 128 + low : t * 128 + high, col : col + 128] = tot[
-                    4 * t + hh, side, to : to + high - low
-                ].astype(F32)
         rows = pl.ds(t * 128, 128)
+        for i in range(6):
+            block = slice(i % 3 * 128, (i % 3 + 1) * 128)
+            wr[rows, i * 128 : (i + 1) * 128] = tot[2 * t, i // 3, block].astype(F32)
         leave(wr.at[rows], wr_out.at[rows])
         for j in range(4):
             cols = pl.ds(j * 768 + t * 128, 128)
-            we[:, cols] = tot[4 * t + 2 + j // 2, j % 2].astype(F32)
+            block = slice(j % 2 * CR, (j % 2 + 1) * CR)
+            we[:, cols] = tot[2 * t + 1, j // 2, block].astype(F32)
     leave(we, we_out)
-    for i, (src, dst) in enumerate([(wo, wo_out)] + [(wi, wi_out)] * 3):
-        loads[6 + i].wait()
-        base = 24 + 3 * i
-        start = 768 * max(i - 1, 0)
-        for n in range(3):
-            for side in range(2):
-                col = start + n * 256 + side * 128
-                src[:, col : col + 128] = tot[base + n, side].astype(F32)
-        cols = pl.ds(start, 768)
-        leave(src.at[:, cols], dst.at[:, cols])
-    loads[10].wait()
+    for n, col in enumerate(COLUMNS):
+        if n % 8 == 0:
+            loads[6 + n // 8].wait()
+        block = slice(n % 2 * CR, (n % 2 + 1) * CR)
+        value = tot[12 + n // 4, n % 4 // 2, block].astype(F32)
+        if n < 6:
+            wo[:, col * 128 : (col + 1) * 128] = value
+        else:
+            wi[:, col * 128 : (col + 1) * 128] = value
+        if n == 5:
+            leave(wo, wo_out)
+    leave(wi, wi_out)
+    loads[9].wait()
     gt_s[1] = gtr[...].astype(F32)
     leave(gt_s.at[1], gt.at[1 - y, 0])
+    loads[10].wait()
+    leave(gt_s.at[0], gt.at[y, 0])
     loads[11].wait()
-    leave(gt_s.at[0], gt.at[y, 0])
-    loads[12].wait()
     leave(lo_s.at[0], lo_out.at[0, 0])
     leave(lo_s.at[1], lo_out.at[1, 0])
-    mine = vs[0:8, 0:HR]
+    mine = vs[0:8, 0:CR]
     row = vs[8:9]
     for f in range(1, 4):
-        mine = jnp.where(frame == f, vs[0:8, f * HR : (f + 1) * HR], mine)
+        mine = jnp.where(frame == f, vs[0:8, f * CR : (f + 1) * CR], mine)
         row = jnp.where(frame == f, vs[8 + f : 9 + f], row)
     g0[...] = mine[0]
     g1[...] = mine[1]
@@ -1194,15 +1201,17 @@
             pltpu.VMEM((ROWS, D), F32),
             pltpu.VMEM((ROWS, D), BF),
             pltpu.VMEM((ROWS, 3 * D), BF),
+            pltpu.VMEM((128, ROWS), F32),
             pltpu.VMEM((2, 2, ROWS, 128), F32),
+            pltpu.VMEM((2, ROWS, 128), F32),
             pltpu.VMEM((2, 2, ROWS, 128), BF),
             pltpu.VMEM((6, 2, ROWS, 128), BF),
             pltpu.VMEM((ROWS, D), BF),
             pltpu.VMEM((PART, D), BF),
             pltpu.VMEM((10, 16, D), F32),
-            dma((7, K)),
-            dma((7, K)),
-            dma((K,)),
+            dma((SLOT_COUNT,)),
+            dma((12,)),
+            dma((6, K)),
             dma((9,)),
             dma((8,)),
             dma((8,)),
@@ -1236,18 +1245,18 @@
         out_shape=(
             shape((MICRO, 1, PART, D), BF),
             shape((MICRO, 1, PART, D), F32),
-            shape((HR,), F32),
-            shape((HR,), F32),
-            shape((HR, 3 * D), F32),
-            shape((2, HR), F32),
-            shape((HR, D), F32),
-            shape((HR,), F32),
-            shape((HR,), F32),
-            shape((HR,), F32),
-            shape((HR, FF), F32),
+            shape((CR,), F32),
+            shape((CR,), F32),
+            shape((CR, 3 * D), F32),
+            shape((2, CR), F32),
+            shape((CR, D), F32),
+            shape((CR,), F32),
+            shape((CR,), F32),
+            shape((CR,), F32),
+            shape((CR, FF), F32),
             shape((D,), F32),
             shape((D, D), F32),
-            shape((HR,), F32),
+            shape((CR,), F32),
         ),
         in_specs=[anywhere, vmem, anywhere, anywhere, anywhere],
         out_specs=tuple(anywhere if i in (0, 1, 4, 6, 10, 12) else vmem for i in range(14)),
@@ -1256,11 +1265,11 @@
             pltpu.VMEM((PART, D), BF),
             pltpu.VMEM((2, PART, D), F32),
             pltpu.VMEM((2, PART, D), BF),
-            pltpu.VMEM((HR, 3 * D), F32),
-            pltpu.VMEM((HR, D), F32),
-            pltpu.VMEM((HR, FF), F32),
+            pltpu.VMEM((CR, 3 * D), F32),
+            pltpu.VMEM((CR, D), F32),
+            pltpu.VMEM((CR, FF), F32),
             pltpu.VMEM((D, D), F32),
-            dma((13,)),
+            dma((12,)),
             dma((16,)),
         ],
         compiler_params=pltpu.CompilerParams(vmem_limit_bytes=62 << 20),

time: 160 us -> 148 us (0.925)
  Pallas kernels: 159 us -> 147 us
    pallas_call x1, Pallas kernels: 152 us -> 141 us  [local_slice(): pl.pallas_call(layer_kernel, out_shape=(shape((K, 2, HR, 128), BF), shape...]
where the time goes in v4:
time: 148 us
  Pallas kernels  147 us (99%)
    pallas_call x1, Pallas kernels, local_slice(): pl.pallas_call(layer_kernel, out_shape=(shape((K, 2, HR, 128), BF), shape...  141 us
    pallas_call x1, Pallas kernels, local_slice(): pl.pallas_call(finish_kernel, out_shape=(shape((MICRO, 1, PART, D), BF),...  6.6 us

profile of v4, /device:TPU:0, one launch (start us, length us, event | category | flops | bytes accessed | tf_op | source)
XLA Modules:
  0.0 148.0 jit_solution(6491041239688613429)
XLA Ops:
  0.7 140.6 %shard_map.254 = (bf16[18,2,384,128]{3,2,1,0:T(8,128)(2,1)}, f32[16,768]{1,0:T(8,128)}, bf16[2,256,768]{2,1,0:T(8,128)(2,1)}, f32[256,768]{1,0:T(8,128)}, bf16[256,768]{1,0:T(8,128)(2,1)}) custom-call(bf16[2,1,256,768]{3,2,1,0:T(8,128)(2,1)} %tok_ref.1, bf16[2,1,256,768]{3,2,1,0:T(8,128)(2,1)} %cot_ref.1, s32[2,1,4]{2,1,0:T(1,128)} %cnt_ref.1, ...), custom_call_target="tpu_custom_call" | custom-call | tf_op jit(solution)/shard_map/pallas_call | solution.py:1164
  141.3 6.6 %shard_map.255 = (bf16[2,1,256,768]{3,2,1,0:T(8,128)(2,1)}, f32[2,1,256,768]{3,2,1,0:T(8,128)}, f32[192]{0:T(256)}, f32[192]{0:T(256)}, f32[192,2304]{1,0:T(8,12...) custom-call(bf16[18,2,384,128]{3,2,1,0:T(8,128)(2,1)} %get-tuple-ele, ...), custom_call_target="tpu_custom_call" | custom-call | tf_op jit(solution)/shard_map/pallas_call | solution.py:1243

commit v5 on v4

--- a/solution.py
+++ b/solution.py
@@ -298,7 +298,8 @@
 MESH = pl.DeviceIdType.MESH
 BF = jnp.bfloat16
 F32 = jnp.float32
-K = 18
+K = 20
+BUFFERS = 18
 QR = 768
 HR = 384
 CR = 192
@@ -307,15 +308,17 @@
 PART = 256
 FF = 3072
 LOW = -1e30
-COLUMNS = (0, 1, 2, 3, 4, 5, 0, 1, 6, 7, 12, 13, 2, 3, 8, 9, 14, 15, 4, 5, 10, 11, 16, 17)
-WAYS = "accbabbccbabccbaaa"
-FEED_STEPS = (((), (), (101, 102), (104,), (200, 106), (203, 108, 204, 109)), ((), (100,), (103,), (105,), (201, 107), (202,)))
-NORM_STEPS = ((301, 205, 110), (111,))
-OUT_STEPS = (300, 303, 207)
-ATTEND_STEPS = (((302,), (208,), (403,), (503, 308, 212, 405, 211), (505, 406, 408), (504, 309, 213)), ((), (304,), (307, 209), (402,), (502,), ()), ((112,), (400,), (401,), (600, 404, 113, 114), (), (312, 605, 410, 601, 506, 214, 115)), ((305, 206), (210,), (500, 306), (501, 310, 603, 407), (), (507, 311, 508)))
-PROJECT_STEPS = (602, 604, 313)
-LAST_STEPS = ((510, 409, 412, 314, 116), (606, 607, 608, 411, 117))
-DRAIN_STEPS = (215, 509, 610, 0, 413, 512, 216, 414, 1, 511, 315, 2, 217, 514, 609, 3, 612, 513, 415, 316, 4, 611, 317, 5, 614, 515, 416, 613, 417, 615, 516, 517, 616, 617)
+COLUMNS = (0, 1, 2, 3, 4, 5, 0, 1, 6, 7, 12, 13, 2, 3, 8, 9, 14, 4, 15, 5, 10, 16, 11, 17)
+LAST_BIG = 16
+WAYS = "acababbccbabccbaaaab"
+CUTS = (0, 1, 2, 3)
+FEED_STEPS = (((), (), (101, 102), (104,), (200, 106), (203, 202, 108, 109)), ((), (100,), (103,), (105,), (201, 107), ()))
+NORM_STEPS = ((), (205, 110, 204, 111))
+OUT_STEPS = (207, 300)
+ATTEND_STEPS = (((301,), (400, 302), (209, 500), (600, 306, 402, 211, 401), (501,), (213, 605, 312, 410)), ((), (), (307, 212, 304), (603, 404, 113, 505, 310, 114), (), (507, 214, 311, 506, 115, 601, 116, 508)), ((303, 112, 208, 206), (403,), (503, 308), (407,), (), (602,)), ((305,), (210,), (405,), (406, 408, 502), (309, 504), (409, 313, 604, 510, 412)))
+PROJECT_STEPS = (411, 314, 607, 606, 608, 509)
+LAST_STEPS = ((215, 117, 413, 118, 119, 610, 512, 216), (414, 511))
+DRAIN_STEPS = (217, 315, 0, 218, 609, 219, 514, 513, 1, 415, 611, 612, 2, 316, 614, 317, 3, 515, 318, 4, 416, 319, 417, 613, 615, 418, 5, 516, 419, 517, 518, 519, 616, 617, 618, 619)
 
 
 def dot_nn(a, b):
@@ -394,63 +397,102 @@
     def last(self, src, dst, kind, end, peer):
         return remote(src, dst, self.send.at[kind], self.send.at[end], peer)
 
-    def part(self, far):
-        return pl.ds(pl.multiple_of((1 - self.p.x if far else self.p.x) * CR, CR), CR)
+    def place(self, k):
+        if k < LAST_BIG:
+            return k, 0, HR
+        return LAST_BIG + (k - LAST_BIG) // 2, (k - LAST_BIG) % 2 * CR, CR
+
+    def part(self, k, far):
+        _, low, rows = self.place(k)
+        side = 1 - self.p.x if far else self.p.x
+        return pl.ds(pl.multiple_of(low + side * (rows // 2), 32), rows // 2)
 
     def c_core(self, k):
         slot = self.seat(k)
-        return remote(self.nbr.at[slot], self.rc.at[k], self.csend.at[slot], self.recv.at[0, k], self.p.to_core)
+        src, dst = self.nbr.at[slot], self.rc.at[k] if not isinstance(k, int) or k < LAST_BIG else None
+        if dst is None:
+            b, low, rows = self.place(k)
+            src, dst = self.nbr.at[slot, :, :, pl.ds(0, rows)], self.rc.at[b, :, :, pl.ds(low, rows)]
+        return remote(src, dst, self.csend.at[slot], self.recv.at[0, k], self.p.to_core)
+
+    def side(self, ref, k, *lead):
+        b, low, rows = self.place(k)
+        return ref.at[(b, *lead, pl.ds(low, rows))]
 
     def a_y(self, k):
-        return self.copy(self.own.at[k, 1 - self.p.y], self.ry.at[k], 0, 1, k, self.p.to_y)
+        return self.copy(
+            self.side(self.own, k, 1 - self.p.y, slice(None)), self.side(self.ry, k, slice(None)), 0, 1, k, self.p.to_y
+        )
 
     def a_x(self, k):
-        return self.copy(self.own.at[k, self.p.y, 1 - self.p.x], self.rx.at[k], 1, 2, k, self.p.to_x)
+        return self.copy(
+            self.side(self.own, k, self.p.y, 1 - self.p.x), self.side(self.rx, k), 1, 2, k, self.p.to_x
+        )
 
     def b_x(self, k):
-        return self.copy(self.own.at[k, :, 1 - self.p.x], self.ry.at[k], 0, 1, k, self.p.to_x)
+        return self.copy(
+            self.side(self.own, k, slice(None), 1 - self.p.x), self.side(self.ry, k, slice(None)), 0, 1, k, self.p.to_x
+        )
 
     def b_y(self, k):
-        return self.copy(self.own.at[k, 1 - self.p.y, self.p.x], self.rx.at[k], 1, 2, k, self.p.to_y)
+        return self.copy(
+            self.side(self.own, k, 1 - self.p.y, self.p.x), self.side(self.rx, k), 1, 2, k, self.p.to_y
+        )
 
     def half(self, k):
-        return self.own.at[k, self.p.y, self.p.x]
+        return self.side(self.own, k, self.p.y, self.p.x)
 
     def l_in(self, k):
-        return self.copy(self.half(k), self.r1.at[k], 2, 3, k, self.p.to_mate)
+        return self.copy(self.half(k), self.side(self.r1, k), 2, 3, k, self.p.to_mate)
 
     def l_mid(self, k):
-        return self.copy(self.half(k), self.r2.at[k], 3, 4, k, self.p.to_far)
+        return self.copy(self.half(k), self.side(self.r2, k), 3, 4, k, self.p.to_far)
 
     def l_out(self, k):
-        return self.copy(self.r2.at[k], self.r1.at[k], 2, 3, k, self.p.to_mate)
+        return self.copy(self.side(self.r2, k), self.side(self.r1, k), 2, 3, k, self.p.to_mate)
 
     def l_leave(self, k, inner):
-        src = self.r2 if inner else self.r1
-        self.last(src.at[k], self.tot.at[k, self.p.x], 4, 5, self.p.to_x).start()
-        self.keep(src.at[k], self.tot.at[k, self.p.x]).start()
+        src = self.side(self.r2 if inner else self.r1, k)
+        dst = self.side(self.tot, k, self.p.x)
+        self.last(src, dst, 4, 5, self.p.to_x).start()
+        self.keep(src, dst).start()
 
     def q_pair(self, k):
-        return self.copy(self.own.at[k, :, 1 - self.p.h], self.ry.at[k], 0, 1, k, self.p.to_mate)
+        return self.copy(
+            self.side(self.own, k, slice(None), 1 - self.p.h),
+            self.side(self.ry, k, slice(None)),
+            0,
+            1,
+            k,
+            self.p.to_mate,
+        )
 
     def q_y(self, k):
-        return self.copy(self.own.at[k, 1 - self.p.y, self.p.h], self.rx.at[k], 1, 2, k, self.p.to_y)
+        return self.copy(
+            self.side(self.own, k, 1 - self.p.y, self.p.h), self.side(self.rx, k), 1, 2, k, self.p.to_y
+        )
+
+    def q_own(self, k, far):
+        return self.own.at[self.place(k)[0], self.p.y, self.p.h, self.part(k, far)]
+
+    def q_in(self, k, second):
+        b, low, rows = self.place(k)
+        return self.r1.at[b, pl.ds(low + second * (rows // 2), rows // 2)]
 
     def q_x(self, k):
-        src = self.own.at[k, self.p.y, self.p.h, self.part(True)]
-        return self.copy(src, self.r1.at[k, pl.ds(0, CR)], 6, 3, k, self.p.to_x)
+        return self.copy(self.q_own(k, True), self.q_in(k, 0), 6, 3, k, self.p.to_x)
 
     def q_far(self, k):
-        src = self.own.at[k, self.p.y, self.p.h, self.part(False)]
-        return self.copy(src, self.r1.at[k, pl.ds(CR, CR)], 7, 4, k, self.p.to_far)
+        return self.copy(self.q_own(k, False), self.q_in(k, 1), 7, 4, k, self.p.to_far)
 
     def q_gather(self, k):
-        both = self.r2.at[k, self.part(False)]
+        both = self.r2.at[self.place(k)[0], self.part(k, False)]
         return self.copy(both, both, 8, 5, k, self.p.to_x)
 
     def q_leave(self, k):
-        self.last(self.r2.at[k], self.tot.at[k, self.p.h], 9, 10, self.p.to_mate).start()
-        self.keep(self.r2.at[k], self.tot.at[k, self.p.h]).start()
+        src, dst = self.side(self.r2, k), self.side(self.tot, k, self.p.h)
+        self.last(src, dst, 9, 10, self.p.to_mate).start()
+        self.keep(src, dst).start()
 
     def keep(self, src, dst):
         return pltpu.make_async_copy(src, dst, self.send.at[11])
@@ -476,6 +518,15 @@
                 self.own[k, yy, side, rows] = grad[yy * CR : (yy + 1) * CR, cols]
                 self.nbr[slot, yy, side, rows] = grad[(2 + yy) * CR : (3 + yy) * CR, cols]
 
+    def put_small(self, k, grad):
+        slot = self.seat(k)
+        b, low, rows = self.place(k)
+        for yy in range(2):
+            for i in range(2):
+                cols = slice(i * 128, (i + 1) * 128)
+                self.own[b, yy, i, low : low + rows] = grad[yy * CR : (yy + 1) * CR, cols]
+                self.nbr[slot, yy, i, 0:rows] = grad[(2 + yy) * CR : (3 + yy) * CR, cols]
+
     def put_tall(self, k, grad):
         slot = self.seat(k)
         for yy in range(2):
@@ -485,9 +536,13 @@
                 self.own[k, yy, i // 3, rows] = grad[yy * 128 : (yy + 1) * 128, cols]
                 self.nbr[slot, yy, i // 3, rows] = grad[(2 + yy) * 128 : (3 + yy) * 128, cols]
 
+    def add(self, to, more):
+        to[...] = to[...] + more[...]
+
     def stage_1(self, k):
         self.c_core(k).wait_recv()
-        self.own[k] = self.own[k] + self.rc[k]
+        both = (slice(None), slice(None))
+        self.add(self.side(self.own, k, *both), self.side(self.rc, k, *both))
         self.split(
             k,
             lambda k: self.a_y(k).start(),
@@ -497,30 +552,32 @@
 
     def stage_2(self, k):
         self.a_y(k).wait_recv()
+        came = self.side(self.ry, k, slice(None))
 
         def a(k):
-            self.own[k, self.p.y] = self.own[k, self.p.y] + self.ry[k]
+            self.add(self.side(self.own, k, self.p.y, slice(None)), came)
             self.a_x(k).start()
 
         def b(k):
-            self.own[k, :, self.p.x] = self.own[k, :, self.p.x] + self.ry[k]
+            self.add(self.side(self.own, k, slice(None), self.p.x), came)
             self.b_y(k).start()
 
         def c(k):
-            self.own[k, :, self.p.h] = self.own[k, :, self.p.h] + self.ry[k]
+            self.add(self.side(self.own, k, slice(None), self.p.h), came)
             self.q_y(k).start()
 
         self.split(k, a, b, c)
 
     def stage_3(self, k):
         self.a_x(k).wait_recv()
+        came = self.side(self.rx, k)
 
         def line(k):
-            self.own[k, self.p.y, self.p.x] = self.own[k, self.p.y, self.p.x] + self.rx[k]
+            self.add(self.half(k), came)
             pl.when(self.p.outer)(lambda: self.l_in(k).start())
 
         def c(k):
-            self.own[k, self.p.y, self.p.h] = self.own[k, self.p.y, self.p.h] + self.rx[k]
+            self.add(self.side(self.own, k, self.p.y, self.p.h), came)
             self.q_x(k).start()
 
         self.split(k, line, line, c)
@@ -530,13 +587,12 @@
             @pl.when(self.p.inner)
             def _():
                 self.l_in(k).wait_recv()
-                self.own[k, self.p.y, self.p.x] = self.own[k, self.p.y, self.p.x] + self.r1[k]
+                self.add(self.half(k), self.side(self.r1, k))
                 self.l_mid(k).start()
 
         def c(k):
             self.q_x(k).wait_recv()
-            mine = self.own.at[k, self.p.y, self.p.h, self.part(False)]
-            mine[...] = mine[...] + self.r1[k, pl.ds(0, CR)]
+            self.add(self.q_own(k, False), self.q_in(k, 0))
             self.q_far(k).start()
 
         self.split(k, line, line, c)
@@ -546,14 +602,14 @@
             @pl.when(self.p.inner)
             def _():
                 self.l_mid(k).wait_recv()
-                self.r2[k] = self.r2[k] + self.own[k, self.p.y, self.p.x]
+                self.add(self.side(self.r2, k), self.half(k))
                 self.l_out(k).start()
                 self.l_leave(k, True)
 
         def c(k):
             self.q_far(k).wait_recv()
-            mine = self.own.at[k, self.p.y, self.p.h, self.part(False)]
-            self.r2[k, self.part(False)] = mine[...] + self.r1[k, pl.ds(CR, CR)]
+            total = self.q_own(k, False)[...] + self.q_in(k, 1)[...]
+            self.r2[self.place(k)[0], self.part(k, False)] = total
             self.q_gather(k).start()
 
         self.split(k, line, line, c)
@@ -572,8 +628,8 @@
         self.split(k, line, line, c)
 
     def close(self):
-        rest = WAYS.count("c")
-        line = K - rest
+        rest = WAYS[:LAST_BIG].count("c") + WAYS[LAST_BIG:].count("c") // 2
+        line = BUFFERS - rest
         peer = self.p.to_x
 
         def whole(ref, count, kind):
@@ -586,8 +642,8 @@
 
         for k in range(K - SLOT_COUNT, K):
             self.c_core(k).wait_send()
-        whole(self.ry, K, 0).wait_send()
-        whole(self.rx, K, 1).wait_send()
+        whole(self.ry, BUFFERS, 0).wait_send()
+        whole(self.rx, BUFFERS, 1).wait_send()
         whole(self.r1, line, 2).wait_send()
         pl.when(self.p.inner)(lambda: whole(self.r1, line, 3).wait_send())
         whole(self.r1, line, 4).wait_send()
@@ -743,29 +799,37 @@
         k_there = jnp.concatenate([kvr[:, at128(col)], kaug[pl.ds(ROWS, ROWS)]], axis=1)
         v_here = jnp.concatenate([qkv[:, at128(1536 + col)], ones], axis=1)
         v_there = jnp.concatenate([kvr[:, at128(768 + col)], ones], axis=1)
-        for block in range(2):
+        def scores(unit):
+            block, h = unit // 2, unit % 2
+            query = qkv[pl.ds(block * PART, PART), at128(col)]
+            lifted = jnp.concatenate([query * head_mask[h], first], axis=1)
+            return dot_nt(lifted, k_here), dot_nt(lifted, k_there)
+
+        ready = scores(0)
+        for unit in range(4):
+            block, h = unit // 2, unit % 2
             rows = pl.ds(block * PART, PART)
-            query = qkv[rows, at128(col)]
-            extra = qaug[rows]
-            outs = []
-            for h in range(2):
-                lifted = jnp.concatenate([query * head_mask[h], first], axis=1)
-                s_here = dot_nt(lifted, k_here)
-                s_there = dot_nt(lifted, k_there)
-                top = jnp.maximum(
-                    jnp.max(s_here, axis=-1, keepdims=True), jnp.max(s_there, axis=-1, keepdims=True)
-                )
-                e_here = jnp.exp(s_here - top).astype(BF)
-                e_there = jnp.exp(s_there - top).astype(BF)
-                both = dot_nn(e_here, v_here) + dot_nn(e_there, v_there)
-                total = both[:, 128:]
-                outs.append(both[:, :128] / total)
-                parts = three_parts(top + jnp.log(total))
-                base = 1 + 3 * (2 * pair + h)
-                for i in range(3):
-                    extra = jnp.where(lane_q == base + i, -parts[i], extra)
-            qaug[rows] = extra
-            att[rows, at128(col)] = jnp.where(lane_q < 64, outs[0], outs[1]).astype(BF)
+            s_here, s_there = ready
+            if unit < 3:
+                ready = scores(unit + 1)
+            top = jnp.maximum(
+                jnp.max(s_here, axis=-1, keepdims=True), jnp.max(s_there, axis=-1, keepdims=True)
+            )
+            e_here = jnp.exp(s_here - top).astype(BF)
+            e_there = jnp.exp(s_there - top).astype(BF)
+            both = dot_nn(e_here, v_here) + dot_nn(e_there, v_there)
+            total = both[:, 128:]
+            out = both[:, :128] / total
+            parts = three_parts(top + jnp.log(total))
+            base = 1 + 3 * (2 * pair + h)
+            extra = qaug[rows] if h == 0 else extra
+            for i in range(3):
+                extra = jnp.where(lane_q == base + i, -parts[i], extra)
+            if h == 0:
+                held = out
+            else:
+                qaug[rows] = extra
+                att[rows, at128(col)] = jnp.where(lane_q < 64, held, out).astype(BF)
 
     loop(0, 6, attend)
 
@@ -885,16 +949,27 @@
 
     loop(0, 2, turn_first)
 
-    def in_grads(group):
-        def one(i):
-            at = 3 * group + i + 1
-            k, side = 13 + at // 2, lax.rem(at, 2)
-            pl.when(side == 0)(lambda: red.slot(k))
-            cols = at256(i * 768 + group * 256)
-            red.put_wide(k, side, dot_nn(turned[...], dp[:, cols]).astype(BF))
-            pl.when(side == 1)(lambda: red.c_core(k).start())
-
-        loop(0, 3, one)
+    def in_grad(first):
+        return dot_nn(turned[...], dp[:, at256(first)]).astype(BF)
+
+    def put_side(at):
+        k, side = 13 + at // 2, lax.rem(at, 2)
+        pl.when(side == 0)(lambda: red.slot(k))
+        red.put_wide(k, side, in_grad(lax.rem(at - 1, 3) * 768 + (at - 1) // 3 * 256))
+        pl.when(side == 1)(lambda: red.c_core(k).start())
+
+    def put_last(k):
+        red.slot(k)
+        red.put_small(k, in_grad((k + 1) % 3 * 768 + (k - 11) // 3 * 256))
+        red.c_core(k).start()
+
+    def in_grads(pair):
+        pl.when(pair == 2)(lambda: loop(1, 4, put_side))
+
+        @pl.when(pair == 4)
+        def _():
+            loop(4, 6, put_side)
+            put_last(16)
 
     def c_dkv(pair):
         return remote(
@@ -923,7 +998,8 @@
         def _():
             settle(pair - 1)
 
-        for h in range(2):
+        def products(unit):
+            h, side = unit // 2, unit % 2
             q_h = query * head_mask[h]
             g_h = grads * head_mask[h]
             parts = three_parts(jnp.sum(g_h.astype(F32) * outs, axis=-1, keepdims=True))
@@ -936,29 +1012,39 @@
             mark = jnp.where(
                 jnp.logical_and(lane_k >= base, lane_k < base + 3), 1.0, 0.0
             ).astype(BF)
-            for side in range(2):
-                if side == 0:
-                    key, value = qkv[:, at128(768 + col)], qkv[:, at128(1536 + col)]
-                else:
-                    key, value = kvr[:, at128(col)], kvr[:, at128(768 + col)]
-                k_wide = jnp.concatenate([key, kaug[pl.ds(side * ROWS, ROWS)] + mark], axis=1)
-                v_wide = jnp.concatenate([value, three], axis=1)
-                weight = jnp.exp(dot_nt(k_wide, q_wide))
-                slope = (weight * dot_nt(v_wide, g_wide)).astype(BF)
-                add_k, add_v = dot_nn(slope, q_h), dot_nn(weight.astype(BF), g_h)
-                add_q = dot_nn((key * head_mask[h]).T, slope)
-                if h == 0 and side == 0:
-                    dq_sum[...] = add_q
-                else:
-                    dq_sum[...] += add_q
-                sums = dkv_own.at[slot] if side == 0 else dkv_far
-                if h == 0:
-                    sums[0] = add_k
-                    sums[1] = add_v
-                else:
-                    sums[0] += add_k
-                    sums[1] += add_v
-                red.run_at(pair, ATTEND_STEPS[2 * h + side])
+            if side == 0:
+                key, value = qkv[:, at128(768 + col)], qkv[:, at128(1536 + col)]
+            else:
+                key, value = kvr[:, at128(col)], kvr[:, at128(768 + col)]
+            k_wide = jnp.concatenate([key, kaug[pl.ds(side * ROWS, ROWS)] + mark], axis=1)
+            v_wide = jnp.concatenate([value, three], axis=1)
+            return dot_nt(k_wide, q_wide), dot_nt(v_wide, g_wide), q_h, g_h, (key * head_mask[h]).T
+
+        ready = products(0)
+        for unit in range(4):
+            h, side = unit // 2, unit % 2
+            score, slope, q_h, g_h, key_t = ready
+            if unit < 3 and unit not in CUTS:
+                ready = products(unit + 1)
+            weight = jnp.exp(score)
+            slope = (weight * slope).astype(BF)
+            add_k, add_v = dot_nn(slope, q_h), dot_nn(weight.astype(BF), g_h)
+            add_q = dot_nn(key_t, slope)
+            if unit == 0:
+                dq_sum[...] = add_q
+            else:
+                dq_sum[...] += add_q
+            sums = dkv_own.at[slot] if side == 0 else dkv_far
+            if h == 0:
+                sums[0] = add_k
+                sums[1] = add_v
+            else:
+                sums[0] += add_k
+                sums[1] += add_v
+            if unit in CUTS:
+                red.run_at(pair, ATTEND_STEPS[CUTS.index(unit)])
+                if unit < 3:
+                    ready = products(unit + 1)
         dp[:, at128(col)] = (dq_sum[...].T.astype(BF).astype(F32) * 0.125).astype(BF)
 
         @pl.when(pair >= 2)
@@ -967,7 +1053,7 @@
 
         dkv_send[slot] = dkv_far[...].astype(BF)
         c_dkv(pair).start()
-        pl.when(jnp.logical_and(pair >= 2, lax.rem(pair, 2) == 0))(lambda: in_grads(pair // 2 - 1))
+        in_grads(pair)
         pl.when(pair == 1)(lambda: c_lo.start())
 
     loop(0, 6, attend_back)
@@ -975,7 +1061,8 @@
     c_dkv(4).wait_send()
     c_dkv(5).wait_send()
 
-    in_grads(2)
+    for k in range(17, 20):
+        put_last(k)
     red.run(PROJECT_STEPS)
     vs[2:3] = jnp.sum(dp[:, 0:768].astype(F32), axis=0, keepdims=True)
     vs[3:4] = jnp.sum(dp[:, 1536:2304].astype(F32), axis=0, keepdims=True)
@@ -1164,7 +1251,7 @@
     tot, vs, lo, gto, gtr = pl.pallas_call(
         layer_kernel,
         out_shape=(
-            shape((K, 2, HR, 128), BF),
+            shape((BUFFERS, 2, HR, 128), BF),
             shape((16, D), F32),
             shape((2, PART, D), BF),
             shape((PART, D), F32),
@@ -1173,13 +1260,13 @@
         in_specs=[anywhere, anywhere, smem] + [vmem] * 8 + [anywhere] * 4,
         out_specs=(anywhere, vmem, anywhere, anywhere, anywhere),
         scratch_shapes=[
-            pltpu.VMEM((K, 2, 2, HR, 128), BF),
+            pltpu.VMEM((BUFFERS, 2, 2, HR, 128), BF),
             pltpu.VMEM((SLOT_COUNT, 2, 2, HR, 128), BF),
-            pltpu.VMEM((K, 2, 2, HR, 128), BF),
-            pltpu.VMEM((K, 2, HR, 128), BF),
-            pltpu.VMEM((K, HR, 128), BF),
-            pltpu.VMEM((K, HR, 128), BF),
-            pltpu.VMEM((K, HR, 128), BF),
+            pltpu.VMEM((BUFFERS, 2, 2, HR, 128), BF),
+            pltpu.VMEM((BUFFERS, 2, HR, 128), BF),
+            pltpu.VMEM((BUFFERS, HR, 128), BF),
+            pltpu.VMEM((BUFFERS, HR, 128), BF),
+            pltpu.VMEM((BUFFERS, HR, 128), BF),
             pltpu.VMEM((12, D), F32),
             pltpu.VMEM((ROWS, D), BF),
             pltpu.VMEM((ROWS, D), BF),
@@ -1261,7 +1348,7 @@
         in_specs=[anywhere, vmem, anywhere, anywhere, anywhere],
         out_specs=tuple(anywhere if i in (0, 1, 4, 6, 10, 12) else vmem for i in range(14)),
         scratch_shapes=[
-            pltpu.VMEM((K, 2, HR, 128), BF),
+            pltpu.VMEM((BUFFERS, 2, HR, 128), BF),
             pltpu.VMEM((PART, D), BF),
             pltpu.VMEM((2, PART, D), F32),
             pltpu.VMEM((2, PART, D), BF),

time: 148 us -> 145 us (0.980)
  Pallas kernels: 147 us -> 144 us
    pallas_call x1, Pallas kernels: 141 us -> 137 us  [local_slice(): pl.pallas_call(layer_kernel, out_shape=(shape((BUFFERS, 2, HR, 128), BF),...]
where the time goes in v5:
time: 145 us
  Pallas kernels  144 us (99%)
    pallas_call x1, Pallas kernels, local_slice(): pl.pallas_call(layer_kernel, out_shape=(shape((BUFFERS, 2, HR, 128), BF),...  137 us
    pallas_call x1, Pallas kernels, local_slice(): pl.pallas_call(finish_kernel, out_shape=(shape((MICRO, 1, PART, D), BF),...  6.6 us

profile of v5, /device:TPU:0, one launch (start us, length us, event | category | flops | bytes accessed | tf_op | source)
XLA Modules:
  0.0 144.5 jit_solution(10157595537053703036)
XLA Ops:
  0.7 137.1 %shard_map.254 = (bf16[18,2,384,128]{3,2,1,0:T(8,128)(2,1)}, f32[16,768]{1,0:T(8,128)}, bf16[2,256,768]{2,1,0:T(8,128)(2,1)}, f32[256,768]{1,0:T(8,128)}, bf16[256,768]{1,0:T(8,128)(2,1)}) custom-call(bf16[2,1,256,768]{3,2,1,0:T(8,128)(2,1)} %tok_ref.1, bf16[2,1,256,768]{3,2,1,0:T(8,128)(2,1)} %cot_ref.1, s32[2,1,4]{2,1,0:T(1,128)} %cnt_ref.1, ...), custom_call_target="tpu_custom_call" | custom-call | tf_op jit(solution)/shard_map/pallas_call | solution.py:1251
  137.8 6.6 %shard_map.255 = (bf16[2,1,256,768]{3,2,1,0:T(8,128)(2,1)}, f32[2,1,256,768]{3,2,1,0:T(8,128)}, f32[192]{0:T(256)}, f32[192]{0:T(256)}, f32[192,2304]{1,0:T(8,12...) custom-call(bf16[18,2,384,128]{3,2,1,0:T(8,128)(2,1)} %get-tuple-ele, ...), custom_call_target="tpu_custom_call" | custom-call | tf_op jit(solution)/shard_map/pallas_call | solution.py:1330

commit v6 on v5

--- a/solution.py
+++ b/solution.py
@@ -310,15 +310,15 @@
 LOW = -1e30
 COLUMNS = (0, 1, 2, 3, 4, 5, 0, 1, 6, 7, 12, 13, 2, 3, 8, 9, 14, 4, 15, 5, 10, 16, 11, 17)
 LAST_BIG = 16
-WAYS = "acababbccbabccbaaaab"
+WAYS = "acabcbbccbabcabaaaab"
 CUTS = (0, 1, 2, 3)
-FEED_STEPS = (((), (), (101, 102), (104,), (200, 106), (203, 202, 108, 109)), ((), (100,), (103,), (105,), (201, 107), ()))
-NORM_STEPS = ((), (205, 110, 204, 111))
-OUT_STEPS = (207, 300)
-ATTEND_STEPS = (((301,), (400, 302), (209, 500), (600, 306, 402, 211, 401), (501,), (213, 605, 312, 410)), ((), (), (307, 212, 304), (603, 404, 113, 505, 310, 114), (), (507, 214, 311, 506, 115, 601, 116, 508)), ((303, 112, 208, 206), (403,), (503, 308), (407,), (), (602,)), ((305,), (210,), (405,), (406, 408, 502), (309, 504), (409, 313, 604, 510, 412)))
-PROJECT_STEPS = (411, 314, 607, 606, 608, 509)
-LAST_STEPS = ((215, 117, 413, 118, 119, 610, 512, 216), (414, 511))
-DRAIN_STEPS = (217, 315, 0, 218, 609, 219, 514, 513, 1, 415, 611, 612, 2, 316, 614, 317, 3, 515, 318, 4, 416, 319, 417, 613, 615, 418, 5, 516, 419, 517, 518, 519, 616, 617, 618, 619)
+FEED_STEPS = (((), (), (101, 102), (104,), (200, 106), (203, 202, 108, 109)), ((), (100,), (103,), (105,), (201, 107), (204,)))
+NORM_STEPS = ((301, 205, 110), (111,))
+OUT_STEPS = (303, 300, 207)
+ATTEND_STEPS = (((304,), (302,), (401,), (405, 211, 309, 404, 603, 402), (504, 601), (311, 506, 214)), ((), (403,), (503, 306), (501, 310, 113, 600, 407, 114), (), (508, 604, 602, 115)), ((112, 305, 206), (210,), (212,), (406, 408, 505), (502, 410), (412, 116, 213, 607)), ((208,), (400, 307, 209), (308, 500), (409,), (312, 507, 605), (509, 411, 606, 314)))
+PROJECT_STEPS = (510, 608, 512)
+LAST_STEPS = ((215, 117, 511, 313, 118, 119, 216, 414, 609), (612, 610))
+DRAIN_STEPS = (217, 315, 413, 514, 0, 218, 219, 611, 316, 1, 513, 415, 2, 416, 614, 3, 317, 515, 613, 318, 516, 4, 319, 417, 418, 615, 5, 616, 419, 517, 518, 519, 617, 618, 619)
 
 
 def dot_nn(a, b):
@@ -713,21 +713,18 @@
     def swap(index, src, dst, peer):
         return remote(src, dst, xsend.at[index], xrecv.at[index], peer)
 
-    c_tok = swap(0, tok_ref.at[1 - p.y, 0], tokx.at[pl.ds(PART, PART)], p.to_y)
+    c_tok = [
+        swap(8 * i, tok_ref.at[1 - p.y, 0, pl.ds(i * 128, 128)], tokx.at[pl.ds(PART + i * 128, 128)], p.to_y)
+        for i in range(2)
+    ]
     c_cot = swap(1, cot_ref.at[1 - p.y, 0], dyx.at[pl.ds(PART, PART)], p.to_y)
     c_row = swap(2, rowb.at[2], rowb.at[1], p.to_y)
     c_aug = swap(3, kaug.at[pl.ds(0, ROWS)], kaug.at[pl.ds(ROWS, ROWS)], p.to_core)
+    pieces = ((0, PART), (PART, 128), (PART + 128, 128))
     c_kv = [
-        swap(4 + r, qkv.at[pl.ds(r * PART, PART), pl.ds(768, 1536)], kvr.at[pl.ds(r * PART, PART)], p.to_core)
-        for r in range(2)
+        swap(index, qkv.at[pl.ds(first, rows), pl.ds(768, 1536)], kvr.at[pl.ds(first, rows)], p.to_core)
+        for index, (first, rows) in zip((4, 5, 9), pieces)
     ]
-    c_tok.start()
-
-    for row, ref in ((0, fg_ref), (1, fb_ref), (4, ob_ref), (5, sg_ref), (6, sb_ref), (7, rb_ref)):
-        vec[row : row + 1] = ref[...].astype(F32).reshape(1, D)
-    vec[2:4] = ib_ref[...].astype(F32)
-    for f in range(4):
-        vec[8 + f : 9 + f] = eb_ref[f * D : (f + 1) * D].astype(F32).reshape(1, D)
 
     lane = lax.broadcasted_iota(jnp.int32, (16, PART), 1)
 
@@ -738,9 +735,16 @@
             kept = jnp.where(frame == j, cnt_ref[m, 0, j], kept)
         return jnp.where(lane - frame * SLOTS < kept, 0.0, LOW).astype(BF)
 
-    rowb[0] = bias_row(p.y)
     rowb[2] = bias_row(1 - p.y)
     c_row.start()
+    for one in c_tok:
+        one.start()
+    rowb[0] = bias_row(p.y)
+    for row, ref in ((0, fg_ref), (1, fb_ref), (4, ob_ref), (5, sg_ref), (6, sb_ref), (7, rb_ref)):
+        vec[row : row + 1] = ref[...].astype(F32).reshape(1, D)
+    vec[2:4] = ib_ref[...].astype(F32)
+    for f in range(4):
+        vec[8 + f : 9 + f] = eb_ref[f * D : (f + 1) * D].astype(F32).reshape(1, D)
     pick = jnp.where(
         jnp.logical_and(
             lax.broadcasted_iota(jnp.int32, (16, 128), 0) == 0,
@@ -759,7 +763,7 @@
     vs[...] = jnp.zeros_like(vs)
 
     def project(r):
-        rows = pl.ds(r * PART, PART)
+        rows = pl.ds(*pieces[r])
         hat, _ = norm_parts(tokx[rows].astype(F32))
         low2[rows] = (hat * vec[0:1] + vec[1:2]).astype(BF)
 
@@ -779,17 +783,19 @@
     loads[0].wait()
     loads[1].wait()
     project(0)
-    c_tok.wait_recv()
     c_row.wait_recv()
-    c_cot.start()
     kaug[pl.ds(PART, PART)] = dot_tn(rowb[1], pick).astype(BF)
     c_aug.start()
+    c_tok[0].wait_recv()
     project(1)
+    c_tok[1].wait_recv()
+    c_cot.start()
+    project(2)
     load_we = pltpu.make_async_copy(we_ref, w1, lsem.at[5])
     load_we.start()
-    c_kv[0].wait_recv()
-    c_kv[1].wait_recv()
     c_aug.wait_recv()
+    for one in c_kv:
+        one.wait_recv()
 
     def attend(pair):
         col = pl.multiple_of(pair * 128, 128)
@@ -1139,12 +1145,11 @@
         else:
             red.run((step,))
     red.close()
-    c_tok.wait_send()
+    for one in c_tok + c_kv:
+        one.wait_send()
     c_row.wait_send()
     c_cot.wait_send()
     c_aug.wait_send()
-    c_kv[0].wait_send()
-    c_kv[1].wait_send()
     c_lo.wait()
     c_gt.wait()
     keep_lo.wait()
@@ -1300,8 +1305,8 @@
             dma((12,)),
             dma((6, K)),
             dma((9,)),
-            dma((8,)),
-            dma((8,)),
+            dma((10,)),
+            dma((10,)),
             dma((6,)),
             dma((6,)),
             dma((5,)),

time: 145 us -> 143 us (0.986)
  Pallas kernels: 144 us -> 142 us
    pallas_call x1, Pallas kernels: 137 us -> 136 us  [local_slice(): pl.pallas_call(layer_kernel, out_shape=(shape((BUFFERS, 2, HR, 128), BF),...]
where the time goes in v6:
time: 143 us
  Pallas kernels  142 us (99%)
    pallas_call x1, Pallas kernels, local_slice(): pl.pallas_call(layer_kernel, out_shape=(shape((BUFFERS, 2, HR, 128), BF),...  136 us
    pallas_call x1, Pallas kernels, local_slice(): pl.pallas_call(finish_kernel, out_shape=(shape((MICRO, 1, PART, D), BF),...  6.6 us

profile of v6, /device:TPU:0, one launch (start us, length us, event | category | flops | bytes accessed | tf_op | source)
XLA Modules:
  0.0 143.0 jit_solution(2509155625000657997)
XLA Ops:
  0.7 135.6 %shard_map.254 = (bf16[18,2,384,128]{3,2,1,0:T(8,128)(2,1)}, f32[16,768]{1,0:T(8,128)}, bf16[2,256,768]{2,1,0:T(8,128)(2,1)}, f32[256,768]{1,0:T(8,128)}, bf16[256,768]{1,0:T(8,128)(2,1)}) custom-call(bf16[2,1,256,768]{3,2,1,0:T(8,128)(2,1)} %tok_ref.1, bf16[2,1,256,768]{3,2,1,0:T(8,128)(2,1)} %cot_ref.1, s32[2,1,4]{2,1,0:T(1,128)} %cnt_ref.1, ...), custom_call_target="tpu_custom_call" | custom-call | tf_op jit(solution)/shard_map/pallas_call | solution.py:1256
  136.3 6.6 %shard_map.255 = (bf16[2,1,256,768]{3,2,1,0:T(8,128)(2,1)}, f32[2,1,256,768]{3,2,1,0:T(8,128)}, f32[192]{0:T(256)}, f32[192]{0:T(256)}, f32[192,2304]{1,0:T(8,12...) custom-call(bf16[18,2,384,128]{3,2,1,0:T(8,128)(2,1)} %get-tuple-ele, ...), custom_call_target="tpu_custom_call" | custom-call | tf_op jit(solution)/shard_map/pallas_call | solution.py:1335

commit v7 on v6

--- a/solution.py
+++ b/solution.py
@@ -797,37 +797,38 @@
     for one in c_kv:
         one.wait_recv()
 
-    def attend(pair):
-        col = pl.multiple_of(pair * 128, 128)
+    def attend(group):
+        cols = [pl.multiple_of(group * 256 + i * 128, 128) for i in range(2)]
         ones = jnp.ones((ROWS, 128), BF)
         first = jnp.where(lane_q == 0, 1.0, 0.0).astype(BF)
-        k_here = jnp.concatenate([qkv[:, at128(768 + col)], kaug[pl.ds(0, ROWS)]], axis=1)
-        k_there = jnp.concatenate([kvr[:, at128(col)], kaug[pl.ds(ROWS, ROWS)]], axis=1)
-        v_here = jnp.concatenate([qkv[:, at128(1536 + col)], ones], axis=1)
-        v_there = jnp.concatenate([kvr[:, at128(768 + col)], ones], axis=1)
+        k_here = [jnp.concatenate([qkv[:, at128(768 + c)], kaug[pl.ds(0, ROWS)]], axis=1) for c in cols]
+        k_there = [jnp.concatenate([kvr[:, at128(c)], kaug[pl.ds(ROWS, ROWS)]], axis=1) for c in cols]
+        v_here = [jnp.concatenate([qkv[:, at128(1536 + c)], ones], axis=1) for c in cols]
+        v_there = [jnp.concatenate([kvr[:, at128(768 + c)], ones], axis=1) for c in cols]
+
         def scores(unit):
-            block, h = unit // 2, unit % 2
-            query = qkv[pl.ds(block * PART, PART), at128(col)]
+            i, block, h = unit // 4, unit // 2 % 2, unit % 2
+            query = qkv[pl.ds(block * PART, PART), at128(cols[i])]
             lifted = jnp.concatenate([query * head_mask[h], first], axis=1)
-            return dot_nt(lifted, k_here), dot_nt(lifted, k_there)
+            return dot_nt(lifted, k_here[i]), dot_nt(lifted, k_there[i])
 
         ready = scores(0)
-        for unit in range(4):
-            block, h = unit // 2, unit % 2
+        for unit in range(8):
+            one, block, h = unit // 4, unit // 2 % 2, unit % 2
             rows = pl.ds(block * PART, PART)
             s_here, s_there = ready
-            if unit < 3:
+            if unit < 7:
                 ready = scores(unit + 1)
             top = jnp.maximum(
                 jnp.max(s_here, axis=-1, keepdims=True), jnp.max(s_there, axis=-1, keepdims=True)
             )
             e_here = jnp.exp(s_here - top).astype(BF)
             e_there = jnp.exp(s_there - top).astype(BF)
-            both = dot_nn(e_here, v_here) + dot_nn(e_there, v_there)
+            both = dot_nn(e_here, v_here[one]) + dot_nn(e_there, v_there[one])
             total = both[:, 128:]
             out = both[:, :128] / total
             parts = three_parts(top + jnp.log(total))
-            base = 1 + 3 * (2 * pair + h)
+            base = 1 + 3 * (2 * (2 * group + one) + h)
             extra = qaug[rows] if h == 0 else extra
             for i in range(3):
                 extra = jnp.where(lane_q == base + i, -parts[i], extra)
@@ -835,9 +836,9 @@
                 held = out
             else:
                 qaug[rows] = extra
-                att[rows, at128(col)] = jnp.where(lane_q < 64, held, out).astype(BF)
-
-    loop(0, 6, attend)
+                att[rows, at128(cols[one])] = jnp.where(lane_q < 64, held, out).astype(BF)
+
+    loop(0, 3, attend)
 
     def turn(rows, block):
         flipped = block.T

time: 143 us -> 142 us (level)
  no operation moved by 1% of the time
where the time goes in v7:
time: 142 us
  Pallas kernels  141 us (99%)
    pallas_call x1, Pallas kernels, local_slice(): pl.pallas_call(layer_kernel, out_shape=(shape((BUFFERS, 2, HR, 128), BF),...  134 us
    pallas_call x1, Pallas kernels, local_slice(): pl.pallas_call(finish_kernel, out_shape=(shape((MICRO, 1, PART, D), BF),...  6.6 us

profile of v7, /device:TPU:0, one launch (start us, length us, event | category | flops | bytes accessed | tf_op | source)
XLA Modules:
  0.0 141.9 jit_solution(3759723640476507576)
XLA Ops:
  0.7 134.5 %shard_map.254 = (bf16[18,2,384,128]{3,2,1,0:T(8,128)(2,1)}, f32[16,768]{1,0:T(8,128)}, bf16[2,256,768]{2,1,0:T(8,128)(2,1)}, f32[256,768]{1,0:T(8,128)}, bf16[256,768]{1,0:T(8,128)(2,1)}) custom-call(bf16[2,1,256,768]{3,2,1,0:T(8,128)(2,1)} %tok_ref.1, bf16[2,1,256,768]{3,2,1,0:T(8,128)(2,1)} %cot_ref.1, s32[2,1,4]{2,1,0:T(1,128)} %cnt_ref.1, ...), custom_call_target="tpu_custom_call" | custom-call | tf_op jit(solution)/shard_map/pallas_call | solution.py:1257
  135.1 6.6 %shard_map.255 = (bf16[2,1,256,768]{3,2,1,0:T(8,128)(2,1)}, f32[2,1,256,768]{3,2,1,0:T(8,128)}, f32[192]{0:T(256)}, f32[192]{0:T(256)}, f32[192,2304]{1,0:T(8,12...) custom-call(bf16[18,2,384,128]{3,2,1,0:T(8,128)(2,1)} %get-tuple-ele, ...), custom_call_target="tpu_custom_call" | custom-call | tf_op jit(solution)/shard_map/pallas_call | solution.py:1336
